TPU v7x, 128 devices: a whole 4x4x4 slice. The times are simulated.
128 devices in a mesh: rows: 64 (over x, z, y), blk: 2 (over core).
Axes of the slice: x: 4, y: 4, z: 4, core: 2. Of those that a mesh axis runs over, the one named last changes fastest.
Arguments:
- off_blocks: bfloat16 [2048, 6, 192, 192], P('rows', None, 'blk'), may hold values from -0.15625 to 0.15625
- diag_blocks: bfloat16 [2048, 192, 192], P('rows', 'blk')
- precond: bfloat16 [2048, 192, 192], P('rows', 'blk')
- adj_rhs: float32 [2048, 16, 192], P('rows'), may hold values from -6 to 6
- col_owner: int32 [2048, 6], P('rows'), may hold values from 0 to 63, as said below
- col_local: int32 [2048, 6], P('rows'), may hold values from 0 to 31
Outputs:
- adjoint: float32 [2048, 16, 192], P('rows')
- residual: float32 [2048, 16, 192], P('rows')
Inputs may be any that keep to these rules, and one draw needn't show every extreme that they name: `col_owner`: for a block row held by device r, entry k is r itself or (r + o) mod 64, where o is the k-th of 1, 63, 2, 62, 32, 33. In one device's block rows, at most 16 entries of one column differ from the device's own index, at least one does, and on every device some column has exactly 16 such entries.
All inputs are finite; a program needn't handle non-finite values.
Results may differ from a plain program's by a relative error of at most 0.011.
Values may be sent and summed in bfloat16 or wider, within the bound.
No kernel may reach another device: no remote copies, remote signals or barrier semaphores. Data moves between devices by JAX's collectives and lax.ppermute only.
A program may use at most 128 MiB of HBM per device.

v0:
```python
import jax
import jax.numpy as jnp
from jax import lax
from jax.sharding import PartitionSpec as P

ITERS = 2


def from_behind(x, axis, by):
    devices = lax.axis_size(axis)
    return lax.ppermute(x, axis, [(i, (i + by) % devices) for i in range(devices)])


def face_tables(col_owner, col_local, own, cap):
    rows_here, fan = col_owner.shape
    remote = col_owner != own
    rank = jnp.cumsum(remote.astype(jnp.int32), axis=0) - 1
    slot_ids = jnp.arange(cap, dtype=jnp.int32)
    row_ids = jnp.arange(rows_here, dtype=jnp.int32)
    match = remote[None, :, :] & (rank[None, :, :] == slot_ids[:, None, None])
    valid = jnp.any(match, axis=1)
    match_int = match.astype(jnp.int32)
    entry = jnp.sum(match_int * row_ids[None, :, None], axis=1)
    label = jnp.sum(match_int * (col_local + 1)[None, :, :], axis=1)
    local = jnp.logical_not(remote)[None, :, :] & (col_local[None, :, :] == row_ids[:, None, None])
    local_placer = local.reshape(rows_here, rows_here * fan).astype(jnp.float32)
    return (entry, valid, label, local_placer)


def arrival_placer(got_label, rows_here):
    row_ids = jnp.arange(rows_here, dtype=jnp.int32)
    return (got_label.astype(jnp.int32)[None, :] - 1 == row_ids[:, None]).astype(jnp.float32)


def on_device(off_blocks, diag_blocks, precond, adj_rhs, col_owner, col_local):
    nrows = lax.axis_size("rows")
    rows_here, fan, half, width = off_blocks.shape
    nadj_cols = adj_rhs.shape[1]
    cap = max(2, rows_here // 2)
    half_way = nrows // 2
    offsets = (1, nrows - 1, 2, nrows - 2, half_way, half_way + 1)
    own = lax.axis_index("rows")
    start = lax.axis_index("blk") * half
    entry, valid, label, local_placer = face_tables(col_owner, col_local, own, cap)

    def precondition(field):
        mine = jnp.einsum(
            "nrc,nac->nar", precond, field.astype(jnp.bfloat16), preferred_element_type=jnp.float32
        )
        return lax.all_gather(mine, "blk", axis=2, tiled=True)

    labels_wire = label.astype(jnp.float32)
    adjoint = precondition(adj_rhs)
    residual = adj_rhs
    for step in range(ITERS):
        xb = adjoint.astype(jnp.bfloat16)
        xh = lax.dynamic_slice_in_dim(xb, start, half, 2)
        diag_part = jnp.einsum("nrc,nar->nac", diag_blocks, xh, preferred_element_type=jnp.float32)
        off_part = jnp.einsum("nkrc,nar->nkac", off_blocks, xh, preferred_element_type=jnp.float32)
        off_part = off_part.reshape(rows_here * fan, nadj_cols, width)
        diag_sum, off_sum = lax.psum((diag_part, off_part), "blk")
        total = diag_sum + jnp.einsum(
            "nm,mac->nac", local_placer, off_sum, precision=lax.Precision.HIGHEST
        )
        off_faces = off_sum.reshape(rows_here, fan, nadj_cols, width)
        for face in range(fan):
            picked = off_faces[entry[:, face], face]
            sending = jnp.where(valid[:, face, None, None], picked, 0.0)
            got, got_label = (
                from_behind(sending.astype(jnp.bfloat16), "rows", offsets[face]).astype(
                    sending.dtype
                ),
                from_behind(
                    labels_wire[:, face].astype(jnp.bfloat16), "rows", offsets[face]
                ).astype(jnp.float32),
            )
            placer = arrival_placer(got_label, rows_here)
            total = total + jnp.einsum("ns,sac->nac", placer, got, precision=lax.Precision.HIGHEST)
        residual = adj_rhs - total
        adjoint = adjoint + precondition(residual)
    return (adjoint, residual)


def solution(mesh):
    in_specs = (
        P("rows", None, "blk", None),
        P("rows", "blk", None),
        P("rows", "blk", None),
        P("rows", None, None),
        P("rows", None),
        P("rows", None),
    )
    out_specs = (P("rows", None, None), P("rows", None, None))
    return jax.shard_map(
        on_device, mesh=mesh, in_specs=in_specs, out_specs=out_specs, check_vma=False
    )
```

profile of v0, /device:TPU:1, one launch (start us, length us, event | category | flops | bytes accessed | tf_op | source)
XLA Modules:
  0.0 226.6 jit_solution(6807158104268082523)
XLA Ops:
  7.2 2.2 fusion.19
  10.7 4.2 %all_gather.9 = f32[32,16,192]{0,1,2:T(8,128)S(1)} all-gather(f32[32,16,96]{0,1,2:T(8,128)} %copy.134), channel_id=1, replica_groups=mesh['rows'=64,'blk'=2] {'blk'}, dimensions={2}, use_global_device_ids=true | all-gather | bytes 589824 | tf_op jit(solution)/shard_map/all_gather | solution.py:50
  16.6 2.2 fusion.25
  18.8 4.7 %fusion.23 = f32[32,16,6,192]{3,1,2,0:T(8,128)S(1)} fusion(bf16[32,6,96,192]{3,2,1,0:T(8,128)(2,1)} %param.6, f32[32,16,192]{2,1,0:T(8,128)} %copy.156, s32[]{:T(128)S(6)} %select_n.71), kind=kOutput, calls=%fused_computation.62 | convolution fusion | flops 113246208 | bytes 11927556 | tf_op jit(solution)/shard_map/nkrc,nar->nkac/dot_general | solution.py:59
  23.5 3.5 %copy.138 = f32[192,16,192]{2,0,1:T(8,128)} copy(f32[192,16,192]{2,1,0:T(8,128)S(1)} %bitcast.104) | data formatting | bytes 4718592 | tf_op jit(solution)/shard_map/reshape | solution.py:60
  29.7 3.8 %collective-permute-start.10 = (bf16[16]{0:T(256)(128)(2,1)S(1)}, bf16[16]{0:T(256)(128)(2,1)S(1)}, u32[]{:S(2)}, u32[]{:S(2)}) collective-permute-start(bf16[16]{0:T(256)(128)(2,1)S(1)} %get-tuple-element.17), channel_id=1, source_target_pairs={{0,66},{2,68},{4,70},{6,72},{8,74},{10,76},{12,78},{14,80},{16,82}... | collective-permute-start | bytes 104 | tf_op jit(solution)/shard_map/ppermute | solution.py:11
  33.7 7.1 %collective-permute-start.6 = (bf16[16]{0:T(256)(128)(2,1)S(1)}, bf16[16]{0:T(256)(128)(2,1)S(1)}, u32[]{:S(2)}, u32[]{:S(2)}) collective-permute-start(bf16[16]{0:T(256)(128)(2,1)S(1)} %get-tuple-element.19), channel_id=1, source_target_pairs={{0,124},{2,126},{4,0},{6,2},{8,4},{10,6},{12,8},{14,10},{16,12},{1... | collective-permute-start | bytes 104 | tf_op jit(solution)/shard_map/ppermute | solution.py:11
  41.5 4.6 %collective-permute-start.2 = (bf16[16]{0:T(256)(128)(2,1)S(1)}, bf16[16]{0:T(256)(128)(2,1)S(1)}, u32[]{:S(2)}, u32[]{:S(2)}) collective-permute-start(bf16[16]{0:T(256)(128)(2,1)S(1)} %get-tuple-element.21), channel_id=1, source_target_pairs={{0,126},{2,0},{4,2},{6,4},{8,6},{10,8},{12,10},{14,12},{16,14},{18... | collective-permute-start | bytes 104 | tf_op jit(solution)/shard_map/ppermute | solution.py:11
  46.2 2.7 %collective-permute-done.4 = bf16[16]{0:T(256)(128)(2,1)S(1)} collective-permute-done((bf16[16]{0:T(256)(128)(2,1)S(1)}, bf16[16]{0:T(256)(128)(2,1)S(1)}, u32[]{:S(2)}, u32[]{:S(2)}) %collective-permute-start.4) | collective-permute-done | bytes 64 | tf_op jit(solution)/shard_map/ppermute | solution.py:11
  49.0 10.8 %all-reduce.13.cloned.1.call-done = (f32[192,16,192]{2,0,1:T(8,128)}, f32[32,16,192]{2,1,0:T(8,128)}) async-done(((f32[192,16,192]{2,0,1:T(8,128)}, f32[32,16,192]{2,1,0:T(8,128)}), (f32[192,16,192]{2,0,1:T(8,128)}, f32[32,16,192]{2,1,0:T(8,128)})) %all-reduce.13.cloned.1.call-update) | async-done | bytes 2752528 | tf_op jit(solution)/shard_map/psum | solution.py:61
  59.7 3.6 %copy.142 = bf16[192,16,192]{2,1,0:T(8,128)(2,1)S(1)} copy(f32[192,16,192]{2,0,1:T(8,128)} %get-tuple-element.6) | data formatting | bytes 3538944 | tf_op jit(solution)/shard_map/psum | solution.py:61
  70.4 7.1 %collective-permute-start.3 = (bf16[16,16,192]{2,0,1:T(8,128)(2,1)S(1)}, bf16[16,16,192]{2,0,1:T(8,128)(2,1)S(1)}, u32[]{:S(2)}, u32[]{:S(2)}) collective-permute-start(bf16[16,16,192]{2,0,1:T(8,128)(2,1)S(1)} %fusion.15), channel_id=1, source_target_pairs={{0,126},{2,0},{4,2},{6,4},{8,6},{10,8},{12,10},{14,12},{16,14},{18... | collective-permute-start | bytes 294920 | tf_op jit(solution)/shard_map/ppermute | solution.py:11
  80.7 7.2 %collective-permute-start.7 = (bf16[16,16,192]{2,0,1:T(8,128)(2,1)S(1)}, bf16[16,16,192]{2,0,1:T(8,128)(2,1)S(1)}, u32[]{:S(2)}, u32[]{:S(2)}) collective-permute-start(bf16[16,16,192]{2,0,1:T(8,128)(2,1)S(1)} %fusion.13), channel_id=1, source_target_pairs={{0,124},{2,126},{4,0},{6,2},{8,4},{10,6},{12,8},{14,10},{16,12},{1... | collective-permute-start | bytes 294920 | tf_op jit(solution)/shard_map/ppermute | solution.py:11
  88.3 3.2 %fusion.33 = f32[32,16,192]{2,0,1:T(8,128)S(1)} fusion(f32[192,16,192]{2,0,1:T(8,128)} %get-tuple-element.6, s32[192]{0:T(256)S(1)} %eq.51, pred[192]{0:T(512)(128)(4,1)S(1)} %and.21), kind=kOutput, calls=%fused_computation.75 | convolution fusion | flops 226504704 | bytes 2753472 | tf_op jit(solution)/shard_map/nm,mac->nac/dot_general | solution.py:62
  91.6 4.9 %collective-permute-done.11 = bf16[16,16,192]{2,0,1:T(8,128)(2,1)S(1)} collective-permute-done((bf16[16,16,192]{2,0,1:T(8,128)(2,1)S(1)}, bf16[16,16,192]{2,0,1:T(8,128)(2,1)S(1)}, u32[]{:S(2)}, u32[]{:S(2)}) %collective-permute-start.11) | collective-permute-done | bytes 98336 | tf_op jit(solution)/shard_map/ppermute | solution.py:11
  96.9 4.9 %collective-permute-done.9 = bf16[16,16,192]{2,0,1:T(8,128)(2,1)S(1)} collective-permute-done((bf16[16,16,192]{2,0,1:T(8,128)(2,1)S(1)}, bf16[16,16,192]{2,0,1:T(8,128)(2,1)S(1)}, u32[]{:S(2)}, u32[]{:S(2)}) %collective-permute-start.9) | collective-permute-done | bytes 98336 | tf_op jit(solution)/shard_map/ppermute | solution.py:11
  103.7 2.3 %fusion.3 = f32[32,16,96]{2,1,0:T(8,128)S(1)} fusion(bf16[32,96,192]{2,1,0:T(8,128)(2,1)S(1)} %copy-done.1, f32[32,16,192]{2,1,0:T(8,128)S(1)} %copy-done.3, f32[32,16,192]{2,0,1:T(8,128)S(1)} %fusion.67, f32[32,16,192]{2,0,1:T(8,128)S(1)} %fusion.62, f32[32,16,192]{2,0,1:T(8,128)S(1)} %fusion.57, f32[32,16,192]{2,0,1:T(8,128)S(1)} %fusion.52, ...), kind=kOutput, calls=%fused_computation.29 | convolution fusion | flops 19759104 | bytes 4915200 | tf_op jit(solution)/shard_map/nrc,nac->nar/dot_general | solution.py:47
  107.2 13.2 %all_gather.10 = f32[32,16,192]{0,1,2:T(8,128)} all-gather(f32[32,16,96]{0,1,2:T(8,128)} %copy.155), channel_id=1, replica_groups=mesh['rows'=64,'blk'=2] {'blk'}, dimensions={2}, use_global_device_ids=true | all-gather | bytes 589824 | tf_op jit(solution)/shard_map/all_gather | solution.py:50
  120.4 3.0 %copy.157 = f32[32,16,192]{2,1,0:T(8,128)} copy(f32[32,16,192]{0,1,2:T(8,128)} %all_gather.10) | data formatting | bytes 786432 | tf_op jit(solution)/shard_map/all_gather | solution.py:50
  126.0 4.6 %fusion.21 = f32[32,16,6,192]{3,1,2,0:T(8,128)S(1)} fusion(bf16[32,6,96,192]{3,2,1,0:T(8,128)(2,1)} %param.6, f32[32,16,192]{2,1,0:T(8,128)S(1)} %add.137, s32[]{:T(128)S(6)} %select_n.71), kind=kOutput, calls=%fused_computation.60 | convolution fusion | flops 113246208 | bytes 9568260 | tf_op jit(solution)/shard_map/nkrc,nar->nkac/dot_general | solution.py:59
  130.5 3.5 %copy.158 = f32[192,16,192]{2,0,1:T(8,128)} copy(f32[192,16,192]{2,1,0:T(8,128)S(1)} %bitcast.103) | data formatting | bytes 4718592 | tf_op jit(solution)/shard_map/reshape | solution.py:60
  134.1 24.1 %all-reduce.11.cloned.1.call-done = (f32[192,16,192]{2,0,1:T(8,128)}, f32[32,16,192]{2,1,0:T(8,128)}) async-done(((f32[192,16,192]{2,0,1:T(8,128)}, f32[32,16,192]{2,1,0:T(8,128)}), (f32[192,16,192]{2,0,1:T(8,128)}, f32[32,16,192]{2,1,0:T(8,128)})) %all-reduce.11.cloned.1.call-update) | async-done | bytes 2752528 | tf_op jit(solution)/shard_map/psum | solution.py:61
  158.2 4.1 %fusion.31 = f32[32,16,192]{2,0,1:T(8,128)} fusion(f32[192,16,192]{2,0,1:T(8,128)} %get-tuple-element.4, s32[192]{0:T(256)S(1)} %eq.51, pred[192]{0:T(512)(128)(4,1)S(1)} %and.21), kind=kOutput, calls=%fused_computation.74 | convolution fusion | flops 226504704 | bytes 2753472 | tf_op jit(solution)/shard_map/nm,mac->nac/dot_general | solution.py:62
  162.3 2.8 %copy.160 = bf16[192,16,192]{2,1,0:T(8,128)(2,1)} copy(f32[192,16,192]{2,0,1:T(8,128)S(1)} %copy-done.2) | data formatting | bytes 3538944 | tf_op jit(solution)/shard_map/psum | solution.py:61
  165.2 2.6 %gather_fusion.11 = bf16[16,16,192]{2,1,0:T(8,128)(2,1)} fusion(bf16[32,6,16,192]{3,2,1,0:T(8,128)(2,1)} %bitcast.105, s32[16]{0:T(128)S(1)} %get-tuple-element.11), kind=kCustom, calls=%fused_computation.11 | custom fusion | bytes 196736 | tf_op jit(solution)/shard_map/gather | solution.py:67
  167.8 2.6 %gather_fusion.10 = bf16[16,16,192]{2,1,0:T(8,128)(2,1)} fusion(bf16[32,6,16,192]{3,2,1,0:T(8,128)(2,1)} %bitcast.106, s32[16]{0:T(128)S(1)} %get-tuple-element.12), kind=kCustom, calls=%fused_computation.10 | custom fusion | bytes 196736 | tf_op jit(solution)/shard_map/gather | solution.py:67
  176.5 2.6 %gather_fusion.6 = bf16[16,16,192]{2,1,0:T(8,128)(2,1)} fusion(bf16[32,6,16,192]{3,2,1,0:T(8,128)(2,1)} %bitcast.110, s32[16]{0:T(128)S(1)} %get-tuple-element.10), kind=kCustom, calls=%fused_computation.6 | custom fusion | bytes 196736 | tf_op jit(solution)/shard_map/gather | solution.py:67
  183.6 3.8 %collective-permute-start.17 = (bf16[16,16,192]{2,0,1:T(8,128)(2,1)S(1)}, bf16[16,16,192]{2,0,1:T(8,128)(2,1)S(1)}, u32[]{:S(2)}, u32[]{:S(2)}) collective-permute-start(bf16[16,16,192]{2,0,1:T(8,128)(2,1)S(1)} %fusion.5), channel_id=1, source_target_pairs={{0,66},{2,68},{4,70},{6,72},{8,74},{10,76},{12,78},{14,80},{16,82}... | collective-permute-start | bytes 294920 | tf_op jit(solution)/shard_map/ppermute | solution.py:11
  188.1 3.6 %collective-permute-start.13 = (bf16[16,16,192]{2,0,1:T(8,128)(2,1)S(1)}, bf16[16,16,192]{2,0,1:T(8,128)(2,1)S(1)}, u32[]{:S(2)}, u32[]{:S(2)}) collective-permute-start(bf16[16,16,192]{2,0,1:T(8,128)(2,1)S(1)} %fusion.9), channel_id=1, source_target_pairs={{0,126},{2,0},{4,2},{6,4},{8,6},{10,8},{12,10},{14,12},{16,14},{18... | collective-permute-start | bytes 294920 | tf_op jit(solution)/shard_map/ppermute | solution.py:11
  192.1 6.9 %collective-permute-start.15 = (bf16[16,16,192]{2,0,1:T(8,128)(2,1)S(1)}, bf16[16,16,192]{2,0,1:T(8,128)(2,1)S(1)}, u32[]{:S(2)}, u32[]{:S(2)}) collective-permute-start(bf16[16,16,192]{2,0,1:T(8,128)(2,1)S(1)} %fusion.7), channel_id=1, source_target_pairs={{0,124},{2,126},{4,0},{6,2},{8,4},{10,6},{12,8},{14,10},{16,12},{1... | collective-permute-start | bytes 294920 | tf_op jit(solution)/shard_map/ppermute | solution.py:11
  200.0 4.6 %collective-permute-done.16 = bf16[16,16,192]{2,0,1:T(8,128)(2,1)S(1)} collective-permute-done((bf16[16,16,192]{2,0,1:T(8,128)(2,1)S(1)}, bf16[16,16,192]{2,0,1:T(8,128)(2,1)S(1)}, u32[]{:S(2)}, u32[]{:S(2)}) %collective-permute-start.16) | collective-permute-done | bytes 98336 | tf_op jit(solution)/shard_map/ppermute | solution.py:11
  211.0 5.0 %all_gather.11 = f32[32,16,192]{0,1,2:T(8,128)S(1)} all-gather(f32[32,16,96]{0,1,2:T(8,128)} %copy.173), channel_id=1, replica_groups=mesh['rows'=64,'blk'=2] {'blk'}, dimensions={2}, use_global_device_ids=true | all-gather | bytes 589824 | tf_op jit(solution)/shard_map/all_gather | solution.py:50
  (152 shorter events, 45.6 us)
Async XLA Ops:
  7.2 52.6 %all-reduce.13.cloned.1.call-start = ((), (), s32[]{:S(2)}) async-start(), calls=%async_computation.1 | async-start | bytes 7340032 | tf_op jit(solution)/shard_map/psum | solution.py:61
  27.1 131.1 %all-reduce.11.cloned.1.call-start = ((), (), s32[]{:S(2)}) async-start(), calls=%async_computation | async-start | bytes 7340032 | tf_op jit(solution)/shard_map/psum | solution.py:61
  28.3 13.2 %collective-permute-start = (bf16[16]{0:T(256)(128)(2,1)S(1)}, bf16[16]{0:T(256)(128)(2,1)S(1)}, u32[]{:S(2)}, u32[]{:S(2)}) collective-permute-start(bf16[16]{0:T(256)(128)(2,1)S(1)} %get-tuple-element.16), channel_id=1, source_target_pairs={{0,2},{2,4},{4,6},{6,8},{8,10},{10,12},{12,14},{14,16},{16,18},{18... | collective-permute-start | bytes 104 | tf_op jit(solution)/shard_map/ppermute | solution.py:11
  29.7 16.4 %collective-permute-start.10 = (bf16[16]{0:T(256)(128)(2,1)S(1)}, bf16[16]{0:T(256)(128)(2,1)S(1)}, u32[]{:S(2)}, u32[]{:S(2)}) collective-permute-start(bf16[16]{0:T(256)(128)(2,1)S(1)} %get-tuple-element.17), channel_id=1, source_target_pairs={{0,66},{2,68},{4,70},{6,72},{8,74},{10,76},{12,78},{14,80},{16,82}... | collective-permute-start | bytes 104 | tf_op jit(solution)/shard_map/ppermute | solution.py:11
  33.5 12.7 %collective-permute-start.8 = (bf16[16]{0:T(256)(128)(2,1)S(1)}, bf16[16]{0:T(256)(128)(2,1)S(1)}, u32[]{:S(2)}, u32[]{:S(2)}) collective-permute-start(bf16[16]{0:T(256)(128)(2,1)S(1)} %get-tuple-element.18), channel_id=1, source_target_pairs={{0,64},{2,66},{4,68},{6,70},{8,72},{10,74},{12,76},{14,78},{16,80}... | collective-permute-start | bytes 104 | tf_op jit(solution)/shard_map/ppermute | solution.py:11
  33.7 12.5 %collective-permute-start.6 = (bf16[16]{0:T(256)(128)(2,1)S(1)}, bf16[16]{0:T(256)(128)(2,1)S(1)}, u32[]{:S(2)}, u32[]{:S(2)}) collective-permute-start(bf16[16]{0:T(256)(128)(2,1)S(1)} %get-tuple-element.19), channel_id=1, source_target_pairs={{0,124},{2,126},{4,0},{6,2},{8,4},{10,6},{12,8},{14,10},{16,12},{1... | collective-permute-start | bytes 104 | tf_op jit(solution)/shard_map/ppermute | solution.py:11
  40.8 8.1 %collective-permute-start.4 = (bf16[16]{0:T(256)(128)(2,1)S(1)}, bf16[16]{0:T(256)(128)(2,1)S(1)}, u32[]{:S(2)}, u32[]{:S(2)}) collective-permute-start(bf16[16]{0:T(256)(128)(2,1)S(1)} %get-tuple-element.20), channel_id=1, source_target_pairs={{0,4},{2,6},{4,8},{6,10},{8,12},{10,14},{12,16},{14,18},{16,20},{1... | collective-permute-start | bytes 104 | tf_op jit(solution)/shard_map/ppermute | solution.py:11
  41.4 36.1 %copy-start.12 = (pred[16]{0:T(512)(128)(4,1)}, pred[16]{0:T(512)(128)(4,1)S(1)}, u32[]{:S(2)}) copy-start(pred[16]{0:T(512)(128)(4,1)S(1)} %get-tuple-element.22) | copy-start | bytes 52
  41.4 37.2 %copy-start.13 = (pred[16]{0:T(512)(128)(4,1)}, pred[16]{0:T(512)(128)(4,1)S(1)}, u32[]{:S(2)}) copy-start(pred[16]{0:T(512)(128)(4,1)S(1)} %get-tuple-element.26) | copy-start | bytes 52
  41.5 38.3 %copy-start.14 = (pred[16]{0:T(512)(128)(4,1)}, pred[16]{0:T(512)(128)(4,1)S(1)}, u32[]{:S(2)}) copy-start(pred[16]{0:T(512)(128)(4,1)S(1)} %get-tuple-element.25) | copy-start | bytes 52
  41.5 46.5 %copy-start.16 = (pred[16]{0:T(512)(128)(4,1)}, pred[16]{0:T(512)(128)(4,1)S(1)}, u32[]{:S(2)}) copy-start(pred[16]{0:T(512)(128)(4,1)S(1)} %get-tuple-element.23) | copy-start | bytes 52
  41.5 50.1 %copy-start.15 = (pred[16]{0:T(512)(128)(4,1)}, pred[16]{0:T(512)(128)(4,1)S(1)}, u32[]{:S(2)}) copy-start(pred[16]{0:T(512)(128)(4,1)S(1)} %get-tuple-element.24) | copy-start | bytes 52
  41.5 7.4 %collective-permute-start.2 = (bf16[16]{0:T(256)(128)(2,1)S(1)}, bf16[16]{0:T(256)(128)(2,1)S(1)}, u32[]{:S(2)}, u32[]{:S(2)}) collective-permute-start(bf16[16]{0:T(256)(128)(2,1)S(1)} %get-tuple-element.21), channel_id=1, source_target_pairs={{0,126},{2,0},{4,2},{6,4},{8,6},{10,8},{12,10},{14,12},{16,14},{18... | collective-permute-start | bytes 104 | tf_op jit(solution)/shard_map/ppermute | solution.py:11
  46.1 56.8 %copy-start.18 = (s32[16]{0:T(128)}, s32[16]{0:T(128)S(1)}, u32[]{:S(2)}) copy-start(s32[16]{0:T(128)S(1)} %convert_add_fusion.5) | copy-start | bytes 196
  46.2 50.4 %copy-start.28 = (s32[16]{0:T(128)}, s32[16]{0:T(128)S(1)}, u32[]{:S(2)}) copy-start(s32[16]{0:T(128)S(1)} %convert_add_fusion) | copy-start | bytes 196
  46.2 55.7 %copy-start.26 = (s32[16]{0:T(128)}, s32[16]{0:T(128)S(1)}, u32[]{:S(2)}) copy-start(s32[16]{0:T(128)S(1)} %convert_add_fusion.1) | copy-start | bytes 196
  46.2 56.0 %copy-start.24 = (s32[16]{0:T(128)}, s32[16]{0:T(128)S(1)}, u32[]{:S(2)}) copy-start(s32[16]{0:T(128)S(1)} %convert_add_fusion.2) | copy-start | bytes 196
  48.9 53.7 %copy-start.22 = (s32[16]{0:T(128)}, s32[16]{0:T(128)S(1)}, u32[]{:S(2)}) copy-start(s32[16]{0:T(128)S(1)} %convert_add_fusion.3) | copy-start | bytes 196
  48.9 54.4 %copy-start.20 = (s32[16]{0:T(128)}, s32[16]{0:T(128)S(1)}, u32[]{:S(2)}) copy-start(s32[16]{0:T(128)S(1)} %convert_add_fusion.4) | copy-start | bytes 196
  70.4 32.9 %collective-permute-start.3 = (bf16[16,16,192]{2,0,1:T(8,128)(2,1)S(1)}, bf16[16,16,192]{2,0,1:T(8,128)(2,1)S(1)}, u32[]{:S(2)}, u32[]{:S(2)}) collective-permute-start(bf16[16,16,192]{2,0,1:T(8,128)(2,1)S(1)} %fusion.15), channel_id=1, source_target_pairs={{0,126},{2,0},{4,2},{6,4},{8,6},{10,8},{12,10},{14,12},{16,14},{18... | collective-permute-start | bytes 294920 | tf_op jit(solution)/shard_map/ppermute | solution.py:11
  78.6 24.4 %collective-permute-start.1 = (bf16[16,16,192]{2,0,1:T(8,128)(2,1)S(1)}, bf16[16,16,192]{2,0,1:T(8,128)(2,1)S(1)}, u32[]{:S(2)}, u32[]{:S(2)}) collective-permute-start(bf16[16,16,192]{2,0,1:T(8,128)(2,1)S(1)} %fusion.16), channel_id=1, source_target_pairs={{0,2},{2,4},{4,6},{6,8},{8,10},{10,12},{12,14},{14,16},{16,18},{18... | collective-permute-start | bytes 294920 | tf_op jit(solution)/shard_map/ppermute | solution.py:11
  79.6 22.9 %collective-permute-start.5 = (bf16[16,16,192]{2,0,1:T(8,128)(2,1)S(1)}, bf16[16,16,192]{2,0,1:T(8,128)(2,1)S(1)}, u32[]{:S(2)}, u32[]{:S(2)}) collective-permute-start(bf16[16,16,192]{2,0,1:T(8,128)(2,1)S(1)} %fusion.14), channel_id=1, source_target_pairs={{0,4},{2,6},{4,8},{6,10},{8,12},{10,14},{12,16},{14,18},{16,20},{1... | collective-permute-start | bytes 294920 | tf_op jit(solution)/shard_map/ppermute | solution.py:11
  80.7 21.5 %collective-permute-start.7 = (bf16[16,16,192]{2,0,1:T(8,128)(2,1)S(1)}, bf16[16,16,192]{2,0,1:T(8,128)(2,1)S(1)}, u32[]{:S(2)}, u32[]{:S(2)}) collective-permute-start(bf16[16,16,192]{2,0,1:T(8,128)(2,1)S(1)} %fusion.13), channel_id=1, source_target_pairs={{0,124},{2,126},{4,0},{6,2},{8,4},{10,6},{12,8},{14,10},{16,12},{1... | collective-permute-start | bytes 294920 | tf_op jit(solution)/shard_map/ppermute | solution.py:11
  88.1 8.5 %collective-permute-start.11 = (bf16[16,16,192]{2,0,1:T(8,128)(2,1)S(1)}, bf16[16,16,192]{2,0,1:T(8,128)(2,1)S(1)}, u32[]{:S(2)}, u32[]{:S(2)}) collective-permute-start(bf16[16,16,192]{2,0,1:T(8,128)(2,1)S(1)} %fusion.11), channel_id=1, source_target_pairs={{0,66},{2,68},{4,70},{6,72},{8,74},{10,76},{12,78},{14,80},{16,82}... | collective-permute-start | bytes 294920 | tf_op jit(solution)/shard_map/ppermute | solution.py:11
  96.6 5.3 %collective-permute-start.9 = (bf16[16,16,192]{2,0,1:T(8,128)(2,1)S(1)}, bf16[16,16,192]{2,0,1:T(8,128)(2,1)S(1)}, u32[]{:S(2)}, u32[]{:S(2)}) collective-permute-start(bf16[16,16,192]{2,0,1:T(8,128)(2,1)S(1)} %fusion.12), channel_id=1, source_target_pairs={{0,64},{2,66},{4,68},{6,70},{8,72},{10,74},{12,76},{14,78},{16,80}... | collective-permute-start | bytes 294920 | tf_op jit(solution)/shard_map/ppermute | solution.py:11
  172.4 32.1 %copy-start.27 = (s32[16]{0:T(128)S(1)}, s32[16]{0:T(128)}, u32[]{:S(2)}) copy-start(s32[16]{0:T(128)} %copy-done.26) | copy-start | bytes 196
  183.6 15.4 %collective-permute-start.17 = (bf16[16,16,192]{2,0,1:T(8,128)(2,1)S(1)}, bf16[16,16,192]{2,0,1:T(8,128)(2,1)S(1)}, u32[]{:S(2)}, u32[]{:S(2)}) collective-permute-start(bf16[16,16,192]{2,0,1:T(8,128)(2,1)S(1)} %fusion.5), channel_id=1, source_target_pairs={{0,66},{2,68},{4,70},{6,72},{8,74},{10,76},{12,78},{14,80},{16,82}... | collective-permute-start | bytes 294920 | tf_op jit(solution)/shard_map/ppermute | solution.py:11
  188.1 17.9 %collective-permute-start.13 = (bf16[16,16,192]{2,0,1:T(8,128)(2,1)S(1)}, bf16[16,16,192]{2,0,1:T(8,128)(2,1)S(1)}, u32[]{:S(2)}, u32[]{:S(2)}) collective-permute-start(bf16[16,16,192]{2,0,1:T(8,128)(2,1)S(1)} %fusion.9), channel_id=1, source_target_pairs={{0,126},{2,0},{4,2},{6,4},{8,6},{10,8},{12,10},{14,12},{16,14},{18... | collective-permute-start | bytes 294920 | tf_op jit(solution)/shard_map/ppermute | solution.py:11
  191.8 13.9 %collective-permute-start.12 = (bf16[16,16,192]{2,0,1:T(8,128)(2,1)S(1)}, bf16[16,16,192]{2,0,1:T(8,128)(2,1)S(1)}, u32[]{:S(2)}, u32[]{:S(2)}) collective-permute-start(bf16[16,16,192]{2,0,1:T(8,128)(2,1)S(1)} %fusion.10), channel_id=1, source_target_pairs={{0,2},{2,4},{4,6},{6,8},{8,10},{10,12},{12,14},{14,16},{16,18},{18... | collective-permute-start | bytes 294920 | tf_op jit(solution)/shard_map/ppermute | solution.py:11
  191.8 13.5 %collective-permute-start.14 = (bf16[16,16,192]{2,0,1:T(8,128)(2,1)S(1)}, bf16[16,16,192]{2,0,1:T(8,128)(2,1)S(1)}, u32[]{:S(2)}, u32[]{:S(2)}) collective-permute-start(bf16[16,16,192]{2,0,1:T(8,128)(2,1)S(1)} %fusion.8), channel_id=1, source_target_pairs={{0,4},{2,6},{4,8},{6,10},{8,12},{10,14},{12,16},{14,18},{16,20},{1... | collective-permute-start | bytes 294920 | tf_op jit(solution)/shard_map/ppermute | solution.py:11
  192.1 12.8 %collective-permute-start.15 = (bf16[16,16,192]{2,0,1:T(8,128)(2,1)S(1)}, bf16[16,16,192]{2,0,1:T(8,128)(2,1)S(1)}, u32[]{:S(2)}, u32[]{:S(2)}) collective-permute-start(bf16[16,16,192]{2,0,1:T(8,128)(2,1)S(1)} %fusion.7), channel_id=1, source_target_pairs={{0,124},{2,126},{4,0},{6,2},{8,4},{10,6},{12,8},{14,10},{16,12},{1... | collective-permute-start | bytes 294920 | tf_op jit(solution)/shard_map/ppermute | solution.py:11
  199.0 5.6 %collective-permute-start.16 = (bf16[16,16,192]{2,0,1:T(8,128)(2,1)S(1)}, bf16[16,16,192]{2,0,1:T(8,128)(2,1)S(1)}, u32[]{:S(2)}, u32[]{:S(2)}) collective-permute-start(bf16[16,16,192]{2,0,1:T(8,128)(2,1)S(1)} %fusion.6), channel_id=1, source_target_pairs={{0,64},{2,66},{4,68},{6,70},{8,72},{10,74},{12,76},{14,78},{16,80}... | collective-permute-start | bytes 294920 | tf_op jit(solution)/shard_map/ppermute | solution.py:11
  (17 other events, 182.9 us)
Sparse Core Ops, SparseCore 0:
  27.2 32.4 all-reduce.12
  134.2 23.9 all-reduce.10
where the time goes:
time: 228 us; the launch traced here: 227 us
  waiting for transfers between devices  52.1 us (23%)
  starting transfers between devices  46.6 us (20%)
  local copies, waits for them, and re-layouts  45.9 us (20%)
  matrix products  29.6 us (13%)
  blocking collectives  22.3 us (10%)
  other arithmetic  15.3 us (7%)
  between operations  14.8 us (6%)
    ppermute x18, starting transfers between devices, from_behind(): lax.ppermute(x, axis, [(i, (i + by) % devices) for i in range(devices)])  46.5 us
    psum x2, waiting for transfers between devices, on_device(): diag_sum, off_sum = lax.psum((diag_part, off_part), 'blk')  34.9 us
    all_gather x3, blocking collectives, precondition(): return lax.all_gather(mine, 'blk', axis=2, tiled=True)  22.3 us
    gather x12, local copies, waits for them, and re-layouts, on_device(): picked = off_faces[entry[:, face], face]  20 us
    ppermute x18, waiting for transfers between devices, from_behind(): lax.ppermute(x, axis, [(i, (i + by) % devices) for i in range(devices)])  17.2 us
    convert_element_type x12, other arithmetic, on_device(): sending.astype(jnp.bfloat16)  9.32 us
    dot_general x2, matrix products, on_device(): jnp.einsum('nkrc,nar->nkac', off_blocks, xh, preferred_element_type=jnp.f...  9.28 us
    dot_general x2, matrix products, on_device(): jnp.einsum('nm,mac->nac', local_placer, off_sum, precision=lax.Precision....  7.35 us
  transfers between devices with their start and end apart: 20, of which 6 were waited for; matrix products, arithmetic and copies ran while one was open for 5% of the time, Pallas kernels for 0%

commit v1 on v0

v1 whole, which is shorter than its diff:
```python
import functools

import jax
import jax.numpy as jnp
from jax import lax
from jax.experimental import pallas as pl
from jax.experimental.pallas import tpu as pltpu
from jax.sharding import PartitionSpec as P

ROWS = 32
FAN = 6
ADJ = 16
WIDTH = 192
HALF = 96
CAP = 16
BODY = CAP * ADJ * WIDTH // 128
WIDE = CAP * ADJ
FACES = ((0, 2), (1, 3), (4, 5))
SLOTS = ROWS + FAN * CAP
CHUNKS = 8
PER = ROWS // CHUNKS
VMEM_LIMIT = 48 * 1024 * 1024

VM = pl.BlockSpec(memory_space=pltpu.VMEM)
SM = pl.BlockSpec(memory_space=pltpu.SMEM)
ANY = pl.BlockSpec(memory_space=pl.ANY)


def my_face(p, core):
    return jnp.where(core == 0, FACES[p][0], FACES[p][1])


def load_blocks(hbm, vmem, sems):
    copies = []
    for chunk in range(CHUNKS):
        part = pl.ds(chunk * PER, PER)
        copies.append([pltpu.make_async_copy(h.at[part], v.at[part], sems.at[k, chunk]) for k, (h, v) in enumerate(zip(hbm, vmem))])
    return copies


def terms_phase(copies, x_half, off_v, diag_v, owner, local, sums, labels):
    own = lax.axis_index("rows")
    sums[...] = jnp.zeros(sums.shape, sums.dtype)
    if labels is not None:
        labels[...] = jnp.zeros(labels.shape, labels.dtype)

    def row(i, ranks):
        x = x_half[i].astype(jnp.bfloat16)
        terms = [jnp.dot(x, diag_v[i], preferred_element_type=jnp.float32)]
        places, after = [i], []
        for k in range(FAN):
            terms.append(jnp.dot(x, off_v[i, k], preferred_element_type=jnp.float32))
            remote = owner[k, i] != own
            places.append(jnp.where(remote, ROWS + k * CAP + ranks[k], local[k, i]))
            after.append(ranks[k] + remote.astype(jnp.int32))
        for place, term in zip(places, terms):
            sums[place] = sums[place] + term
        if labels is not None:
            for k in range(FAN):
                labels[pl.ds(places[k + 1], 1), :] = jnp.full((1, 128), local[k, i] + 1, jnp.int32).astype(jnp.float32)
        return tuple(after)

    ranks = (jnp.int32(0),) * FAN
    for chunk in range(CHUNKS):
        for copy in copies[chunk]:
            copy.wait()
        ranks = lax.fori_loop(chunk * PER, (chunk + 1) * PER, row, ranks, unroll=True)


def pack(sums, face):
    slots = pl.ds(ROWS + face * CAP, CAP)
    wide = sums[slots, :, 0:128].reshape(WIDE, 128)
    low = sums[pl.ds(ROWS + face * CAP, CAP // 2), :, 128:WIDTH]
    high = sums[pl.ds(ROWS + face * CAP + CAP // 2, CAP // 2), :, 128:WIDTH]
    narrow = jnp.concatenate([low, high], axis=2).reshape(WIDE // 2, 128)
    return wide, narrow


def emit(sums, labels, mine, theirs, partial):
    core = lax.axis_index("blk")
    partial[...] = sums[0:ROWS]
    for p in range(len(FACES)):
        face = my_face(p, core)
        wide, narrow = pack(sums, face)
        mine[p][0:WIDE] = wide
        mine[p][WIDE:BODY] = narrow
        if labels is not None:
            mine[p][BODY:] = labels[pl.ds(ROWS + face * CAP, CAP), :]
        wide, narrow = pack(sums, my_face(p, 1 - core))
        theirs[p][0:WIDE] = wide.astype(jnp.bfloat16)
        theirs[p][WIDE:BODY] = narrow.astype(jnp.bfloat16)
        if labels is not None:
            theirs[p][BODY:] = jnp.zeros((CAP, 128), jnp.bfloat16)


def solve(field, block):
    return lax.dot_general(field.astype(jnp.bfloat16), block, (((1,), (1,)), ((), ())), preferred_element_type=jnp.float32)


def first_kernel(off, diag, precond, rhs, owner, local, x_half, partial, m0, m1, m2, t0, t1, t2, off_v, diag_v, pre_v, sums, labels, sems, pre_sem):
    pre_copy = pltpu.make_async_copy(precond, pre_v, pre_sem)
    pre_copy.start()
    copies = load_blocks((off, diag), (off_v, diag_v), sems)
    for chunk in copies:
        for copy in chunk:
            copy.start()
    pre_copy.wait()

    def row(n, _):
        x_half[n] = solve(rhs[n], pre_v[n])
        return 0

    lax.fori_loop(0, ROWS, row, 0, unroll=4)
    terms_phase(copies, x_half, off_v, diag_v, owner, local, sums, labels)
    emit(sums, labels, (m0, m1, m2), (t0, t1, t2), partial)


def place(messages, label_of, first, narrow_sum, wide_sum):
    wide_sum[...] = jnp.zeros(wide_sum.shape, wide_sum.dtype)
    narrow_sum[...] = jnp.zeros(narrow_sum.shape, narrow_sum.dtype)
    lane = lax.broadcasted_iota(jnp.int32, (ADJ, 128), 1)
    for p, message in enumerate(messages):
        for s in range(CAP // 2):
            at = []
            for slot in (s, s + CAP // 2):
                label = label_of(first + p * CAP + slot)
                at.append(jnp.where(label == 0, ROWS, label - 1))
                wide_sum[at[-1]] += message[slot * ADJ : (slot + 1) * ADJ].astype(jnp.float32)
            both = message[WIDE + s * ADJ : WIDE + (s + 1) * ADJ].astype(jnp.float32)
            narrow_sum[at[0]] += jnp.where(lane < 64, both, 0.0)
            narrow_sum[at[1]] += jnp.where(lane < 64, 0.0, both)


def read_labels(messages, row_v, labels_s, sem):
    found = jnp.concatenate([m[BODY:].astype(jnp.float32) for m in messages], axis=0)
    rows = lax.broadcasted_iota(jnp.int32, found.shape, 0)
    lanes = lax.broadcasted_iota(jnp.int32, found.shape, 1)
    row = jnp.sum(jnp.where(rows == lanes, found, 0.0), axis=0, keepdims=True)
    row_v[...] = row.astype(jnp.int32)
    copy = pltpu.make_async_copy(row_v, labels_s, sem)
    copy.start()
    return copy


def residual_of(n, rhs, ours, other, wides, narrows):
    narrow = narrows[0][n] + narrows[1][n]
    narrow = narrow + pltpu.roll(narrow, 64, 1)
    got = jnp.concatenate([wides[0][n] + wides[1][n], narrow[:, 0:64]], axis=1)
    return rhs[n] - ((ours[n] + other[n]) + got)


def middle_kernel(off, diag, precond, rhs, owner, local, x_before, ours, other, g0, g1, g2, f0, f1, f2,
                  residual, labels_out, partial, m0, m1, m2, t0, t1, t2,
                  off_v, diag_v, pre_v, sums, x_half, wide_a, wide_b, narrow_a, narrow_b, row_v, sems, pre_sem, label_sem):
    pre_copy = pltpu.make_async_copy(precond, pre_v, pre_sem)
    pre_copy.start()
    copies = load_blocks((off, diag), (off_v, diag_v), sems)
    for chunk in copies:
        for copy in chunk:
            copy.start()
    label_copy = read_labels((g0, g1, g2, f0, f1, f2), row_v, labels_out, label_sem)
    label_copy.wait()
    label_of = lambda at: labels_out[0, at]
    place((g0, g1, g2), label_of, 0, narrow_a, wide_a)
    place((f0, f1, f2), label_of, 3 * CAP, narrow_b, wide_b)
    pre_copy.wait()

    def row(n, _):
        left = residual_of(n, rhs, ours, other, (wide_a, wide_b), (narrow_a, narrow_b))
        residual[n] = left
        x_half[n] = x_before[n] + solve(left, pre_v[n])
        return 0

    lax.fori_loop(0, ROWS, row, 0, unroll=4)
    terms_phase(copies, x_half, off_v, diag_v, owner, local, sums, None)
    emit(sums, None, (m0, m1, m2), (t0, t1, t2), partial)


def last_kernel(precond, precond_other, rhs, before, ours, other, labels, g0, g1, g2, f0, f1, f2,
                adjoint, residual, pre_v, wide_a, wide_b, narrow_a, narrow_b, pre_sem):
    core = lax.axis_index("blk")
    mine = pltpu.make_async_copy(precond, pre_v.at[core], pre_sem.at[0])
    theirs = pltpu.make_async_copy(precond_other, pre_v.at[1 - core], pre_sem.at[1])
    mine.start()
    theirs.start()
    label_of = lambda at: labels[0, at]
    place((g0, g1, g2), label_of, 0, narrow_a, wide_a)
    place((f0, f1, f2), label_of, 3 * CAP, narrow_b, wide_b)
    mine.wait()
    theirs.wait()

    def row(n, _):
        left = residual_of(n, rhs, ours, other, (wide_a, wide_b), (narrow_a, narrow_b))
        residual[n] = left
        fields = jnp.concatenate([left, before[n], rhs[n]], axis=0)
        for half in range(2):
            three = solve(fields, pre_v[half, n])
            adjoint[n, :, half * HALF : (half + 1) * HALF] = (three[2 * ADJ :] + three[ADJ : 2 * ADJ]) + three[0:ADJ]
        return 0

    lax.fori_loop(0, ROWS, row, 0, unroll=4)


def params():
    return pltpu.CompilerParams(vmem_limit_bytes=VMEM_LIMIT)


def on_device(off_blocks, diag_blocks, precond, adj_rhs, col_owner, col_local):
    nrows = lax.axis_size("rows")
    offsets = (1, nrows - 1, 2, nrows - 2, nrows // 2, nrows // 2 + 1)
    shape = jax.ShapeDtypeStruct
    field = shape((ROWS, ADJ, WIDTH), jnp.float32)
    half_field = shape((ROWS, ADJ, HALF), jnp.float32)

    def across(x):
        return lax.ppermute(x, "blk", [(0, 1), (1, 0)])

    def to_faces(x, p):
        pairs = [(2 * i + c, 2 * ((i + offsets[FACES[p][c]]) % nrows) + c) for i in range(nrows) for c in range(2)]
        return lax.ppermute(x, ("rows", "blk"), pairs)

    def exchange(partial, mine, theirs):
        got = []
        for p in range(len(FACES)):
            sending = (mine[p] + across(theirs[p]).astype(jnp.float32)).astype(jnp.bfloat16)
            got.append(to_faces(sending, p))
        other = across(partial)
        forwarded = [across(g) for g in got]
        return other, got, forwarded

    blocks = [
        pltpu.VMEM((ROWS, FAN, HALF, WIDTH), jnp.bfloat16),
        pltpu.VMEM((ROWS, HALF, WIDTH), jnp.bfloat16),
        pltpu.VMEM((ROWS, HALF, WIDTH), jnp.bfloat16),
        pltpu.VMEM((SLOTS, ADJ, WIDTH), jnp.float32),
    ]
    sums_of_messages = [pltpu.VMEM((ROWS + 1, ADJ, 128), jnp.float32)] * 4
    owner, local = col_owner.T, col_local.T
    precond_other = across(precond)

    x_half, partial, *messages = pl.pallas_call(
        first_kernel,
        out_shape=[half_field, field] + [shape((BODY + CAP, 128), jnp.float32)] * 3 + [shape((BODY + CAP, 128), jnp.bfloat16)] * 3,
        in_specs=[ANY, ANY, ANY, VM, SM, SM],
        out_specs=[VM] * 8,
        scratch_shapes=blocks + [pltpu.VMEM((SLOTS, 128), jnp.float32), pltpu.SemaphoreType.DMA((2, CHUNKS)), pltpu.SemaphoreType.DMA],
        compiler_params=params(),
        name="first_terms",
    )(off_blocks, diag_blocks, precond, adj_rhs, owner, local)
    other, got, forwarded = exchange(partial, messages[:3], messages[3:])

    before, labels, partial, *messages = pl.pallas_call(
        middle_kernel,
        out_shape=[field, shape((1, 128), jnp.int32), field] + [shape((BODY, 128), jnp.float32)] * 3 + [shape((BODY, 128), jnp.bfloat16)] * 3,
        in_specs=[ANY, ANY, ANY, VM, SM, SM] + [VM] * 9,
        out_specs=[VM, SM] + [VM] * 7,
        scratch_shapes=blocks + [pltpu.VMEM((ROWS, ADJ, HALF), jnp.float32)] + sums_of_messages
        + [pltpu.VMEM((1, 128), jnp.int32), pltpu.SemaphoreType.DMA((2, CHUNKS)), pltpu.SemaphoreType.DMA, pltpu.SemaphoreType.DMA],
        compiler_params=params(),
        name="residual_and_terms",
    )(off_blocks, diag_blocks, precond, adj_rhs, owner, local, x_half, partial, other, *got, *forwarded)
    other, got, forwarded = exchange(partial, messages[:3], messages[3:])

    return pl.pallas_call(
        last_kernel,
        out_shape=[field, field],
        in_specs=[ANY, ANY] + [VM] * 4 + [SM] + [VM] * 6,
        out_specs=[VM] * 2,
        scratch_shapes=[pltpu.VMEM((2, ROWS, HALF, WIDTH), jnp.bfloat16)] + sums_of_messages + [pltpu.SemaphoreType.DMA((2,))],
        compiler_params=params(),
        name="last_residual",
    )(precond, precond_other, adj_rhs, before, partial, other, labels, *got, *forwarded)


def solution(mesh):
    in_specs = (
        P("rows", None, "blk", None),
        P("rows", "blk", None),
        P("rows", "blk", None),
        P("rows", None, None),
        P("rows", None),
        P("rows", None),
    )
    out_specs = (P("rows", None, None), P("rows", None, None))

    def program(*arrays):
        return tuple(on_device(*arrays))

    return jax.shard_map(program, mesh=mesh, in_specs=in_specs, out_specs=out_specs, check_vma=False)
```

time: 228 us -> 66.5 us (0.29)
  local copies, waits for them, and re-layouts: 45.9 us -> 3.83 us
  waiting for transfers between devices: 52.1 us -> 13.8 us
  matrix products: 29.6 us -> 0 us
  blocking collectives: 22.3 us -> 0 us
  Pallas kernels: 0 us -> 21.6 us
  starting transfers between devices: 46.6 us -> 26 us
  other arithmetic: 15.3 us -> 0.16 us
  between operations: 14.8 us -> 0.74 us
    psum x2 -> x0, waiting for transfers between devices: 34.9 us -> none  [on_device(): diag_sum, off_sum = lax.psum((diag_part, off_part), 'blk')]
    dot_general x21 -> x0, matrix products: 29.6 us -> none  [the longest x2 9.28 us: on_device(): jnp.einsum('nkrc,nar->nkac', off_blocks, xh, preferred_element_type=jnp.f...]
    all_gather x3 -> x0, blocking collectives: 22.3 us -> none  [precondition(): return lax.all_gather(mine, 'blk', axis=2, tiled=True)]
    pallas_call x0 -> x3, Pallas kernels: none -> 21.6 us  [the longest x1 9.13 us: on_device(): pl.pallas_call(middle_kernel, out_shape=[field, shape((1, 128), jnp.int32...]
    ppermute x18 -> x21, starting transfers between devices: 46.5 us -> 26 us  [the longest x6 19.5 us: to_faces(): return lax.ppermute(x, ('rows', 'blk'), pairs)]
    gather x12 -> x0, local copies, waits for them, and re-layouts: 20 us -> none  [on_device(): picked = off_faces[entry[:, face], face]]
    convert_element_type x13 -> x6, other arithmetic: 9.33 us -> 0.16 us  [exchange(): (mine[p] + across(theirs[p]).astype(jnp.float32)).astype(jnp.bfloat16)]
    reshape x2 -> x0, local copies, waits for them, and re-layouts: 7.04 us -> none  [on_device(): off_part = off_part.reshape(rows_here * fan, nadj_cols, width)]
  transfers between devices with their start and end apart: 20 -> 21, of which waited for: 6 -> 9; matrix products, arithmetic and copies ran while one was open for 5% -> 0% of each run, Pallas kernels for 0% -> 14%
where the time goes in v1:
time: 66.5 us; the launch traced here: 66.2 us
  starting transfers between devices  26 us (39%)
  Pallas kernels  21.6 us (32%)
  waiting for transfers between devices  13.8 us (21%)
  local copies, waits for them, and re-layouts  3.83 us (6%)
  between operations  0.74 us (1%)
    ppermute x6, starting transfers between devices, to_faces(): return lax.ppermute(x, ('rows', 'blk'), pairs)  19.5 us
    ppermute x6, waiting for transfers between devices, to_faces(): return lax.ppermute(x, ('rows', 'blk'), pairs)  11 us
    pallas_call x1, Pallas kernels, on_device(): pl.pallas_call(middle_kernel, out_shape=[field, shape((1, 128), jnp.int32...  9.13 us
    pallas_call x1, Pallas kernels, on_device(): pl.pallas_call(first_kernel, out_shape=[half_field, field] + [shape((BODY...  6.81 us
    ppermute x15, starting transfers between devices, across(): return lax.ppermute(x, 'blk', [(0, 1), (1, 0)])  6.5 us
    pallas_call x1, Pallas kernels, on_device(): pl.pallas_call(last_kernel, out_shape=[field, field], in_specs=[ANY, ANY]...  5.67 us
    unnamed x14, local copies, waits for them, and re-layouts  3.83 us
    ppermute x15, waiting for transfers between devices, across(): return lax.ppermute(x, 'blk', [(0, 1), (1, 0)])  2.79 us
  transfers between devices with their start and end apart: 21, of which 9 were waited for; matrix products, arithmetic and copies ran while one was open for 0% of the time, Pallas kernels for 14%

profile of v1, /device:TPU:1, one launch (start us, length us, event | category | flops | bytes accessed | tf_op | source)
XLA Modules:
  0.0 66.2 jit_solution(3784569631182632148)
XLA Ops:
  0.6 1.4 %copy-done = bf16[32,96,192]{2,1,0:T(8,128)(2,1)S(1)} copy-done((bf16[32,96,192]{2,1,0:T(8,128)(2,1)S(1)}, bf16[32,96,192]{2,1,0:T(8,128)(2,1)}, u32[]{:S(2)}) %copy-start) | copy-done | bytes 1179672
  2.0 1.0 %copy-done.1 = f32[32,16,192]{2,1,0:T(8,128)S(1)} copy-done((f32[32,16,192]{2,1,0:T(8,128)S(1)}, f32[32,16,192]{2,1,0:T(8,128)}, u32[]{:S(2)}) %copy-start.1) | copy-done | bytes 393240
  3.1 0.7 %copy-done.3 = s32[32,6]{0,1:T(8,128)S(1)} copy-done((s32[32,6]{0,1:T(8,128)S(1)}, s32[32,6]{0,1:T(8,128)}, u32[]{:S(2)}) %copy-start.3) | copy-done | bytes 792
  3.8 0.7 %copy-done.5 = s32[32,6]{0,1:T(8,128)S(1)} copy-done((s32[32,6]{0,1:T(8,128)S(1)}, s32[32,6]{0,1:T(8,128)}, u32[]{:S(2)}) %copy-start.5) | copy-done | bytes 792
  4.5 6.8 %first_terms.1 = (f32[32,16,96]{2,1,0:T(8,128)S(1)}, f32[32,16,192]{2,1,0:T(8,128)S(1)}, f32[400,128]{1,0:T(8,128)S(1)}, f32[400,128]{1,0:T(8,128)S(1)}, f32[400...) custom-call(bf16[32,6,96,192]{3,2,1,0:T(8,128)(2,1)} %off.3, ...), custom_call_target="tpu_custom_call" | custom-call | tf_op jit(solution)/shard_map/first_terms/pallas_call | solution.py:241
  11.3 1.5 %collective-permute-start.6 = (bf16[400,128]{1,0:T(8,128)(2,1)S(1)}, bf16[400,128]{1,0:T(8,128)(2,1)S(1)}, u32[]{:S(2)}, u32[]{:S(2)}) collective-permute-start(bf16[400,128]{1,0:T(8,128)(2,1)S(1)} %get-tuple-element.26), channel_id=1, source_target_pairs={{0,1},{1,0},{2,3},{3,2},{4,5},{5,4},{6,7},{7,6},{8,9},{9,8},{10,11... | collective-permute-start | bytes 307208 | tf_op jit(solution)/shard_map/ppermute | solution.py:216
  12.9 0.4 collective-permute-start.4
  13.3 0.1 collective-permute-start.1
  13.4 0.3 collective-permute-done.6
  13.8 3.9 %collective-permute-start.7 = (bf16[400,128]{1,0:T(8,128)(2,1)S(1)}, bf16[400,128]{1,0:T(8,128)(2,1)S(1)}, u32[]{:S(2)}, u32[]{:S(2)}) collective-permute-start(bf16[400,128]{1,0:T(8,128)(2,1)S(1)} %add_convert_fusion), channel_id=1, source_target_pairs={{0,64},{1,67},{2,66},{3,69},{4,68},{5,71},{6,70},{7,73},{8,72},{9,... | collective-permute-start | bytes 307208 | tf_op jit(solution)/shard_map/ppermute | solution.py:220
  17.7 2.7 %collective-permute-start.3 = (bf16[400,128]{1,0:T(8,128)(2,1)S(1)}, bf16[400,128]{1,0:T(8,128)(2,1)S(1)}, u32[]{:S(2)}, u32[]{:S(2)}) collective-permute-start(bf16[400,128]{1,0:T(8,128)(2,1)S(1)} %add_convert_fusion.2), channel_id=1, source_target_pairs={{0,2},{1,5},{2,4},{3,7},{4,6},{5,9},{6,8},{7,11},{8,10},{9,13},{10... | collective-permute-start | bytes 307208 | tf_op jit(solution)/shard_map/ppermute | solution.py:220
  20.4 4.6 %collective-permute-start.5 = (bf16[400,128]{1,0:T(8,128)(2,1)S(1)}, bf16[400,128]{1,0:T(8,128)(2,1)S(1)}, u32[]{:S(2)}, u32[]{:S(2)}) collective-permute-start(bf16[400,128]{1,0:T(8,128)(2,1)S(1)} %add_convert_fusion.1), channel_id=1, source_target_pairs={{0,126},{1,125},{2,0},{3,127},{4,2},{5,1},{6,4},{7,3},{8,6},{9,5},... | collective-permute-start | bytes 307208 | tf_op jit(solution)/shard_map/ppermute | solution.py:220
  25.1 0.5 collective-permute-start.10
  25.6 2.4 %collective-permute-done.3.g0 = bf16[400,128]{1,0:T(8,128)(2,1)S(1)} collective-permute-done((bf16[400,128]{1,0:T(8,128)(2,1)S(1)}, bf16[400,128]{1,0:T(8,128)(2,1)S(1)}, u32[]{:S(2)}, u32[]{:S(2)}) %collective-permute-start.3) | collective-permute-done | bytes 102432 | tf_op jit(solution)/shard_map/ppermute | solution.py:220
  28.0 0.5 collective-permute-start.9
  28.5 0.8 %collective-permute-done.8.f0 = bf16[400,128]{1,0:T(8,128)(2,1)S(1)} collective-permute-done((bf16[400,128]{1,0:T(8,128)(2,1)S(1)}, bf16[400,128]{1,0:T(8,128)(2,1)S(1)}, u32[]{:S(2)}, u32[]{:S(2)}) %collective-permute-start.8) | collective-permute-done | bytes 102432 | tf_op jit(solution)/shard_map/ppermute | solution.py:216
  29.3 0.2 collective-permute-done.9.f1
  29.5 9.1 %residual_and_terms.1 = (f32[32,16,192]{2,1,0:T(8,128)S(1)}, s32[1,128]{1,0:T(1,128)S(1)}, f32[32,16,192]{2,1,0:T(8,128)S(1)}, f32[384,128]{1,0:T(8,128)S(1)}, f...) custom-call(bf16[32,6,96,192]{3,2,1,0:T(8,128)(2,1)} %off.3, ...), custom_call_target="tpu_custom_call" | custom-call | tf_op jit(solution)/shard_map/residual_and_terms/pallas_call | solution.py:252
  38.6 0.4 collective-permute-start.16
  39.1 0.1 collective-permute-start.14
  39.2 0.4 collective-permute-start.12
  39.6 0.1 collective-permute-start.11
  39.7 0.3 collective-permute-done.16
  40.1 0.2 collective-permute-done.14
  40.4 8.2 %collective-permute-start.15 = (bf16[384,128]{1,0:T(8,128)(2,1)S(1)}, bf16[384,128]{1,0:T(8,128)(2,1)S(1)}, u32[]{:S(2)}, u32[]{:S(2)}) collective-permute-start(bf16[384,128]{1,0:T(8,128)(2,1)S(1)} %add_convert_fusion.4), channel_id=1, source_target_pairs={{0,126},{1,125},{2,0},{3,127},{4,2},{5,1},{6,4},{7,3},{8,6},{9,5},... | collective-permute-start | bytes 294920 | tf_op jit(solution)/shard_map/ppermute | solution.py:220
  48.7 0.3 collective-permute-start.20
  48.9 2.0 %collective-permute-done.15.g1 = bf16[384,128]{1,0:T(8,128)(2,1)S(1)} collective-permute-done((bf16[384,128]{1,0:T(8,128)(2,1)S(1)}, bf16[384,128]{1,0:T(8,128)(2,1)S(1)}, u32[]{:S(2)}, u32[]{:S(2)}) %collective-permute-start.15) | collective-permute-done | bytes 98336 | tf_op jit(solution)/shard_map/ppermute | solution.py:220
  50.9 0.7 %collective-permute-start.19 = (bf16[384,128]{1,0:T(8,128)(2,1)S(1)}, bf16[384,128]{1,0:T(8,128)(2,1)S(1)}, u32[]{:S(2)}, u32[]{:S(2)}) collective-permute-start(bf16[384,128]{1,0:T(8,128)(2,1)S(1)} %collective-permute-done.15.g1), channel_id=1, source_target_pairs={{0,1},{1,0},{2,3},{3,2},{4,5},{5,4},{6,7},{7,6},{8,9},{9,8},{10,11... | collective-permute-start | bytes 294920 | tf_op jit(solution)/shard_map/ppermute | solution.py:216
  51.6 6.7 %collective-permute-done.13.g0 = bf16[384,128]{1,0:T(8,128)(2,1)S(1)} collective-permute-done((bf16[384,128]{1,0:T(8,128)(2,1)S(1)}, bf16[384,128]{1,0:T(8,128)(2,1)S(1)}, u32[]{:S(2)}, u32[]{:S(2)}) %collective-permute-start.13) | collective-permute-done | bytes 98336 | tf_op jit(solution)/shard_map/ppermute | solution.py:220
  58.2 1.4 %collective-permute-start.18 = (bf16[384,128]{1,0:T(8,128)(2,1)S(1)}, bf16[384,128]{1,0:T(8,128)(2,1)S(1)}, u32[]{:S(2)}, u32[]{:S(2)}) collective-permute-start(bf16[384,128]{1,0:T(8,128)(2,1)S(1)} %collective-permute-done.13.g0), channel_id=1, source_target_pairs={{0,1},{1,0},{2,3},{3,2},{4,5},{5,4},{6,7},{7,6},{8,9},{9,8},{10,11... | collective-permute-start | bytes 294920 | tf_op jit(solution)/shard_map/ppermute | solution.py:216
  59.6 0.9 %collective-permute-done.18.f0 = bf16[384,128]{1,0:T(8,128)(2,1)S(1)} collective-permute-done((bf16[384,128]{1,0:T(8,128)(2,1)S(1)}, bf16[384,128]{1,0:T(8,128)(2,1)S(1)}, u32[]{:S(2)}, u32[]{:S(2)}) %collective-permute-start.18) | collective-permute-done | bytes 98336 | tf_op jit(solution)/shard_map/ppermute | solution.py:216
  60.5 5.7 %last_residual.1 = (f32[32,16,192]{2,1,0:T(8,128)}, f32[32,16,192]{2,1,0:T(8,128)}) custom-call(bf16[32,96,192]{2,1,0:T(8,128)(2,1)} %precond.5, bf16[32,96,192]{2,1,0:T(8,128)(2,1)S(1)} %collective-permute-done.precond_other, f32[32,16,192]{2,1,0:T(8,128)S(1)} %copy-done.2, f32[32,16,192]{2,1,0:T(8,128)S(1)} %get-tuple-element.27.before, ...), custom_call_target="tpu_custom_call" | custom-call | tf_op jit(solution)/shard_map/last_residual/pallas_call | solution.py:264
  (33 shorter events, 0.5 us)
Async XLA Ops:
  0.6 1.4 %copy-start = (bf16[32,96,192]{2,1,0:T(8,128)(2,1)S(1)}, bf16[32,96,192]{2,1,0:T(8,128)(2,1)}, u32[]{:S(2)}) copy-start(bf16[32,96,192]{2,1,0:T(8,128)(2,1)} %diag.3) | copy-start | bytes 3538948
  2.0 1.0 %copy-start.1 = (f32[32,16,192]{2,1,0:T(8,128)S(1)}, f32[32,16,192]{2,1,0:T(8,128)}, u32[]{:S(2)}) copy-start(f32[32,16,192]{2,1,0:T(8,128)} %rhs.5) | copy-start | bytes 1179652
  3.1 0.7 %copy-start.3 = (s32[32,6]{0,1:T(8,128)S(1)}, s32[32,6]{0,1:T(8,128)}, u32[]{:S(2)}) copy-start(s32[32,6]{0,1:T(8,128)} %param.10) | copy-start | bytes 2308
  3.8 0.7 %copy-start.5 = (s32[32,6]{0,1:T(8,128)S(1)}, s32[32,6]{0,1:T(8,128)}, u32[]{:S(2)}) copy-start(s32[32,6]{0,1:T(8,128)} %param.11) | copy-start | bytes 2308
  4.5 25.0 %copy-start.4 = (s32[32,6]{0,1:T(8,128)S(1)}, s32[32,6]{0,1:T(8,128)}, u32[]{:S(2)}) copy-start(s32[32,6]{0,1:T(8,128)} %param.10) | copy-start | bytes 2308
  4.5 25.0 %copy-start.6 = (s32[32,6]{0,1:T(8,128)S(1)}, s32[32,6]{0,1:T(8,128)}, u32[]{:S(2)}) copy-start(s32[32,6]{0,1:T(8,128)} %param.11) | copy-start | bytes 2308
  11.3 18.2 %copy-start.2 = (f32[32,16,192]{2,1,0:T(8,128)S(1)}, f32[32,16,192]{2,1,0:T(8,128)}, u32[]{:S(2)}) copy-start(f32[32,16,192]{2,1,0:T(8,128)} %rhs.5) | copy-start | bytes 1179652
  11.3 2.5 %collective-permute-start.6 = (bf16[400,128]{1,0:T(8,128)(2,1)S(1)}, bf16[400,128]{1,0:T(8,128)(2,1)S(1)}, u32[]{:S(2)}, u32[]{:S(2)}) collective-permute-start(bf16[400,128]{1,0:T(8,128)(2,1)S(1)} %get-tuple-element.26), channel_id=1, source_target_pairs={{0,1},{1,0},{2,3},{3,2},{4,5},{5,4},{6,7},{7,6},{8,9},{9,8},{10,11... | collective-permute-start | bytes 307208 | tf_op jit(solution)/shard_map/ppermute | solution.py:216
  12.8 4.9 %collective-permute-start.2 = (bf16[400,128]{1,0:T(8,128)(2,1)S(1)}, bf16[400,128]{1,0:T(8,128)(2,1)S(1)}, u32[]{:S(2)}, u32[]{:S(2)}) collective-permute-start(bf16[400,128]{1,0:T(8,128)(2,1)S(1)} %get-tuple-element.22), channel_id=1, source_target_pairs={{0,1},{1,0},{2,3},{3,2},{4,5},{5,4},{6,7},{7,6},{8,9},{9,8},{10,11... | collective-permute-start | bytes 307208 | tf_op jit(solution)/shard_map/ppermute | solution.py:216
  12.9 7.5 %collective-permute-start.4 = (bf16[400,128]{1,0:T(8,128)(2,1)S(1)}, bf16[400,128]{1,0:T(8,128)(2,1)S(1)}, u32[]{:S(2)}, u32[]{:S(2)}) collective-permute-start(bf16[400,128]{1,0:T(8,128)(2,1)S(1)} %get-tuple-element.24), channel_id=1, source_target_pairs={{0,1},{1,0},{2,3},{3,2},{4,5},{5,4},{6,7},{7,6},{8,9},{9,8},{10,11... | collective-permute-start | bytes 307208 | tf_op jit(solution)/shard_map/ppermute | solution.py:216
  13.3 16.2 %collective-permute-start.1 = (f32[32,16,192]{2,1,0:T(8,128)S(1)}, f32[32,16,192]{2,1,0:T(8,128)S(1)}, u32[]{:S(2)}, u32[]{:S(2)}) collective-permute-start(f32[32,16,192]{2,1,0:T(8,128)S(1)} %get-tuple-element.20.ours), channel_id=1, source_target_pairs={{0,1},{1,0},{2,3},{3,2},{4,5},{5,4},{6,7},{7,6},{8,9},{9,8},{10,11... | collective-permute-start | bytes 1179656 | tf_op jit(solution)/shard_map/ppermute | solution.py:216
  13.8 11.3 %collective-permute-start.7 = (bf16[400,128]{1,0:T(8,128)(2,1)S(1)}, bf16[400,128]{1,0:T(8,128)(2,1)S(1)}, u32[]{:S(2)}, u32[]{:S(2)}) collective-permute-start(bf16[400,128]{1,0:T(8,128)(2,1)S(1)} %add_convert_fusion), channel_id=1, source_target_pairs={{0,64},{1,67},{2,66},{3,69},{4,68},{5,71},{6,70},{7,73},{8,72},{9,... | collective-permute-start | bytes 307208 | tf_op jit(solution)/shard_map/ppermute | solution.py:220
  17.7 10.3 %collective-permute-start.3 = (bf16[400,128]{1,0:T(8,128)(2,1)S(1)}, bf16[400,128]{1,0:T(8,128)(2,1)S(1)}, u32[]{:S(2)}, u32[]{:S(2)}) collective-permute-start(bf16[400,128]{1,0:T(8,128)(2,1)S(1)} %add_convert_fusion.2), channel_id=1, source_target_pairs={{0,2},{1,5},{2,4},{3,7},{4,6},{5,9},{6,8},{7,11},{8,10},{9,13},{10... | collective-permute-start | bytes 307208 | tf_op jit(solution)/shard_map/ppermute | solution.py:220
  20.4 7.6 %collective-permute-start.5 = (bf16[400,128]{1,0:T(8,128)(2,1)S(1)}, bf16[400,128]{1,0:T(8,128)(2,1)S(1)}, u32[]{:S(2)}, u32[]{:S(2)}) collective-permute-start(bf16[400,128]{1,0:T(8,128)(2,1)S(1)} %add_convert_fusion.1), channel_id=1, source_target_pairs={{0,126},{1,125},{2,0},{3,127},{4,2},{5,1},{6,4},{7,3},{8,6},{9,5},... | collective-permute-start | bytes 307208 | tf_op jit(solution)/shard_map/ppermute | solution.py:220
  25.1 35.5 %collective-permute-start = (bf16[32,96,192]{2,1,0:T(8,128)(2,1)}, bf16[32,96,192]{2,1,0:T(8,128)(2,1)S(1)}, u32[]{:S(2)}, u32[]{:S(2)}) collective-permute-start(bf16[32,96,192]{2,1,0:T(8,128)(2,1)} %precond.5), channel_id=1, source_target_pairs={{0,1},{1,0},{2,3},{3,2},{4,5},{5,4},{6,7},{7,6},{8,9},{9,8},{10,11... | collective-permute-start | bytes 3538952 | tf_op jit(solution)/shard_map/ppermute | solution.py:216
  25.1 3.4 %collective-permute-start.10 = (bf16[400,128]{1,0:T(8,128)(2,1)S(1)}, bf16[400,128]{1,0:T(8,128)(2,1)S(1)}, u32[]{:S(2)}, u32[]{:S(2)}) collective-permute-start(bf16[400,128]{1,0:T(8,128)(2,1)S(1)} %collective-permute-done.7.g2), channel_id=1, source_target_pairs={{0,1},{1,0},{2,3},{3,2},{4,5},{5,4},{6,7},{7,6},{8,9},{9,8},{10,11... | collective-permute-start | bytes 307208 | tf_op jit(solution)/shard_map/ppermute | solution.py:216
  28.0 1.3 %collective-permute-start.8 = (bf16[400,128]{1,0:T(8,128)(2,1)S(1)}, bf16[400,128]{1,0:T(8,128)(2,1)S(1)}, u32[]{:S(2)}, u32[]{:S(2)}) collective-permute-start(bf16[400,128]{1,0:T(8,128)(2,1)S(1)} %collective-permute-done.3.g0), channel_id=1, source_target_pairs={{0,1},{1,0},{2,3},{3,2},{4,5},{5,4},{6,7},{7,6},{8,9},{9,8},{10,11... | collective-permute-start | bytes 307208 | tf_op jit(solution)/shard_map/ppermute | solution.py:216
  28.0 1.5 %collective-permute-start.9 = (bf16[400,128]{1,0:T(8,128)(2,1)S(1)}, bf16[400,128]{1,0:T(8,128)(2,1)S(1)}, u32[]{:S(2)}, u32[]{:S(2)}) collective-permute-start(bf16[400,128]{1,0:T(8,128)(2,1)S(1)} %collective-permute-done.5.g1), channel_id=1, source_target_pairs={{0,1},{1,0},{2,3},{3,2},{4,5},{5,4},{6,7},{7,6},{8,9},{9,8},{10,11... | collective-permute-start | bytes 307208 | tf_op jit(solution)/shard_map/ppermute | solution.py:216
  38.6 1.4 %collective-permute-start.16 = (bf16[384,128]{1,0:T(8,128)(2,1)S(1)}, bf16[384,128]{1,0:T(8,128)(2,1)S(1)}, u32[]{:S(2)}, u32[]{:S(2)}) collective-permute-start(bf16[384,128]{1,0:T(8,128)(2,1)S(1)} %get-tuple-element.35), channel_id=1, source_target_pairs={{0,1},{1,0},{2,3},{3,2},{4,5},{5,4},{6,7},{7,6},{8,9},{9,8},{10,11... | collective-permute-start | bytes 294920 | tf_op jit(solution)/shard_map/ppermute | solution.py:216
  39.1 1.3 %collective-permute-start.14 = (bf16[384,128]{1,0:T(8,128)(2,1)S(1)}, bf16[384,128]{1,0:T(8,128)(2,1)S(1)}, u32[]{:S(2)}, u32[]{:S(2)}) collective-permute-start(bf16[384,128]{1,0:T(8,128)(2,1)S(1)} %get-tuple-element.33), channel_id=1, source_target_pairs={{0,1},{1,0},{2,3},{3,2},{4,5},{5,4},{6,7},{7,6},{8,9},{9,8},{10,11... | collective-permute-start | bytes 294920 | tf_op jit(solution)/shard_map/ppermute | solution.py:216
  39.2 9.3 %collective-permute-start.12 = (bf16[384,128]{1,0:T(8,128)(2,1)S(1)}, bf16[384,128]{1,0:T(8,128)(2,1)S(1)}, u32[]{:S(2)}, u32[]{:S(2)}) collective-permute-start(bf16[384,128]{1,0:T(8,128)(2,1)S(1)} %get-tuple-element.31), channel_id=1, source_target_pairs={{0,1},{1,0},{2,3},{3,2},{4,5},{5,4},{6,7},{7,6},{8,9},{9,8},{10,11... | collective-permute-start | bytes 294920 | tf_op jit(solution)/shard_map/ppermute | solution.py:216
  39.6 21.0 %collective-permute-start.11 = (f32[32,16,192]{2,1,0:T(8,128)S(1)}, f32[32,16,192]{2,1,0:T(8,128)S(1)}, u32[]{:S(2)}, u32[]{:S(2)}) collective-permute-start(f32[32,16,192]{2,1,0:T(8,128)S(1)} %get-tuple-element.28.ours), channel_id=1, source_target_pairs={{0,1},{1,0},{2,3},{3,2},{4,5},{5,4},{6,7},{7,6},{8,9},{9,8},{10,11... | collective-permute-start | bytes 1179656 | tf_op jit(solution)/shard_map/ppermute | solution.py:216
  40.0 8.6 %collective-permute-start.17 = (bf16[384,128]{1,0:T(8,128)(2,1)S(1)}, bf16[384,128]{1,0:T(8,128)(2,1)S(1)}, u32[]{:S(2)}, u32[]{:S(2)}) collective-permute-start(bf16[384,128]{1,0:T(8,128)(2,1)S(1)} %add_convert_fusion.3), channel_id=1, source_target_pairs={{0,64},{1,67},{2,66},{3,69},{4,68},{5,71},{6,70},{7,73},{8,72},{9,... | collective-permute-start | bytes 294920 | tf_op jit(solution)/shard_map/ppermute | solution.py:220
  40.4 10.5 %collective-permute-start.15 = (bf16[384,128]{1,0:T(8,128)(2,1)S(1)}, bf16[384,128]{1,0:T(8,128)(2,1)S(1)}, u32[]{:S(2)}, u32[]{:S(2)}) collective-permute-start(bf16[384,128]{1,0:T(8,128)(2,1)S(1)} %add_convert_fusion.4), channel_id=1, source_target_pairs={{0,126},{1,125},{2,0},{3,127},{4,2},{5,1},{6,4},{7,3},{8,6},{9,5},... | collective-permute-start | bytes 294920 | tf_op jit(solution)/shard_map/ppermute | solution.py:220
  48.6 9.6 %collective-permute-start.13 = (bf16[384,128]{1,0:T(8,128)(2,1)S(1)}, bf16[384,128]{1,0:T(8,128)(2,1)S(1)}, u32[]{:S(2)}, u32[]{:S(2)}) collective-permute-start(bf16[384,128]{1,0:T(8,128)(2,1)S(1)} %add_convert_fusion.5), channel_id=1, source_target_pairs={{0,2},{1,5},{2,4},{3,7},{4,6},{5,9},{6,8},{7,11},{8,10},{9,13},{10... | collective-permute-start | bytes 294920 | tf_op jit(solution)/shard_map/ppermute | solution.py:220
  48.7 10.9 %collective-permute-start.20 = (bf16[384,128]{1,0:T(8,128)(2,1)S(1)}, bf16[384,128]{1,0:T(8,128)(2,1)S(1)}, u32[]{:S(2)}, u32[]{:S(2)}) collective-permute-start(bf16[384,128]{1,0:T(8,128)(2,1)S(1)} %collective-permute-done.17.g2), channel_id=1, source_target_pairs={{0,1},{1,0},{2,3},{3,2},{4,5},{5,4},{6,7},{7,6},{8,9},{9,8},{10,11... | collective-permute-start | bytes 294920 | tf_op jit(solution)/shard_map/ppermute | solution.py:216
  50.9 8.7 %collective-permute-start.19 = (bf16[384,128]{1,0:T(8,128)(2,1)S(1)}, bf16[384,128]{1,0:T(8,128)(2,1)S(1)}, u32[]{:S(2)}, u32[]{:S(2)}) collective-permute-start(bf16[384,128]{1,0:T(8,128)(2,1)S(1)} %collective-permute-done.15.g1), channel_id=1, source_target_pairs={{0,1},{1,0},{2,3},{3,2},{4,5},{5,4},{6,7},{7,6},{8,9},{9,8},{10,11... | collective-permute-start | bytes 294920 | tf_op jit(solution)/shard_map/ppermute | solution.py:216
  58.2 2.3 %collective-permute-start.18 = (bf16[384,128]{1,0:T(8,128)(2,1)S(1)}, bf16[384,128]{1,0:T(8,128)(2,1)S(1)}, u32[]{:S(2)}, u32[]{:S(2)}) collective-permute-start(bf16[384,128]{1,0:T(8,128)(2,1)S(1)} %collective-permute-done.13.g0), channel_id=1, source_target_pairs={{0,1},{1,0},{2,3},{3,2},{4,5},{5,4},{6,7},{7,6},{8,9},{9,8},{10,11... | collective-permute-start | bytes 294920 | tf_op jit(solution)/shard_map/ppermute | solution.py:216

commit v2 on v0

v2 whole, which is shorter than its diff:
```python
import jax
import jax.numpy as jnp
from jax import lax
from jax.experimental import pallas as pl
from jax.experimental.pallas import tpu as pltpu
from jax.sharding import PartitionSpec as P

ROWS = 32
FAN = 6
ADJ = 16
WIDTH = 192
HALF = 96
CAP = 16
WIDE = CAP * ADJ
BODY = WIDE + WIDE // 2
NEAR, SEAM, FAR = 0, 1, 2
ORDER = (FAR, SEAM, NEAR)
FACES = (
    ((0, 1, 0, 1), (2, 2, 3, 3)),
    ((1, 0, 1, 0), (3, 3, 2, 2)),
    ((4, 4, 4, 4), (5, 5, 5, 5)),
)
STRIDE = CAP + 1
COUNTS = FAN * STRIDE
CHUNKS = 8
PIECES = 4
PIECE = ROWS // PIECES
PER = ROWS // CHUNKS
VMEM_LIMIT = 24 * 1024 * 1024

VM = pl.BlockSpec(memory_space=pltpu.VMEM)
SM = pl.BlockSpec(memory_space=pltpu.SMEM)
ANY = pl.BlockSpec(memory_space=pl.ANY)
HBM = pl.BlockSpec(memory_space=pltpu.HBM)


def face_of(p, core, own):
    kind = lax.rem(own, 4)
    picks = []
    for faces in FACES[ORDER[p]]:
        pick = faces[3]
        for k in (2, 1, 0):
            pick = jnp.where(kind == k, faces[k], pick)
        picks.append(pick)
    return jnp.where(core == 0, *picks)


def solve(field, block):
    return lax.dot_general(field.astype(jnp.bfloat16), block, (((1,), (1,)), ((), ())), preferred_element_type=jnp.float32)


def remote_terms(core, own, table, x_of, block_of, mine, theirs, local=None):
    for p in range(len(FACES)):
        for other, out in ((True, theirs[p]), (False, mine[p])):
            face = face_of(p, 1 - core if other else core, own)
            count = table[0, COUNTS + face]
            for s in range(CAP // 2):
                terms = []
                for slot in (s, s + CAP // 2):
                    at = jnp.minimum(slot, count - 1)
                    entry = table[0, face * STRIDE + at]
                    terms.append(jnp.dot(x_of(entry), block_of(face, at, entry), preferred_element_type=jnp.float32))
                    out[slot * ADJ : (slot + 1) * ADJ] = terms[-1][:, 0:128].astype(out.dtype)
                    if local is not None and not other:
                        label = jnp.where(slot < count, local[face, entry] + 1, 0)
                        out[BODY + slot : BODY + slot + 1] = jnp.full((1, 128), label, jnp.int32).astype(jnp.float32)
                both = jnp.concatenate([terms[0][:, 128:WIDTH], terms[1][:, 128:WIDTH]], axis=1)
                out[WIDE + s * ADJ : WIDE + (s + 1) * ADJ] = both.astype(out.dtype)
            if local is not None and other:
                out[BODY:] = jnp.zeros((CAP, 128), out.dtype)


def first_kernel(off, precond, rhs, owner, local, x_half, xb, pre_v, table, m0, m1, m2, t0, t1, t2,
                 blocks, rhs_v, owner_s, local_s, sems, pre_sem, small_sems):
    core, own = lax.axis_index("blk"), lax.axis_index("rows")
    copies = [pltpu.make_async_copy(a, b, small_sems.at[k]) for k, (a, b) in enumerate(((owner, owner_s), (local, local_s), (rhs, rhs_v)))]
    for copy in copies:
        copy.start()
    pre_copy = pltpu.make_async_copy(precond, pre_v, pre_sem)
    pre_copy.start()
    copies[0].wait()

    def fetch(face, slot, entry):
        return pltpu.make_async_copy(off.at[entry, face], blocks.at[face * CAP + slot], sems.at[face * CAP + slot])

    def list_row(i, ranks):
        after = []
        for k in range(FAN):
            remote = owner_s[k, i] != own
            rank = ranks[k]
            table[0, k * STRIDE + rank] = i

            @pl.when(remote)
            def _():
                fetch(k, rank, i).start()

            after.append(rank + remote.astype(jnp.int32))
        return tuple(after)

    counts = lax.fori_loop(0, ROWS, list_row, (jnp.int32(0),) * FAN)
    for k in range(FAN):
        table[0, COUNTS + k] = counts[k]
    copies[1].wait()
    copies[2].wait()
    pre_copy.wait()

    def row(n, _):
        x = solve(rhs_v[n], pre_v[n])
        x_half[n] = x
        xb[n] = x.astype(jnp.bfloat16)
        return 0

    lax.fori_loop(0, ROWS, row, 0, unroll=4)

    for k in range(FAN):
        def arrive(slot, _):
            fetch(k, slot, 0).wait()
            return 0

        lax.fori_loop(0, counts[k], arrive, 0)
    remote_terms(core, own, table, lambda e: xb[e], lambda face, at, e: blocks[face * CAP + at], (m0, m1, m2), (t0, t1, t2), local_s)


def local_terms(first, last, own, xb, off_v, diag_v, owner, local, sums):
    def row(i, _):
        x = xb[i]
        places, terms = [i], [jnp.dot(x, diag_v[i], preferred_element_type=jnp.float32)]
        for k in range(FAN):
            places.append(jnp.where(owner[k, i] == own, local[k, i], ROWS))
            terms.append(jnp.dot(x, off_v[i, k], preferred_element_type=jnp.float32))
        for place, term in zip(places, terms):
            sums[place] = sums[place] + term
        return 0

    lax.fori_loop(first, last, row, 0, unroll=True if last - first <= 4 else 4)


def first_local_kernel(off, diag, xb, owner, local, off_v, diag_v, *rest):
    partial, (sums, owner_s, local_s, sems, small_sems) = rest[:PIECES], rest[PIECES:]
    own = lax.axis_index("rows")
    small = [pltpu.make_async_copy(a, b, small_sems.at[k]) for k, (a, b) in enumerate(((owner, owner_s), (local, local_s)))]
    for copy in small:
        copy.start()
    copies = []
    for chunk in range(CHUNKS):
        part = pl.ds(chunk * PER, PER)
        copies.append([pltpu.make_async_copy(a.at[part], b.at[part], sems.at[k, chunk]) for k, (a, b) in enumerate(((off, off_v), (diag, diag_v)))])
        for copy in copies[-1]:
            copy.start()
    sums[...] = jnp.zeros(sums.shape, sums.dtype)
    for copy in small:
        copy.wait()
    for chunk in range(CHUNKS):
        for copy in copies[chunk]:
            copy.wait()
        local_terms(chunk * PER, (chunk + 1) * PER, own, xb, off_v, diag_v, owner_s, local_s, sums)
    for piece in range(PIECES):
        partial[piece][...] = sums[piece * PIECE : (piece + 1) * PIECE]


def place(messages, label_of, first, narrow_sum, wide_sum):
    wide_sum[...] = jnp.zeros(wide_sum.shape, wide_sum.dtype)
    narrow_sum[...] = jnp.zeros(narrow_sum.shape, narrow_sum.dtype)
    lane = lax.broadcasted_iota(jnp.int32, (ADJ, 128), 1)
    for p, message in enumerate(messages):
        for s in range(CAP // 2):
            at = []
            for slot in (s, s + CAP // 2):
                label = label_of(first + p * CAP + slot)
                at.append(jnp.where(label == 0, ROWS, label - 1))
                wide_sum[at[-1]] += message[slot * ADJ : (slot + 1) * ADJ].astype(jnp.float32)
            both = message[WIDE + s * ADJ : WIDE + (s + 1) * ADJ].astype(jnp.float32)
            narrow_sum[at[0]] += jnp.where(lane < 64, both, 0.0)
            narrow_sum[at[1]] += jnp.where(lane < 64, 0.0, both)


def read_labels(messages, row_v, labels_s, sem):
    found = jnp.concatenate([m[BODY:].astype(jnp.float32) for m in messages], axis=0)
    rows = lax.broadcasted_iota(jnp.int32, found.shape, 0)
    lanes = lax.broadcasted_iota(jnp.int32, found.shape, 1)
    row = jnp.sum(jnp.where(rows == lanes, found, 0.0), axis=0, keepdims=True)
    row_v[...] = row.astype(jnp.int32)
    copy = pltpu.make_async_copy(row_v, labels_s, sem)
    copy.start()
    return copy


def residual_of(n, rhs, ours, other, piece, wides, narrows):
    narrow = narrows[0][n] + narrows[1][n]
    narrow = narrow + pltpu.roll(narrow, 64, 1)
    got = jnp.concatenate([wides[0][n] + wides[1][n], narrow[:, 0:64]], axis=1)
    return rhs[n] - ((ours[n - piece * PIECE] + other[n - piece * PIECE]) + got)


def middle_kernel(off_v, pre_v, rhs, table, x_before, *rest):
    ours, others, rest = rest[:PIECES], rest[PIECES : 2 * PIECES], rest[2 * PIECES :]
    middle_body(off_v, pre_v, rhs, table, x_before, ours, others, *rest)


def middle_body(off_v, pre_v, rhs, table, x_before, ours, other, g0, g1, g2, f0, f1, f2,
                  vb, xb, labels_out, m0, m1, m2, t0, t1, t2,
                  wide_a, wide_b, narrow_a, narrow_b, row_v, label_sem):
    core, own = lax.axis_index("blk"), lax.axis_index("rows")
    read_labels((g0, g1, g2, f0, f1, f2), row_v, labels_out, label_sem).wait()
    label_of = lambda at: labels_out[0, at]
    place((g0, g1, g2), label_of, 0, narrow_a, wide_a)
    place((f0, f1, f2), label_of, 3 * CAP, narrow_b, wide_b)

    for piece in range(PIECES):
        def row(n, _):
            left = residual_of(n, rhs, ours[piece], other[piece], piece, (wide_a, wide_b), (narrow_a, narrow_b)).astype(jnp.bfloat16)
            vb[n] = left
            xb[n] = (x_before[n] + solve(left, pre_v[n])).astype(jnp.bfloat16)
            return 0

        lax.fori_loop(piece * PIECE, (piece + 1) * PIECE, row, 0, unroll=4)
    remote_terms(core, own, table, lambda e: xb[e], lambda face, at, e: off_v[e, face], (m0, m1, m2), (t0, t1, t2))


def middle_local_kernel(off_v, diag_v, xb, owner, local, *rest):
    partial, sums = rest[:PIECES], rest[PIECES]
    own = lax.axis_index("rows")
    sums[...] = jnp.zeros(sums.shape, sums.dtype)
    local_terms(0, ROWS, own, xb, off_v, diag_v, owner, local, sums)
    for piece in range(PIECES):
        partial[piece][...] = sums[piece * PIECE : (piece + 1) * PIECE]


def last_kernel(pre_v, pre_other, rhs, vb, *rest):
    ours, others, rest = rest[:PIECES], rest[PIECES : 2 * PIECES], rest[2 * PIECES :]
    last_body(pre_v, pre_other, rhs, vb, ours, others, *rest)


def last_body(pre_v, pre_other, rhs, vb, ours, other, labels, g0, g1, g2, f0, f1, f2,
              adjoint, residual, wide_a, wide_b, narrow_a, narrow_b):
    core = lax.axis_index("blk")
    label_of = lambda at: labels[0, at]
    place((g0, g1, g2), label_of, 0, narrow_a, wide_a)
    place((f0, f1, f2), label_of, 3 * CAP, narrow_b, wide_b)

    for piece in range(PIECES):
        def row(n, _):
            left = residual_of(n, rhs, ours[piece], other[piece], piece, (wide_a, wide_b), (narrow_a, narrow_b))
            residual[n] = left
            fields = jnp.concatenate([rhs[n].astype(jnp.bfloat16), vb[n], left.astype(jnp.bfloat16)], axis=0)
            halves = [solve(fields, pre[n]) for pre in (pre_v, pre_other)]
            mine, theirs = [(half[0:ADJ] + half[ADJ : 2 * ADJ]) + half[2 * ADJ :] for half in halves]
            adjoint[n, :, 0:HALF] = jnp.where(core == 0, mine, theirs)
            adjoint[n, :, HALF:WIDTH] = jnp.where(core == 0, theirs, mine)
            return 0

        lax.fori_loop(piece * PIECE, (piece + 1) * PIECE, row, 0, unroll=4)


def call(kernel, name, out_shape, in_specs, out_specs, scratch_shapes, cost=None):
    params = pltpu.CompilerParams(vmem_limit_bytes=VMEM_LIMIT)
    return pl.pallas_call(kernel, out_shape=out_shape, in_specs=in_specs, out_specs=out_specs, scratch_shapes=scratch_shapes,
                          compiler_params=params, cost_estimate=cost, name=name)


def on_device(off_blocks, diag_blocks, precond, adj_rhs, col_owner, col_local):
    nrows = lax.axis_size("rows")
    offsets = (1, nrows - 1, 2, nrows - 2, nrows // 2, nrows // 2 + 1)
    shape, f32, bf16, i32 = jax.ShapeDtypeStruct, jnp.float32, jnp.bfloat16, jnp.int32
    field, half_blocks = shape((ROWS, ADJ, WIDTH), f32), shape((ROWS, HALF, WIDTH), bf16)
    pieces = [shape((PIECE, ADJ, WIDTH), f32)] * PIECES
    row_of_ints = shape((1, 128), i32)
    dma = pltpu.SemaphoreType.DMA

    def across(x):
        return lax.ppermute(x, "blk", [(0, 1), (1, 0)])

    def to_faces(x, p):
        pairs = [(2 * i + c, 2 * ((i + offsets[FACES[ORDER[p]][c][i % 4]]) % nrows) + c) for i in range(nrows) for c in range(2)]
        return lax.ppermute(x, ("rows", "blk"), pairs)

    def exchange(mine, theirs, *later):
        sums = [(m + across(t).astype(f32)).astype(bf16) for m, t in zip(mine, theirs)]
        got = [to_faces(x, p) for p, x in enumerate(sums)]
        later = lax.optimization_barrier((*sums, *later))[len(sums) :]
        return got, *later

    def tie(x, *others):
        return lax.optimization_barrier((x, *others))

    def hand_on(got, parts):
        got[0], *parts = tie(got[0], *parts)
        got[1] = tie(got[1], parts[0])[0]
        got[2] = tie(got[2], parts[0])[0]
        return parts, [across(x) for x in parts], got, [across(g) for g in got]

    def in_hbm(*arrays):
        return [pltpu.with_memory_space_constraint(x, pltpu.HBM) for x in arrays]

    cost = pl.CostEstimate(flops=2 * ROWS * (FAN + 1) * ADJ * HALF * WIDTH, bytes_accessed=40_000_000, transcendentals=0)
    ints = [pltpu.SMEM((FAN, ROWS), i32)] * 2
    received = [pltpu.VMEM((ROWS + 1, ADJ, 128), f32)] * 4
    sums = pltpu.VMEM((ROWS + 1, ADJ, WIDTH), f32)
    owner, local = col_owner.T, col_local.T

    x_half, xb, pre_v, table, *messages = call(
        first_kernel,
        "first_remote_terms",
        [shape((ROWS, ADJ, HALF), f32), shape((ROWS, ADJ, HALF), bf16), half_blocks, row_of_ints]
        + [shape((BODY + CAP, 128), f32)] * 3 + [shape((BODY + CAP, 128), bf16)] * 3,
        [HBM] * 5,
        [VM, VM, VM, SM] + [VM] * 6,
        [pltpu.VMEM((FAN * CAP, HALF, WIDTH), bf16), pltpu.VMEM((ROWS, ADJ, WIDTH), f32)] + ints + [dma((FAN * CAP,)), dma, dma((3,))],
    )(*in_hbm(off_blocks, precond, adj_rhs, owner, local))
    got, xb, pre_v = exchange(messages[:3], messages[3:], xb, pre_v)
    off_v, diag_v, *partial = call(
        first_local_kernel,
        "first_local_terms",
        [shape((ROWS, FAN, HALF, WIDTH), bf16), half_blocks] + pieces,
        [HBM, HBM, VM, HBM, HBM],
        [VM] * (2 + PIECES),
        [sums] + ints + [dma((2, CHUNKS)), dma((2,))],
        cost,
    )(*in_hbm(off_blocks, diag_blocks), xb, *in_hbm(owner, local))
    partial, other, got, forwarded = hand_on(got, partial)
    pre_other, got[1] = tie(across(pre_v), got[1])

    vb, xb, labels, *messages = call(
        middle_kernel,
        "middle_remote_terms",
        [shape((ROWS, ADJ, WIDTH), bf16), shape((ROWS, ADJ, HALF), bf16), row_of_ints]
        + [shape((BODY, 128), f32)] * 3 + [shape((BODY, 128), bf16)] * 3,
        [VM, VM, VM, SM, VM] + [VM] * (2 * PIECES + 6),
        [VM, VM, SM] + [VM] * 6,
        received + [pltpu.VMEM((1, 128), i32), dma],
    )(off_v, pre_v, adj_rhs, table, x_half, *partial, *other, *got, *forwarded)
    got, xb = exchange(messages[:3], messages[3:], xb)
    partial = call(
        middle_local_kernel,
        "middle_local_terms",
        pieces,
        [VM, VM, VM, SM, SM],
        [VM] * PIECES,
        [sums],
        cost,
    )(off_v, diag_v, xb, owner, local)
    partial, other, got, forwarded = hand_on(got, partial)

    return call(
        last_kernel,
        "last_terms",
        [field, field],
        [VM] * (4 + 2 * PIECES) + [SM] + [VM] * 6,
        [VM] * 2,
        received,
    )(pre_v, pre_other, adj_rhs, vb, *partial, *other, labels, *got, *forwarded)


def solution(mesh):
    in_specs = (
        P("rows", None, "blk", None),
        P("rows", "blk", None),
        P("rows", "blk", None),
        P("rows", None, None),
        P("rows", None),
        P("rows", None),
    )
    out_specs = (P("rows", None, None), P("rows", None, None))

    def program(*arrays):
        return tuple(on_device(*arrays))

    return jax.shard_map(program, mesh=mesh, in_specs=in_specs, out_specs=out_specs, check_vma=False)
```

time: 228 us -> 54.1 us (0.24)
  local copies, waits for them, and re-layouts: 45.9 us -> 0.02 us
  waiting for transfers between devices: 52.1 us -> 6.54 us
  matrix products: 29.6 us -> 0 us
  starting transfers between devices: 46.6 us -> 23.9 us
  Pallas kernels: 0 us -> 22.6 us
  blocking collectives: 22.3 us -> 0 us
  other arithmetic: 15.3 us -> 0.17 us
  between operations: 14.8 us -> 0.78 us
    psum x2 -> x0, waiting for transfers between devices: 34.9 us -> none  [on_device(): diag_sum, off_sum = lax.psum((diag_part, off_part), 'blk')]
    dot_general x21 -> x0, matrix products: 29.6 us -> none  [the longest x2 9.28 us: on_device(): jnp.einsum('nkrc,nar->nkac', off_blocks, xh, preferred_element_type=jnp.f...]
    ppermute x18 -> x27, starting transfers between devices: 46.5 us -> 23.9 us  [the longest x6 17 us: to_faces(): return lax.ppermute(x, ('rows', 'blk'), pairs)]
    pallas_call x0 -> x5, Pallas kernels: none -> 22.6 us  [the longest x1 5.8 us: on_device(): call(first_kernel, 'first_remote_terms', [shape((ROWS, ADJ, HALF), f32),...]
    all_gather x3 -> x0, blocking collectives: 22.3 us -> none  [precondition(): return lax.all_gather(mine, 'blk', axis=2, tiled=True)]
    gather x12 -> x0, local copies, waits for them, and re-layouts: 20 us -> none  [on_device(): picked = off_faces[entry[:, face], face]]
    ppermute x18 -> x27, waiting for transfers between devices: 17.2 us -> 6.54 us  [the longest x21 4.15 us: across(): return lax.ppermute(x, 'blk', [(0, 1), (1, 0)])]
    convert_element_type x13 -> x6, other arithmetic: 9.33 us -> 0.17 us  [exchange(): (m + across(t).astype(f32)).astype(bf16)]
  transfers between devices with their start and end apart: 20 -> 27, of which waited for: 6 -> 12; matrix products, arithmetic and copies ran while one was open for 5% -> 0% of each run, Pallas kernels for 0% -> 14%
where the time goes in v2:
time: 54.1 us; the launch traced here: 54 us
  starting transfers between devices  23.9 us (44%)
  Pallas kernels  22.6 us (42%)
  waiting for transfers between devices  6.54 us (12%)
  between operations  0.78 us (1%)
    ppermute x6, starting transfers between devices, to_faces(): return lax.ppermute(x, ('rows', 'blk'), pairs)  17 us
    ppermute x21, starting transfers between devices, across(): return lax.ppermute(x, 'blk', [(0, 1), (1, 0)])  6.84 us
    pallas_call x1, Pallas kernels, on_device(): call(first_kernel, 'first_remote_terms', [shape((ROWS, ADJ, HALF), f32),...  5.8 us
    pallas_call x1, Pallas kernels, on_device(): call(first_local_kernel, 'first_local_terms', [shape((ROWS, FAN, HALF, WI...  4.61 us
    pallas_call x1, Pallas kernels, on_device(): call(middle_kernel, 'middle_remote_terms', [shape((ROWS, ADJ, WIDTH), bf1...  4.55 us
    pallas_call x1, Pallas kernels, on_device(): call(last_kernel, 'last_terms', [field, field], [VM] * (4 + 2 * PIECES) +...  4.42 us
    ppermute x21, waiting for transfers between devices, across(): return lax.ppermute(x, 'blk', [(0, 1), (1, 0)])  4.15 us
    pallas_call x1, Pallas kernels, on_device(): call(middle_local_kernel, 'middle_local_terms', pieces, [VM, VM, VM, SM,...  3.19 us
  transfers between devices with their start and end apart: 27, of which 12 were waited for; matrix products, arithmetic and copies ran while one was open for 0% of the time, Pallas kernels for 14%

profile of v2, /device:TPU:1, one launch (start us, length us, event | category | flops | bytes accessed | tf_op | source)
XLA Modules:
  0.0 54.0 jit_solution(5839714487638540400)
XLA Ops:
  0.6 5.8 %first_remote_terms.1 = (f32[32,16,96]{2,1,0:T(8,128)S(1)}, bf16[32,16,96]{2,1,0:T(8,128)(2,1)S(1)}, bf16[32,96,192]{2,1,0:T(8,128)(2,1)S(1)}, s32[1,128]{1,0:T(...) custom-call(bf16[32,6,96,192]{3,2,1,0:T(8,128)(2,1)} %off.3, ...), custom_call_target="tpu_custom_call" | custom-call | tf_op jit(solution)/shard_map/first_remote_terms/pallas_call | solution.py:301
  6.4 1.5 %collective-permute-start = (bf16[400,128]{1,0:T(8,128)(2,1)S(1)}, bf16[400,128]{1,0:T(8,128)(2,1)S(1)}, u32[]{:S(2)}, u32[]{:S(2)}) collective-permute-start(bf16[400,128]{1,0:T(8,128)(2,1)S(1)} %get-tuple-element.51), channel_id=1, source_target_pairs={{0,1},{1,0},{2,3},{3,2},{4,5},{5,4},{6,7},{7,6},{8,9},{9,8},{10,11... | collective-permute-start | bytes 307208 | tf_op jit(solution)/shard_map/ppermute | solution.py:271
  8.0 0.4 collective-permute-start.2
  8.5 0.4 collective-permute-done
  8.9 0.3 collective-permute-done.1
  9.4 0.4 collective-permute-start.3
  9.9 3.8 %collective-permute-start.5 = (bf16[400,128]{1,0:T(8,128)(2,1)S(1)}, bf16[400,128]{1,0:T(8,128)(2,1)S(1)}, u32[]{:S(2)}, u32[]{:S(2)}) collective-permute-start(bf16[400,128]{1,0:T(8,128)(2,1)S(1)} %add_convert_fusion.2), channel_id=1, source_target_pairs={{0,64},{1,67},{2,66},{3,69},{4,68},{5,71},{6,70},{7,73},{8,72},{9,... | collective-permute-start | bytes 307208 | tf_op jit(solution)/shard_map/ppermute | solution.py:275
  13.7 6.6 %collective-permute-start.4 = (bf16[400,128]{1,0:T(8,128)(2,1)S(1)}, bf16[400,128]{1,0:T(8,128)(2,1)S(1)}, u32[]{:S(2)}, u32[]{:S(2)}) collective-permute-start(bf16[400,128]{1,0:T(8,128)(2,1)S(1)} %add_convert_fusion.1), channel_id=1, source_target_pairs={{0,126},{1,125},{2,4},{3,127},{4,2},{5,9},{6,8},{7,11},{8,6},{9,5}... | collective-permute-start | bytes 307208 | tf_op jit(solution)/shard_map/ppermute | solution.py:275
  20.3 4.6 %first_local_terms.1 = (bf16[32,6,96,192]{3,2,1,0:T(8,128)(2,1)S(1)}, bf16[32,96,192]{2,1,0:T(8,128)(2,1)S(1)}, f32[8,16,192]{2,1,0:T(8,128)S(1)}, f32[8,16,192]...) custom-call(bf16[32,6,96,192]{3,2,1,0:T(8,128)(2,1)} %off.3, bf16[32,96,192]{2,1,0:T(8,128)(2,1)} %diag.1, ...), custom_call_target="tpu_custom_call" | custom-call | flops 132120576 | bytes 40000000 | tf_op jit(solution)/shard_map/first_local_terms/pallas_call | solution.py:311
  25.0 0.5 collective-permute-start.8
  25.6 0.4 collective-permute-start.13
  26.1 0.3 collective-permute-done.7.rest_5_
  26.6 0.3 collective-permute-start.9
  27.1 0.8 %collective-permute-done.9.rest_7_ = f32[8,16,192]{2,1,0:T(8,128)S(1)} collective-permute-done((f32[8,16,192]{2,1,0:T(8,128)S(1)}, f32[8,16,192]{2,1,0:T(8,128)S(1)}, u32[]{:S(2)}, u32[]{:S(2)}) %collective-permute-start.9) | collective-permute-done | bytes 98336 | tf_op jit(solution)/shard_map/ppermute | solution.py:271
  27.9 0.3 collective-permute-done.6.rest_4_
  28.3 4.6 %middle_remote_terms.1 = (bf16[32,16,192]{2,1,0:T(8,128)(2,1)S(1)}, bf16[32,16,96]{2,1,0:T(8,128)(2,1)S(1)}, s32[1,128]{1,0:T(1,128)S(1)}, f32[384,128]{1,0:T(8,...) custom-call(bf16[32,6,96,192]{3,2,1,0:T(8,128)(2,1)S(1)} %get-tuple-, ...), custom_call_target="tpu_custom_call" | custom-call | tf_op jit(solution)/shard_map/middle_remote_terms/pallas_call | solution.py:323
  32.9 0.3 collective-permute-start.14
  33.1 0.3 collective-permute-start.16
  33.6 0.6 %collective-permute-done.14 = bf16[384,128]{1,0:T(8,128)(2,1)S(1)} collective-permute-done((bf16[384,128]{1,0:T(8,128)(2,1)S(1)}, bf16[384,128]{1,0:T(8,128)(2,1)S(1)}, u32[]{:S(2)}, u32[]{:S(2)}) %collective-permute-start.14) | collective-permute-done | bytes 98336 | tf_op jit(solution)/shard_map/ppermute | solution.py:271
  34.3 2.2 %collective-permute-start.15 = (bf16[384,128]{1,0:T(8,128)(2,1)S(1)}, bf16[384,128]{1,0:T(8,128)(2,1)S(1)}, u32[]{:S(2)}, u32[]{:S(2)}) collective-permute-start(bf16[384,128]{1,0:T(8,128)(2,1)S(1)} %add_convert_fusion.5), channel_id=1, source_target_pairs={{0,64},{1,67},{2,66},{3,69},{4,68},{5,71},{6,70},{7,73},{8,72},{9,... | collective-permute-start | bytes 294920 | tf_op jit(solution)/shard_map/ppermute | solution.py:275
  36.5 4.3 %collective-permute-start.22 = (bf16[384,128]{1,0:T(8,128)(2,1)S(1)}, bf16[384,128]{1,0:T(8,128)(2,1)S(1)}, u32[]{:S(2)}, u32[]{:S(2)}) collective-permute-start(bf16[384,128]{1,0:T(8,128)(2,1)S(1)} %add_convert_fusion.4), channel_id=1, source_target_pairs={{0,126},{1,125},{2,4},{3,127},{4,2},{5,9},{6,8},{7,11},{8,6},{9,5}... | collective-permute-start | bytes 294920 | tf_op jit(solution)/shard_map/ppermute | solution.py:275
  41.0 3.2 %middle_local_terms.1 = (f32[8,16,192]{2,1,0:T(8,128)S(1)}, f32[8,16,192]{2,1,0:T(8,128)S(1)}, f32[8,16,192]{2,1,0:T(8,128)S(1)}, f32[8,16,192]{2,1,0:T(8,128)S(1)}) custom-call(bf16[32,6,96,192]{3,2,1,0:T(8,128)(2,1)S(1)} %get-tuple-element.67.off_v, bf16[32,96,192]{2,1,0:T(8,128)(2,1)S(1)} %get-tuple-element.79.diag_v, ...), custom_call_target="tpu_custom_call" | custom-call | flops 132120576 | bytes 40000000 | tf_op jit(solution)/shard_map/middle_local_terms/pallas_call | solution.py:333
  44.2 2.4 %collective-permute-done.22.rest_10_ = bf16[384,128]{1,0:T(8,128)(2,1)S(1)} collective-permute-done((bf16[384,128]{1,0:T(8,128)(2,1)S(1)}, bf16[384,128]{1,0:T(8,128)(2,1)S(1)}, u32[]{:S(2)}, u32[]{:S(2)}) %collective-permute-start.22) | collective-permute-done | bytes 98336 | tf_op jit(solution)/shard_map/ppermute | solution.py:275
  46.5 0.3 collective-permute-start.25
  47.0 0.3 collective-permute-start.26
  47.6 0.3 collective-permute-start.20
  47.9 0.3 collective-permute-start.21
  48.2 0.2 collective-permute-start.18
  48.4 0.3 collective-permute-done.19.rest_5_
  48.9 0.3 collective-permute-done.21.rest_7_
  49.3 0.3 collective-permute-done.18.rest_4_
  49.5 4.4 %last_terms.1 = (f32[32,16,192]{2,1,0:T(8,128)}, f32[32,16,192]{2,1,0:T(8,128)}) custom-call(bf16[32,96,192]{2,1,0:T(8,128)(2,1)S(1)} %get-tuple-element.58.pre_v, bf16[32,96,192]{2,1,0:T(8,128)(2,1)S(1)} %collective-permute-done.3.pre_other, f32[32,16,192]{2,1,0:T(8,128)S(1)} %copy-done, bf16[32,16,192]{2,1,0:T(8,128)(2,1)S(1)} %get-tuple-element.76.vb, ...), custom_call_target="tpu_custom_call" | custom-call | tf_op jit(solution)/shard_map/last_terms/pallas_call | solution.py:344
  (39 shorter events, 1.8 us)
Async XLA Ops:
  6.4 2.5 %collective-permute-start = (bf16[400,128]{1,0:T(8,128)(2,1)S(1)}, bf16[400,128]{1,0:T(8,128)(2,1)S(1)}, u32[]{:S(2)}, u32[]{:S(2)}) collective-permute-start(bf16[400,128]{1,0:T(8,128)(2,1)S(1)} %get-tuple-element.51), channel_id=1, source_target_pairs={{0,1},{1,0},{2,3},{3,2},{4,5},{5,4},{6,7},{7,6},{8,9},{9,8},{10,11... | collective-permute-start | bytes 307208 | tf_op jit(solution)/shard_map/ppermute | solution.py:271
  7.9 1.3 %collective-permute-start.1 = (bf16[400,128]{1,0:T(8,128)(2,1)S(1)}, bf16[400,128]{1,0:T(8,128)(2,1)S(1)}, u32[]{:S(2)}, u32[]{:S(2)}) collective-permute-start(bf16[400,128]{1,0:T(8,128)(2,1)S(1)} %get-tuple-element.53), channel_id=1, source_target_pairs={{0,1},{1,0},{2,3},{3,2},{4,5},{5,4},{6,7},{7,6},{8,9},{9,8},{10,11... | collective-permute-start | bytes 307208 | tf_op jit(solution)/shard_map/ppermute | solution.py:271
  8.0 1.4 %collective-permute-start.2 = (bf16[400,128]{1,0:T(8,128)(2,1)S(1)}, bf16[400,128]{1,0:T(8,128)(2,1)S(1)}, u32[]{:S(2)}, u32[]{:S(2)}) collective-permute-start(bf16[400,128]{1,0:T(8,128)(2,1)S(1)} %get-tuple-element.55), channel_id=1, source_target_pairs={{0,1},{1,0},{2,3},{3,2},{4,5},{5,4},{6,7},{7,6},{8,9},{9,8},{10,11... | collective-permute-start | bytes 307208 | tf_op jit(solution)/shard_map/ppermute | solution.py:271
  9.4 18.8 %copy-start = (f32[32,16,192]{2,1,0:T(8,128)S(1)}, f32[32,16,192]{2,1,0:T(8,128)}, u32[]{:S(2)}) copy-start(f32[32,16,192]{2,1,0:T(8,128)} %rhs.5) | copy-start | bytes 1179652
  9.4 17.5 %collective-permute-start.3 = (bf16[32,96,192]{2,1,0:T(8,128)(2,1)S(1)}, bf16[32,96,192]{2,1,0:T(8,128)(2,1)S(1)}, u32[]{:S(2)}, u32[]{:S(2)}) collective-permute-start(bf16[32,96,192]{2,1,0:T(8,128)(2,1)S(1)} %get-tuple-element.58.pre_v), channel_id=1, source_target_pairs={{0,1},{1,0},{2,3},{3,2},{4,5},{5,4},{6,7},{7,6},{8,9},{9,8},{10,11... | collective-permute-start | bytes 3538952 | tf_op jit(solution)/shard_map/ppermute | solution.py:271
  9.9 15.1 %collective-permute-start.5 = (bf16[400,128]{1,0:T(8,128)(2,1)S(1)}, bf16[400,128]{1,0:T(8,128)(2,1)S(1)}, u32[]{:S(2)}, u32[]{:S(2)}) collective-permute-start(bf16[400,128]{1,0:T(8,128)(2,1)S(1)} %add_convert_fusion.2), channel_id=1, source_target_pairs={{0,64},{1,67},{2,66},{3,69},{4,68},{5,71},{6,70},{7,73},{8,72},{9,... | collective-permute-start | bytes 307208 | tf_op jit(solution)/shard_map/ppermute | solution.py:275
  13.7 11.8 %collective-permute-start.4 = (bf16[400,128]{1,0:T(8,128)(2,1)S(1)}, bf16[400,128]{1,0:T(8,128)(2,1)S(1)}, u32[]{:S(2)}, u32[]{:S(2)}) collective-permute-start(bf16[400,128]{1,0:T(8,128)(2,1)S(1)} %add_convert_fusion.1), channel_id=1, source_target_pairs={{0,126},{1,125},{2,4},{3,127},{4,2},{5,9},{6,8},{7,11},{8,6},{9,5}... | collective-permute-start | bytes 307208 | tf_op jit(solution)/shard_map/ppermute | solution.py:275
  20.3 5.2 %collective-permute-start.10 = (bf16[400,128]{1,0:T(8,128)(2,1)S(1)}, bf16[400,128]{1,0:T(8,128)(2,1)S(1)}, u32[]{:S(2)}, u32[]{:S(2)}) collective-permute-start(bf16[400,128]{1,0:T(8,128)(2,1)S(1)} %add_convert_fusion), channel_id=1, source_target_pairs={{0,2},{1,5},{2,0},{3,7},{4,6},{5,1},{6,4},{7,3},{8,10},{9,13},{10,... | collective-permute-start | bytes 307208 | tf_op jit(solution)/shard_map/ppermute | solution.py:275
  24.9 1.4 %collective-permute-start.7 = (f32[8,16,192]{2,1,0:T(8,128)S(1)}, f32[8,16,192]{2,1,0:T(8,128)S(1)}, u32[]{:S(2)}, u32[]{:S(2)}) collective-permute-start(f32[8,16,192]{2,1,0:T(8,128)S(1)} %get-tuple-element.70.rest_1_), channel_id=1, source_target_pairs={{0,1},{1,0},{2,3},{3,2},{4,5},{5,4},{6,7},{7,6},{8,9},{9,8},{10,11... | collective-permute-start | bytes 294920 | tf_op jit(solution)/shard_map/ppermute | solution.py:271
  25.0 1.5 %collective-permute-start.8 = (f32[8,16,192]{2,1,0:T(8,128)S(1)}, f32[8,16,192]{2,1,0:T(8,128)S(1)}, u32[]{:S(2)}, u32[]{:S(2)}) collective-permute-start(f32[8,16,192]{2,1,0:T(8,128)S(1)} %get-tuple-element.71.rest_2_), channel_id=1, source_target_pairs={{0,1},{1,0},{2,3},{3,2},{4,5},{5,4},{6,7},{7,6},{8,9},{9,8},{10,11... | collective-permute-start | bytes 294920 | tf_op jit(solution)/shard_map/ppermute | solution.py:271
  25.5 2.7 %collective-permute-start.12 = (bf16[400,128]{1,0:T(8,128)(2,1)S(1)}, bf16[400,128]{1,0:T(8,128)(2,1)S(1)}, u32[]{:S(2)}, u32[]{:S(2)}) collective-permute-start(bf16[400,128]{1,0:T(8,128)(2,1)S(1)} %collective-permute-done.4.rest_9_), channel_id=1, source_target_pairs={{0,1},{1,0},{2,3},{3,2},{4,5},{5,4},{6,7},{7,6},{8,9},{9,8},{10,11... | collective-permute-start | bytes 307208 | tf_op jit(solution)/shard_map/ppermute | solution.py:271
  25.6 2.6 %collective-permute-start.13 = (bf16[400,128]{1,0:T(8,128)(2,1)S(1)}, bf16[400,128]{1,0:T(8,128)(2,1)S(1)}, u32[]{:S(2)}, u32[]{:S(2)}) collective-permute-start(bf16[400,128]{1,0:T(8,128)(2,1)S(1)} %collective-permute-done.10.rest_10_), channel_id=1, source_target_pairs={{0,1},{1,0},{2,3},{3,2},{4,5},{5,4},{6,7},{7,6},{8,9},{9,8},{10,11... | collective-permute-start | bytes 307208 | tf_op jit(solution)/shard_map/ppermute | solution.py:271
  26.4 1.9 %collective-permute-start.11 = (bf16[400,128]{1,0:T(8,128)(2,1)S(1)}, bf16[400,128]{1,0:T(8,128)(2,1)S(1)}, u32[]{:S(2)}, u32[]{:S(2)}) collective-permute-start(bf16[400,128]{1,0:T(8,128)(2,1)S(1)} %collective-permute-done.5.rest_8_), channel_id=1, source_target_pairs={{0,1},{1,0},{2,3},{3,2},{4,5},{5,4},{6,7},{7,6},{8,9},{9,8},{10,11... | collective-permute-start | bytes 307208 | tf_op jit(solution)/shard_map/ppermute | solution.py:271
  26.6 1.3 %collective-permute-start.9 = (f32[8,16,192]{2,1,0:T(8,128)S(1)}, f32[8,16,192]{2,1,0:T(8,128)S(1)}, u32[]{:S(2)}, u32[]{:S(2)}) collective-permute-start(f32[8,16,192]{2,1,0:T(8,128)S(1)} %get-tuple-element.72.rest_3_), channel_id=1, source_target_pairs={{0,1},{1,0},{2,3},{3,2},{4,5},{5,4},{6,7},{7,6},{8,9},{9,8},{10,11... | collective-permute-start | bytes 294920 | tf_op jit(solution)/shard_map/ppermute | solution.py:271
  26.9 1.3 %collective-permute-start.6 = (f32[8,16,192]{2,1,0:T(8,128)S(1)}, f32[8,16,192]{2,1,0:T(8,128)S(1)}, u32[]{:S(2)}, u32[]{:S(2)}) collective-permute-start(f32[8,16,192]{2,1,0:T(8,128)S(1)} %get-tuple-element.64.rest_0_), channel_id=1, source_target_pairs={{0,1},{1,0},{2,3},{3,2},{4,5},{5,4},{6,7},{7,6},{8,9},{9,8},{10,11... | collective-permute-start | bytes 294920 | tf_op jit(solution)/shard_map/ppermute | solution.py:271
  28.3 12.7 %copy-start.1 = (s32[32,6]{0,1:T(8,128)S(1)}, s32[32,6]{0,1:T(8,128)}, u32[]{:S(2)}) copy-start(s32[32,6]{0,1:T(8,128)} %param.10) | copy-start | bytes 2308
  28.3 12.7 %copy-start.2 = (s32[32,6]{0,1:T(8,128)S(1)}, s32[32,6]{0,1:T(8,128)}, u32[]{:S(2)}) copy-start(s32[32,6]{0,1:T(8,128)} %param.11) | copy-start | bytes 2308
  32.9 1.4 %collective-permute-start.14 = (bf16[384,128]{1,0:T(8,128)(2,1)S(1)}, bf16[384,128]{1,0:T(8,128)(2,1)S(1)}, u32[]{:S(2)}, u32[]{:S(2)}) collective-permute-start(bf16[384,128]{1,0:T(8,128)(2,1)S(1)} %get-tuple-element.78), channel_id=1, source_target_pairs={{0,1},{1,0},{2,3},{3,2},{4,5},{5,4},{6,7},{7,6},{8,9},{9,8},{10,11... | collective-permute-start | bytes 294920 | tf_op jit(solution)/shard_map/ppermute | solution.py:271
  33.1 3.4 %collective-permute-start.16 = (bf16[384,128]{1,0:T(8,128)(2,1)S(1)}, bf16[384,128]{1,0:T(8,128)(2,1)S(1)}, u32[]{:S(2)}, u32[]{:S(2)}) collective-permute-start(bf16[384,128]{1,0:T(8,128)(2,1)S(1)} %get-tuple-element.81), channel_id=1, source_target_pairs={{0,1},{1,0},{2,3},{3,2},{4,5},{5,4},{6,7},{7,6},{8,9},{9,8},{10,11... | collective-permute-start | bytes 294920 | tf_op jit(solution)/shard_map/ppermute | solution.py:271
  33.4 7.4 %collective-permute-start.17 = (bf16[384,128]{1,0:T(8,128)(2,1)S(1)}, bf16[384,128]{1,0:T(8,128)(2,1)S(1)}, u32[]{:S(2)}, u32[]{:S(2)}) collective-permute-start(bf16[384,128]{1,0:T(8,128)(2,1)S(1)} %get-tuple-element.83), channel_id=1, source_target_pairs={{0,1},{1,0},{2,3},{3,2},{4,5},{5,4},{6,7},{7,6},{8,9},{9,8},{10,11... | collective-permute-start | bytes 294920 | tf_op jit(solution)/shard_map/ppermute | solution.py:271
  34.3 9.9 %collective-permute-start.15 = (bf16[384,128]{1,0:T(8,128)(2,1)S(1)}, bf16[384,128]{1,0:T(8,128)(2,1)S(1)}, u32[]{:S(2)}, u32[]{:S(2)}) collective-permute-start(bf16[384,128]{1,0:T(8,128)(2,1)S(1)} %add_convert_fusion.5), channel_id=1, source_target_pairs={{0,64},{1,67},{2,66},{3,69},{4,68},{5,71},{6,70},{7,73},{8,72},{9,... | collective-permute-start | bytes 294920 | tf_op jit(solution)/shard_map/ppermute | solution.py:275
  36.5 10.0 %collective-permute-start.22 = (bf16[384,128]{1,0:T(8,128)(2,1)S(1)}, bf16[384,128]{1,0:T(8,128)(2,1)S(1)}, u32[]{:S(2)}, u32[]{:S(2)}) collective-permute-start(bf16[384,128]{1,0:T(8,128)(2,1)S(1)} %add_convert_fusion.4), channel_id=1, source_target_pairs={{0,126},{1,125},{2,4},{3,127},{4,2},{5,9},{6,8},{7,11},{8,6},{9,5}... | collective-permute-start | bytes 294920 | tf_op jit(solution)/shard_map/ppermute | solution.py:275
  40.8 6.2 %collective-permute-start.23 = (bf16[384,128]{1,0:T(8,128)(2,1)S(1)}, bf16[384,128]{1,0:T(8,128)(2,1)S(1)}, u32[]{:S(2)}, u32[]{:S(2)}) collective-permute-start(bf16[384,128]{1,0:T(8,128)(2,1)S(1)} %add_convert_fusion.3), channel_id=1, source_target_pairs={{0,2},{1,5},{2,0},{3,7},{4,6},{5,1},{6,4},{7,3},{8,10},{9,13},{10,... | collective-permute-start | bytes 294920 | tf_op jit(solution)/shard_map/ppermute | solution.py:275
  46.5 1.4 %collective-permute-start.25 = (bf16[384,128]{1,0:T(8,128)(2,1)S(1)}, bf16[384,128]{1,0:T(8,128)(2,1)S(1)}, u32[]{:S(2)}, u32[]{:S(2)}) collective-permute-start(bf16[384,128]{1,0:T(8,128)(2,1)S(1)} %collective-permute-done.22.rest_10_), channel_id=1, source_target_pairs={{0,1},{1,0},{2,3},{3,2},{4,5},{5,4},{6,7},{7,6},{8,9},{9,8},{10,11... | collective-permute-start | bytes 294920 | tf_op jit(solution)/shard_map/ppermute | solution.py:271
  46.9 1.3 %collective-permute-start.24 = (bf16[384,128]{1,0:T(8,128)(2,1)S(1)}, bf16[384,128]{1,0:T(8,128)(2,1)S(1)}, u32[]{:S(2)}, u32[]{:S(2)}) collective-permute-start(bf16[384,128]{1,0:T(8,128)(2,1)S(1)} %collective-permute-done.15.rest_9_), channel_id=1, source_target_pairs={{0,1},{1,0},{2,3},{3,2},{4,5},{5,4},{6,7},{7,6},{8,9},{9,8},{10,11... | collective-permute-start | bytes 294920 | tf_op jit(solution)/shard_map/ppermute | solution.py:271
  47.0 1.4 %collective-permute-start.26 = (bf16[384,128]{1,0:T(8,128)(2,1)S(1)}, bf16[384,128]{1,0:T(8,128)(2,1)S(1)}, u32[]{:S(2)}, u32[]{:S(2)}) collective-permute-start(bf16[384,128]{1,0:T(8,128)(2,1)S(1)} %collective-permute-done.23.rest_11_), channel_id=1, source_target_pairs={{0,1},{1,0},{2,3},{3,2},{4,5},{5,4},{6,7},{7,6},{8,9},{9,8},{10,11... | collective-permute-start | bytes 294920 | tf_op jit(solution)/shard_map/ppermute | solution.py:271
  47.4 1.3 %collective-permute-start.19 = (f32[8,16,192]{2,1,0:T(8,128)S(1)}, f32[8,16,192]{2,1,0:T(8,128)S(1)}, u32[]{:S(2)}, u32[]{:S(2)}) collective-permute-start(f32[8,16,192]{2,1,0:T(8,128)S(1)} %get-tuple-element.91.rest_1_), channel_id=1, source_target_pairs={{0,1},{1,0},{2,3},{3,2},{4,5},{5,4},{6,7},{7,6},{8,9},{9,8},{10,11... | collective-permute-start | bytes 294920 | tf_op jit(solution)/shard_map/ppermute | solution.py:271
  47.6 1.4 %collective-permute-start.20 = (f32[8,16,192]{2,1,0:T(8,128)S(1)}, f32[8,16,192]{2,1,0:T(8,128)S(1)}, u32[]{:S(2)}, u32[]{:S(2)}) collective-permute-start(f32[8,16,192]{2,1,0:T(8,128)S(1)} %get-tuple-element.92.rest_2_), channel_id=1, source_target_pairs={{0,1},{1,0},{2,3},{3,2},{4,5},{5,4},{6,7},{7,6},{8,9},{9,8},{10,11... | collective-permute-start | bytes 294920 | tf_op jit(solution)/shard_map/ppermute | solution.py:271
  47.9 1.3 %collective-permute-start.21 = (f32[8,16,192]{2,1,0:T(8,128)S(1)}, f32[8,16,192]{2,1,0:T(8,128)S(1)}, u32[]{:S(2)}, u32[]{:S(2)}) collective-permute-start(f32[8,16,192]{2,1,0:T(8,128)S(1)} %get-tuple-element.93.rest_3_), channel_id=1, source_target_pairs={{0,1},{1,0},{2,3},{3,2},{4,5},{5,4},{6,7},{7,6},{8,9},{9,8},{10,11... | collective-permute-start | bytes 294920 | tf_op jit(solution)/shard_map/ppermute | solution.py:271
  48.2 1.3 %collective-permute-start.18 = (f32[8,16,192]{2,1,0:T(8,128)S(1)}, f32[8,16,192]{2,1,0:T(8,128)S(1)}, u32[]{:S(2)}, u32[]{:S(2)}) collective-permute-start(f32[8,16,192]{2,1,0:T(8,128)S(1)} %get-tuple-element.90.rest_0_), channel_id=1, source_target_pairs={{0,1},{1,0},{2,3},{3,2},{4,5},{5,4},{6,7},{7,6},{8,9},{9,8},{10,11... | collective-permute-start | bytes 294920 | tf_op jit(solution)/shard_map/ppermute | solution.py:271

commit v3 on v2

v3 whole, which is shorter than its diff:
```python
import jax
import jax.numpy as jnp
from jax import lax
from jax.experimental import pallas as pl
from jax.experimental.pallas import tpu as pltpu
from jax.sharding import PartitionSpec as P

ROWS = 32
FAN = 6
ADJ = 16
WIDTH = 192
HALF = 96
CAP = 16
WIDE = CAP * ADJ
BODY = WIDE + WIDE // 2
NEAR, SEAM, FAR = 0, 1, 2
ORDER = (SEAM, FAR, NEAR)
FACES = (
    ((0, 1, 0, 1), (2, 2, 3, 3)),
    ((1, 0, 1, 0), (3, 3, 2, 2)),
    ((4, 4, 4, 4), (5, 5, 5, 5)),
)
STRIDE = CAP + 1
COUNTS = FAN * STRIDE
CHUNKS = 8
PIECES = 2
TIE = 1
PARTS = 4
UNROLL = 32
LOCAL_UNROLL = 16
PIECE = ROWS // PIECES
PER = ROWS // CHUNKS
VMEM_LIMIT = 24 * 1024 * 1024

VM = pl.BlockSpec(memory_space=pltpu.VMEM)
SM = pl.BlockSpec(memory_space=pltpu.SMEM)
ANY = pl.BlockSpec(memory_space=pl.ANY)
HBM = pl.BlockSpec(memory_space=pltpu.HBM)


def face_of(p, core, own):
    kind = lax.rem(own, 4)
    picks = []
    for faces in FACES[ORDER[p]]:
        pick = faces[3]
        for k in (2, 1, 0):
            pick = jnp.where(kind == k, faces[k], pick)
        picks.append(pick)
    return jnp.where(core == 0, *picks)


def solve(field, block):
    return lax.dot_general(field.astype(jnp.bfloat16), block, (((1,), (1,)), ((), ())), preferred_element_type=jnp.float32)


def faces_in_order(core, own):
    return [face_of(p, 1 - core if other else core, own) for p in range(len(FACES)) for other in (True, False)]


def remote_terms(core, own, table, x_of, block_of, mine, theirs, local=None):
    faces = faces_in_order(core, own)
    for p in range(len(FACES)):
        for other, out in ((True, theirs[p]), (False, mine[p])):
            face = faces[2 * p + (0 if other else 1)]
            count = table[0, COUNTS + face]
            for s in range(CAP // 2):
                terms = []
                for slot in (s, s + CAP // 2):
                    at = jnp.minimum(slot, count - 1)
                    entry = table[0, face * STRIDE + at]
                    terms.append(jnp.dot(x_of(entry), block_of(face, at, entry), preferred_element_type=jnp.float32))
                    out[slot * ADJ : (slot + 1) * ADJ] = terms[-1][:, 0:128].astype(out.dtype)
                    if local is not None and not other:
                        label = jnp.where(slot < count, local[face, entry] + 1, 0)
                        out[BODY + slot : BODY + slot + 1] = jnp.full((1, 128), label, jnp.int32).astype(jnp.float32)
                both = jnp.concatenate([terms[0][:, 128:WIDTH], terms[1][:, 128:WIDTH]], axis=1)
                out[WIDE + s * ADJ : WIDE + (s + 1) * ADJ] = both.astype(out.dtype)
            if local is not None and other:
                out[BODY:] = jnp.zeros((CAP, 128), out.dtype)


def list_face(face, own, owner, table):
    def entry(i, rank):
        table[0, face * STRIDE + rank] = i
        return rank + (owner[face, i] != own).astype(jnp.int32)

    table[0, COUNTS + face] = lax.fori_loop(0, ROWS, entry, jnp.int32(0), unroll=8)


def first_kernel(off, precond, rhs, owner, local, x_half, xb, pre_v, m0, m1, m2, t0, t1, t2,
                 blocks, rhs_v, owner_s, local_s, table, sems, pre_sem, small_sems):
    core, own = lax.axis_index("blk"), lax.axis_index("rows")
    copies = [pltpu.make_async_copy(a, b, small_sems.at[k]) for k, (a, b) in enumerate(((owner, owner_s), (local, local_s), (rhs, rhs_v)))]
    copies.append(pltpu.make_async_copy(precond, pre_v, pre_sem))
    for copy in copies:
        copy.start()
    copies[0].wait()

    def fetch(face, slot, entry):
        return pltpu.make_async_copy(off.at[entry, face], blocks.at[face * CAP + slot], sems.at[face * CAP + slot])

    def list_row(i, ranks):
        after = []
        for k in range(FAN):
            remote, rank = owner_s[k, i] != own, ranks[k]
            table[0, k * STRIDE + rank] = i

            @pl.when(remote)
            def _():
                fetch(k, rank, i).start()

            after.append(rank + remote.astype(jnp.int32))
        return tuple(after)

    counts = lax.fori_loop(0, ROWS, list_row, (jnp.int32(0),) * FAN, unroll=4)
    for k in range(FAN):
        table[0, COUNTS + k] = counts[k]
    for copy in copies[1:]:
        copy.wait()

    def row(n, _):
        x = solve(rhs_v[n], pre_v[n])
        x_half[n] = x
        xb[n] = x.astype(jnp.bfloat16)
        return 0

    lax.fori_loop(0, ROWS, row, 0, unroll=UNROLL)
    for k in range(FAN):
        for slot in range(CAP):

            @pl.when(slot < counts[k])
            def _():
                fetch(k, slot, 0).wait()

    remote_terms(core, own, table, lambda e: xb[e], lambda face, at, e: blocks[face * CAP + at], (m0, m1, m2), (t0, t1, t2), local_s)


def local_terms(first, last, own, xb, off_v, diag_v, owner, local, sums):
    def row(i, _):
        x = xb[i]
        places, terms = [i], [jnp.dot(x, diag_v[i], preferred_element_type=jnp.float32)]
        for k in range(FAN):
            places.append(jnp.where(owner[k, i] == own, local[k, i], ROWS))
            terms.append(jnp.dot(x, off_v[i, k], preferred_element_type=jnp.float32))
        for place, term in zip(places, terms):
            sums[place] = sums[place] + term
        return 0

    lax.fori_loop(first, last, row, 0, unroll=min(last - first, LOCAL_UNROLL))


def first_local_kernel(off, diag, xb, owner, local, off_v, diag_v, table, *rest):
    partial, (sums, owner_s, local_s, sems, small_sems) = rest[:PIECES], rest[PIECES:]
    own = lax.axis_index("rows")
    small = [pltpu.make_async_copy(a, b, small_sems.at[k]) for k, (a, b) in enumerate(((owner, owner_s), (local, local_s)))]
    for copy in small:
        copy.start()
    copies = []
    for chunk in range(CHUNKS):
        part = pl.ds(chunk * PER, PER)
        copies.append([pltpu.make_async_copy(a.at[part], b.at[part], sems.at[k, chunk]) for k, (a, b) in enumerate(((off, off_v), (diag, diag_v)))])
        for copy in copies[-1]:
            copy.start()
    sums[...] = jnp.zeros(sums.shape, sums.dtype)
    for copy in small:
        copy.wait()
    for face in range(FAN):
        list_face(face, own, owner_s, table)
    for chunk in range(CHUNKS):
        for copy in copies[chunk]:
            copy.wait()
        local_terms(chunk * PER, (chunk + 1) * PER, own, xb, off_v, diag_v, owner_s, local_s, sums)
    for piece in range(PIECES):
        partial[piece][...] = sums[piece * PIECE : (piece + 1) * PIECE]


def place(messages, label_of, first, narrow_sum, wide_sum):
    lane = lax.broadcasted_iota(jnp.int32, (ADJ, 128), 1)
    for p, message in enumerate(messages):
        for s in range(CAP // 2):
            at = []
            for slot in (s, s + CAP // 2):
                label = label_of(first + p * CAP + slot)
                at.append(jnp.where(label == 0, ROWS, label - 1))
                wide_sum[at[-1]] += message[slot * ADJ : (slot + 1) * ADJ].astype(jnp.float32)
            both = message[WIDE + s * ADJ : WIDE + (s + 1) * ADJ].astype(jnp.float32)
            narrow_sum[at[0]] += jnp.where(lane < 64, both, 0.0)
            narrow_sum[at[1]] += jnp.where(lane < 64, 0.0, both)


def gather_labels(messages, row):
    found = jnp.concatenate([m[BODY:].astype(jnp.float32) for m in messages], axis=0)
    rows = lax.broadcasted_iota(jnp.int32, found.shape, 0)
    lanes = lax.broadcasted_iota(jnp.int32, found.shape, 1)
    row[...] = jnp.sum(jnp.where(rows == lanes, found, 0.0), axis=0, keepdims=True).astype(jnp.int32)


def receive(labels_copy, labels_s, messages, ours, other, both, wides, narrows):
    for ref in (*wides, *narrows):
        ref[...] = jnp.zeros(ref.shape, ref.dtype)
    for piece in range(PIECES):
        both[piece * PIECE : (piece + 1) * PIECE] = ours[piece][...] + other[piece][...]
    labels_copy.wait()
    label_of = lambda at: labels_s[0, at]
    place(messages[:3], label_of, 0, narrows[0], wides[0])
    place(messages[3:], label_of, 3 * CAP, narrows[1], wides[1])


def residual_of(n, rhs, both, wides, narrows):
    narrow = narrows[0][n] + narrows[1][n]
    narrow = narrow + pltpu.roll(narrow, 64, 1)
    got = jnp.concatenate([wides[0][n] + wides[1][n], narrow[:, 0:64]], axis=1)
    return rhs[n] - (both[n] + got)


def middle_kernel(off_v, pre_v, rhs, table, x_before, *rest):
    ours, others, messages, rest = rest[:PIECES], rest[PIECES : 2 * PIECES], rest[2 * PIECES : 2 * PIECES + 6], rest[2 * PIECES + 6 :]
    vb, xb, labels, m0, m1, m2, t0, t1, t2, both, wide_a, wide_b, narrow_a, narrow_b, table_s, labels_s, sems = rest
    core, own = lax.axis_index("blk"), lax.axis_index("rows")
    table_copy = pltpu.make_async_copy(table, table_s, sems.at[0])
    table_copy.start()
    gather_labels(messages, labels)
    labels_copy = pltpu.make_async_copy(labels, labels_s, sems.at[1])
    labels_copy.start()
    wides, narrows = (wide_a, wide_b), (narrow_a, narrow_b)
    receive(labels_copy, labels_s, messages, ours, others, both, wides, narrows)

    def row(n, _):
        left = residual_of(n, rhs, both, wides, narrows).astype(jnp.bfloat16)
        vb[n] = left
        xb[n] = (x_before[n] + solve(left, pre_v[n])).astype(jnp.bfloat16)
        return 0

    lax.fori_loop(0, ROWS, row, 0, unroll=UNROLL)
    table_copy.wait()
    remote_terms(core, own, table_s, lambda e: xb[e], lambda face, at, e: off_v[e, face], (m0, m1, m2), (t0, t1, t2))


def middle_local_kernel(off_v, diag_v, xb, owner, local, *rest):
    partial, sums = rest[:PIECES], rest[PIECES]
    own = lax.axis_index("rows")
    sums[...] = jnp.zeros(sums.shape, sums.dtype)
    local_terms(0, ROWS, own, xb, off_v, diag_v, owner, local, sums)
    for piece in range(PIECES):
        partial[piece][...] = sums[piece * PIECE : (piece + 1) * PIECE]


def last_kernel(pre_v, pre_other, rhs, vb, *rest):
    ours, others, rest = rest[:PIECES], rest[PIECES : 2 * PIECES], rest[2 * PIECES :]
    labels, messages, rest = rest[0], rest[1:7], rest[7:]
    adjoint, residual, adjoint_v, residual_v, both, wide_a, wide_b, narrow_a, narrow_b, labels_s, label_sem, sems = rest
    core = lax.axis_index("blk")
    labels_copy = pltpu.make_async_copy(labels, labels_s, label_sem)
    labels_copy.start()
    wides, narrows = (wide_a, wide_b), (narrow_a, narrow_b)
    receive(labels_copy, labels_s, messages, ours, others, both, wides, narrows)

    def row(n, _):
        left = residual_of(n, rhs, both, wides, narrows)
        residual_v[n] = left
        fields = jnp.concatenate([rhs[n].astype(jnp.bfloat16), vb[n], left.astype(jnp.bfloat16)], axis=0)
        halves = [solve(fields, blocks[n]) for blocks in (pre_v, pre_other)]
        mine, theirs = [(half[0:ADJ] + half[ADJ : 2 * ADJ]) + half[2 * ADJ :] for half in halves]
        adjoint_v[n, :, 0:HALF] = jnp.where(core == 0, mine, theirs)
        adjoint_v[n, :, HALF:WIDTH] = jnp.where(core == 0, theirs, mine)
        return 0

    copies = []
    for piece in range(PARTS):
        rows = pl.ds(piece * (ROWS // PARTS), ROWS // PARTS)
        lax.fori_loop(piece * (ROWS // PARTS), (piece + 1) * (ROWS // PARTS), row, 0, unroll=True)
        for k, (a, b) in enumerate(((residual_v, residual), (adjoint_v, adjoint))):
            copies.append(pltpu.make_async_copy(a.at[rows], b.at[rows], sems.at[k, piece]))
            copies[-1].start()
    for copy in copies:
        copy.wait()


def call(kernel, name, out_shape, in_specs, out_specs, scratch_shapes, cost=None):
    params = pltpu.CompilerParams(vmem_limit_bytes=VMEM_LIMIT)
    return pl.pallas_call(kernel, out_shape=out_shape, in_specs=in_specs, out_specs=out_specs, scratch_shapes=scratch_shapes,
                          compiler_params=params, cost_estimate=cost, name=name)


def on_device(off_blocks, diag_blocks, precond, adj_rhs, col_owner, col_local):
    nrows = lax.axis_size("rows")
    offsets = (1, nrows - 1, 2, nrows - 2, nrows // 2, nrows // 2 + 1)
    shape, f32, bf16, i32 = jax.ShapeDtypeStruct, jnp.float32, jnp.bfloat16, jnp.int32
    field, half_blocks = shape((ROWS, ADJ, WIDTH), f32), shape((ROWS, HALF, WIDTH), bf16)
    pieces = [shape((PIECE, ADJ, WIDTH), f32)] * PIECES
    row_of_ints = shape((1, 128), i32)
    dma = pltpu.SemaphoreType.DMA

    def across(x):
        return lax.ppermute(x, "blk", [(0, 1), (1, 0)])

    def to_faces(x, p):
        pairs = [(2 * i + c, 2 * ((i + offsets[FACES[ORDER[p]][c][i % 4]]) % nrows) + c) for i in range(nrows) for c in range(2)]
        return lax.ppermute(x, ("rows", "blk"), pairs)

    def tie(*arrays):
        return lax.optimization_barrier(arrays)

    def exchange(mine, theirs, *later, chain=False):
        sums = []
        for m, t in zip(mine, theirs):
            if sums and chain:
                t, sums[0] = tie(t, sums[0])
            sums.append((m + across(t).astype(f32)).astype(bf16))
        got = [to_faces(x, p) for p, x in enumerate(sums)]
        later = lax.optimization_barrier((*sums, *later))[len(sums) :]
        return got, *later

    def hand_on(got, parts):
        for p in range(len(FACES)):
            if p == TIE:
                got[p], parts[0] = tie(got[p], parts[0])
            else:
                got[p] = tie(got[p], parts[0])[0]
        return parts, [across(x) for x in parts], got, [across(g) for g in got]

    def in_hbm(*arrays):
        return [pltpu.with_memory_space_constraint(x, pltpu.HBM) for x in arrays]

    cost = pl.CostEstimate(flops=2 * ROWS * (FAN + 1) * ADJ * HALF * WIDTH, bytes_accessed=40_000_000, transcendentals=0)
    ints = [pltpu.SMEM((FAN, ROWS), i32)] * 2
    received = [pltpu.VMEM((ROWS, ADJ, WIDTH), f32)] + [pltpu.VMEM((ROWS + 1, ADJ, 128), f32)] * 4
    sums = pltpu.VMEM((ROWS + 1, ADJ, WIDTH), f32)
    owner, local = col_owner.T, col_local.T
    pre_other = across(precond)

    x_half, xb, pre_v, *messages = call(
        first_kernel,
        "first_remote_terms",
        [shape((ROWS, ADJ, HALF), f32), shape((ROWS, ADJ, HALF), bf16), half_blocks]
        + [shape((BODY + CAP, 128), f32)] * 3 + [shape((BODY + CAP, 128), bf16)] * 3,
        [HBM] * 5,
        [VM] * 9,
        [pltpu.VMEM((FAN * CAP, HALF, WIDTH), bf16), pltpu.VMEM((ROWS, ADJ, WIDTH), f32)] + ints
        + [pltpu.SMEM((1, 128), i32), dma((FAN * CAP,)), dma, dma((3,))],
    )(*in_hbm(off_blocks, precond, adj_rhs, owner, local))
    got, xb = exchange(messages[:3], messages[3:], xb)
    xb, pre_other = tie(xb, pre_other)
    off_v, diag_v, table, *partial = call(
        first_local_kernel,
        "first_local_terms",
        [shape((ROWS, FAN, HALF, WIDTH), bf16), half_blocks, row_of_ints] + pieces,
        [HBM, HBM, VM, HBM, HBM],
        [VM] * 2 + [SM] + [VM] * PIECES,
        [sums] + ints + [dma((2, CHUNKS)), dma((2,))],
        cost,
    )(*in_hbm(off_blocks, diag_blocks), xb, *in_hbm(owner, local))
    partial, other, got, forwarded = hand_on(got, list(partial))

    vb, xb, labels, *messages = call(
        middle_kernel,
        "middle_remote_terms",
        [shape((ROWS, ADJ, WIDTH), bf16), shape((ROWS, ADJ, HALF), bf16), row_of_ints]
        + [shape((BODY, 128), f32)] * 3 + [shape((BODY, 128), bf16)] * 3,
        [VM, VM, VM, ANY, VM] + [VM] * (2 * PIECES + 6),
        [VM] * 9,
        received + [pltpu.SMEM((1, 128), i32), pltpu.SMEM((1, 128), i32), dma((2,))],
    )(off_v, pre_v, adj_rhs, table, x_half, *partial, *other, *got, *forwarded)
    got, xb = exchange(messages[:3], messages[3:], xb, chain=True)
    partial = call(
        middle_local_kernel,
        "middle_local_terms",
        pieces,
        [VM, VM, VM, SM, SM],
        [VM] * PIECES,
        [sums],
        cost,
    )(off_v, diag_v, xb, owner, local)
    partial, other, got, forwarded = hand_on(got, list(partial))

    return call(
        last_kernel,
        "last_terms",
        [field, field],
        [VM] * (4 + 2 * PIECES) + [ANY] + [VM] * 6,
        [HBM] * 2,
        [pltpu.VMEM((ROWS, ADJ, WIDTH), f32)] * 2 + received + [pltpu.SMEM((1, 128), i32), dma, dma((2, PARTS))],
    )(pre_v, pre_other, adj_rhs, vb, *partial, *other, labels, *got, *forwarded)


def solution(mesh):
    in_specs = (
        P("rows", None, "blk", None),
        P("rows", "blk", None),
        P("rows", "blk", None),
        P("rows", None, None),
        P("rows", None),
        P("rows", None),
    )
    out_specs = (P("rows", None, None), P("rows", None, None))

    def program(*arrays):
        return tuple(on_device(*arrays))

    return jax.shard_map(program, mesh=mesh, in_specs=in_specs, out_specs=out_specs, check_vma=False)
```

time: 54.1 us -> 48.8 us (0.902)
  Pallas kernels: 22.6 us -> 17.1 us
  waiting for transfers between devices: 6.54 us -> 9.56 us
  starting transfers between devices: 23.9 us -> 20.9 us
    ppermute x6, waiting for transfers between devices: 2.39 us -> 5.5 us  [to_faces(): return lax.ppermute(x, ('rows', 'blk'), pairs)]
    pallas_call x1, Pallas kernels: 4.55 us -> 2.44 us  [on_device(): call(middle_kernel, 'middle_remote_terms', [shape((ROWS, ADJ, WIDTH), bf1...]
    ppermute x6, starting transfers between devices: 17 us -> 15.3 us  [to_faces(): return lax.ppermute(x, ('rows', 'blk'), pairs)]
    pallas_call x1, Pallas kernels: 4.42 us -> 2.73 us  [on_device(): call(last_kernel, 'last_terms', [field, field], [VM] * (4 + 2 * PIECES) +...]
    pallas_call x1, Pallas kernels: 5.8 us -> 4.4 us  [on_device(): call(first_kernel, 'first_remote_terms', [shape((ROWS, ADJ, HALF), f32),...]
    ppermute x21 -> x17, starting transfers between devices: 6.84 us -> 5.63 us  [across(): return lax.ppermute(x, 'blk', [(0, 1), (1, 0)])]
    pallas_call x1, Pallas kernels: 3.19 us -> 2.45 us  [on_device(): call(middle_local_kernel, 'middle_local_terms', pieces, [VM, VM, VM, SM,...]
    ppermute x21 -> x17, waiting for transfers between devices: 4.15 us -> 4.05 us  [across(): return lax.ppermute(x, 'blk', [(0, 1), (1, 0)])]
  transfers between devices with their start and end apart: 27 -> 23, of which waited for: 12 -> 10; matrix products, arithmetic and copies ran while one was open for 0% -> 0% of each run, Pallas kernels for 14% -> 25%
where the time goes in v3:
time: 48.8 us; the launch traced here: 48.5 us
  starting transfers between devices  20.9 us (43%)
  Pallas kernels  17.1 us (35%)
  waiting for transfers between devices  9.56 us (20%)
  between operations  0.77 us (2%)
    ppermute x6, starting transfers between devices, to_faces(): return lax.ppermute(x, ('rows', 'blk'), pairs)  15.3 us
    ppermute x17, starting transfers between devices, across(): return lax.ppermute(x, 'blk', [(0, 1), (1, 0)])  5.63 us
    ppermute x6, waiting for transfers between devices, to_faces(): return lax.ppermute(x, ('rows', 'blk'), pairs)  5.5 us
    pallas_call x1, Pallas kernels, on_device(): call(first_local_kernel, 'first_local_terms', [shape((ROWS, FAN, HALF, WI...  5.09 us
    pallas_call x1, Pallas kernels, on_device(): call(first_kernel, 'first_remote_terms', [shape((ROWS, ADJ, HALF), f32),...  4.4 us
    ppermute x17, waiting for transfers between devices, across(): return lax.ppermute(x, 'blk', [(0, 1), (1, 0)])  4.05 us
    pallas_call x1, Pallas kernels, on_device(): call(last_kernel, 'last_terms', [field, field], [VM] * (4 + 2 * PIECES) +...  2.73 us
    pallas_call x1, Pallas kernels, on_device(): call(middle_local_kernel, 'middle_local_terms', pieces, [VM, VM, VM, SM,...  2.45 us
  transfers between devices with their start and end apart: 23, of which 10 were waited for; matrix products, arithmetic and copies ran while one was open for 0% of the time, Pallas kernels for 25%

profile of v3, /device:TPU:1, one launch (start us, length us, event | category | flops | bytes accessed | tf_op | source)
XLA Modules:
  0.0 48.5 jit_solution(3780541680990096824)
XLA Ops:
  0.6 1.5 %collective-permute-start.3 = (bf16[32,96,192]{2,1,0:T(8,128)(2,1)}, bf16[32,96,192]{2,1,0:T(8,128)(2,1)S(1)}, u32[]{:S(2)}, u32[]{:S(2)}) collective-permute-start(bf16[32,96,192]{2,1,0:T(8,128)(2,1)} %precond.1), channel_id=1, source_target_pairs={{0,1},{1,0},{2,3},{3,2},{4,5},{5,4},{6,7},{7,6},{8,9},{9,8},{10,11... | collective-permute-start | bytes 3538952 | tf_op jit(solution)/shard_map/ppermute | solution.py:295
  2.1 4.4 %first_remote_terms.1 = (f32[32,16,96]{2,1,0:T(8,128)S(1)}, bf16[32,16,96]{2,1,0:T(8,128)(2,1)S(1)}, bf16[32,96,192]{2,1,0:T(8,128)(2,1)S(1)}, f32[400,128]{1,0:...) custom-call(bf16[32,6,96,192]{3,2,1,0:T(8,128)(2,1)} %off.3, ...), custom_call_target="tpu_custom_call" | custom-call | tf_op jit(solution)/shard_map/first_remote_terms/pallas_call | solution.py:332
  6.5 0.1 collective-permute-start
  6.6 0.5 %collective-permute-start.1 = (bf16[400,128]{1,0:T(8,128)(2,1)S(1)}, bf16[400,128]{1,0:T(8,128)(2,1)S(1)}, u32[]{:S(2)}, u32[]{:S(2)}) collective-permute-start(bf16[400,128]{1,0:T(8,128)(2,1)S(1)} %get-tuple-element.47), channel_id=1, source_target_pairs={{0,1},{1,0},{2,3},{3,2},{4,5},{5,4},{6,7},{7,6},{8,9},{9,8},{10,11... | collective-permute-start | bytes 307208 | tf_op jit(solution)/shard_map/ppermute | solution.py:295
  7.1 0.1 collective-permute-start.2
  7.2 0.7 %collective-permute-done = bf16[400,128]{1,0:T(8,128)(2,1)S(1)} collective-permute-done((bf16[400,128]{1,0:T(8,128)(2,1)S(1)}, bf16[400,128]{1,0:T(8,128)(2,1)S(1)}, u32[]{:S(2)}, u32[]{:S(2)}) %collective-permute-start) | collective-permute-done | bytes 102432 | tf_op jit(solution)/shard_map/ppermute | solution.py:295
  7.9 8.8 %collective-permute-start.7 = (bf16[400,128]{1,0:T(8,128)(2,1)S(1)}, bf16[400,128]{1,0:T(8,128)(2,1)S(1)}, u32[]{:S(2)}, u32[]{:S(2)}) collective-permute-start(bf16[400,128]{1,0:T(8,128)(2,1)S(1)} %add_convert_fusion.2), channel_id=1, source_target_pairs={{0,126},{1,125},{2,4},{3,127},{4,2},{5,9},{6,8},{7,11},{8,6},{9,5}... | collective-permute-start | bytes 307208 | tf_op jit(solution)/shard_map/ppermute | solution.py:299
  16.8 0.8 %collective-permute-start.4 = (bf16[400,128]{1,0:T(8,128)(2,1)S(1)}, bf16[400,128]{1,0:T(8,128)(2,1)S(1)}, u32[]{:S(2)}, u32[]{:S(2)}) collective-permute-start(bf16[400,128]{1,0:T(8,128)(2,1)S(1)} %add_convert_fusion.1), channel_id=1, source_target_pairs={{0,64},{1,67},{2,66},{3,69},{4,68},{5,71},{6,70},{7,73},{8,72},{9,... | collective-permute-start | bytes 307208 | tf_op jit(solution)/shard_map/ppermute | solution.py:299
  17.7 5.1 %first_local_terms.1 = (bf16[32,6,96,192]{3,2,1,0:T(8,128)(2,1)S(1)}, bf16[32,96,192]{2,1,0:T(8,128)(2,1)S(1)}, s32[1,128]{1,0:T(1,128)S(1)}, f32[16,16,192]{2,1,0:T(8,128)S(1)}, f32[16,16,192]{2,1,0:T(8,128)S(1)}) custom-call(bf16[32,6,96,192]{3,2,1,0:T(8,128)(2,1)} %off.3, bf16[32,96,192]{2,1,0:T(8,128)(2,1)} %diag.1, ...), custom_call_target="tpu_custom_call" | custom-call | flops 132120576 | bytes 40000000 | tf_op jit(solution)/shard_map/first_local_terms/pallas_call | solution.py:344
  22.8 1.8 %collective-permute-done.4.rest_5_ = bf16[400,128]{1,0:T(8,128)(2,1)S(1)} collective-permute-done((bf16[400,128]{1,0:T(8,128)(2,1)S(1)}, bf16[400,128]{1,0:T(8,128)(2,1)S(1)}, u32[]{:S(2)}, u32[]{:S(2)}) %collective-permute-start.4) | collective-permute-done | bytes 102432 | tf_op jit(solution)/shard_map/ppermute | solution.py:299
  24.6 0.5 %collective-permute-start.6 = (f32[16,16,192]{2,1,0:T(8,128)S(1)}, f32[16,16,192]{2,1,0:T(8,128)S(1)}, u32[]{:S(2)}, u32[]{:S(2)}) collective-permute-start(f32[16,16,192]{2,1,0:T(8,128)S(1)} %get-tuple-element.59.rest_1_), channel_id=1, source_target_pairs={{0,1},{1,0},{2,3},{3,2},{4,5},{5,4},{6,7},{7,6},{8,9},{9,8},{10,11... | collective-permute-start | bytes 589832 | tf_op jit(solution)/shard_map/ppermute | solution.py:295
  25.2 0.4 collective-permute-start.10
  25.7 0.1 collective-permute-start.9
  25.7 0.9 %collective-permute-done.11.rest_9_ = bf16[400,128]{1,0:T(8,128)(2,1)S(1)} collective-permute-done((bf16[400,128]{1,0:T(8,128)(2,1)S(1)}, bf16[400,128]{1,0:T(8,128)(2,1)S(1)}, u32[]{:S(2)}, u32[]{:S(2)}) %collective-permute-start.11) | collective-permute-done | bytes 102432 | tf_op jit(solution)/shard_map/ppermute | solution.py:295
  26.7 0.1 collective-permute-done.10.rest_8_
  26.8 0.1 collective-permute-done.9.rest_7_
  27.0 2.4 %middle_remote_terms.1 = (bf16[32,16,192]{2,1,0:T(8,128)(2,1)S(1)}, bf16[32,16,96]{2,1,0:T(8,128)(2,1)S(1)}, s32[1,128]{1,0:T(1,128)S(1)}, f32[384,128]{1,0:T(8,...) custom-call(bf16[32,6,96,192]{3,2,1,0:T(8,128)(2,1)S(1)} %get-tuple-, ...), custom_call_target="tpu_custom_call" | custom-call | tf_op jit(solution)/shard_map/middle_remote_terms/pallas_call | solution.py:355
  29.5 0.2 collective-permute-start.12
  29.7 1.2 %collective-permute-done.12 = bf16[384,128]{1,0:T(8,128)(2,1)S(1)} collective-permute-done((bf16[384,128]{1,0:T(8,128)(2,1)S(1)}, bf16[384,128]{1,0:T(8,128)(2,1)S(1)}, u32[]{:S(2)}, u32[]{:S(2)}) %collective-permute-start.12) | collective-permute-done | bytes 98336 | tf_op jit(solution)/shard_map/ppermute | solution.py:295
  30.9 0.2 collective-permute-start.13
  31.1 0.4 collective-permute-start.15
  31.5 4.0 %collective-permute-start.18 = (bf16[384,128]{1,0:T(8,128)(2,1)S(1)}, bf16[384,128]{1,0:T(8,128)(2,1)S(1)}, u32[]{:S(2)}, u32[]{:S(2)}) collective-permute-start(bf16[384,128]{1,0:T(8,128)(2,1)S(1)} %add_convert_fusion.5), channel_id=1, source_target_pairs={{0,126},{1,125},{2,4},{3,127},{4,2},{5,9},{6,8},{7,11},{8,6},{9,5}... | collective-permute-start | bytes 294920 | tf_op jit(solution)/shard_map/ppermute | solution.py:299
  35.5 1.5 %collective-permute-start.14 = (bf16[384,128]{1,0:T(8,128)(2,1)S(1)}, bf16[384,128]{1,0:T(8,128)(2,1)S(1)}, u32[]{:S(2)}, u32[]{:S(2)}) collective-permute-start(bf16[384,128]{1,0:T(8,128)(2,1)S(1)} %add_convert_fusion.4), channel_id=1, source_target_pairs={{0,64},{1,67},{2,66},{3,69},{4,68},{5,71},{6,70},{7,73},{8,72},{9,... | collective-permute-start | bytes 294920 | tf_op jit(solution)/shard_map/ppermute | solution.py:299
  37.2 2.5 %middle_local_terms.1 = (f32[16,16,192]{2,1,0:T(8,128)S(1)}, f32[16,16,192]{2,1,0:T(8,128)S(1)}) custom-call(bf16[32,6,96,192]{3,2,1,0:T(8,128)(2,1)S(1)} %get-tuple-element.54.off_v, bf16[32,96,192]{2,1,0:T(8,128)(2,1)S(1)} %get-tuple-element.69.diag_v, bf16[32,16,96]{2,1,0:T(8,128)(2,1)S(1)} %get-tuple-element.76.xb, s32[6,32]{1,0:T(8,128)S(1)} %bitcast.4, ...), custom_call_target="tpu_custom_call" | custom-call | flops 132120576 | bytes 40000000 | tf_op jit(solution)/shard_map/middle_local_terms/pallas_call | solution.py:365
  39.6 0.5 %collective-permute-start.17 = (f32[16,16,192]{2,1,0:T(8,128)S(1)}, f32[16,16,192]{2,1,0:T(8,128)S(1)}, u32[]{:S(2)}, u32[]{:S(2)}) collective-permute-start(f32[16,16,192]{2,1,0:T(8,128)S(1)} %get-tuple-element.79.rest_1_), channel_id=1, source_target_pairs={{0,1},{1,0},{2,3},{3,2},{4,5},{5,4},{6,7},{7,6},{8,9},{9,8},{10,11... | collective-permute-start | bytes 589832 | tf_op jit(solution)/shard_map/ppermute | solution.py:295
  40.1 3.7 %collective-permute-done.14.rest_6_ = bf16[384,128]{1,0:T(8,128)(2,1)S(1)} collective-permute-done((bf16[384,128]{1,0:T(8,128)(2,1)S(1)}, bf16[384,128]{1,0:T(8,128)(2,1)S(1)}, u32[]{:S(2)}, u32[]{:S(2)}) %collective-permute-start.14) | collective-permute-done | bytes 98336 | tf_op jit(solution)/shard_map/ppermute | solution.py:299
  43.8 0.5 %collective-permute-start.20 = (bf16[384,128]{1,0:T(8,128)(2,1)S(1)}, bf16[384,128]{1,0:T(8,128)(2,1)S(1)}, u32[]{:S(2)}, u32[]{:S(2)}) collective-permute-start(bf16[384,128]{1,0:T(8,128)(2,1)S(1)} %collective-permute-done.18.rest_5_), channel_id=1, source_target_pairs={{0,1},{1,0},{2,3},{3,2},{4,5},{5,4},{6,7},{7,6},{8,9},{9,8},{10,11... | collective-permute-start | bytes 294920 | tf_op jit(solution)/shard_map/ppermute | solution.py:295
  44.4 0.4 collective-permute-start.21
  44.8 0.6 %collective-permute-done.20.rest_8_ = bf16[384,128]{1,0:T(8,128)(2,1)S(1)} collective-permute-done((bf16[384,128]{1,0:T(8,128)(2,1)S(1)}, bf16[384,128]{1,0:T(8,128)(2,1)S(1)}, u32[]{:S(2)}, u32[]{:S(2)}) %collective-permute-start.20) | collective-permute-done | bytes 98336 | tf_op jit(solution)/shard_map/ppermute | solution.py:295
  45.5 0.1 collective-permute-done.22.rest_10_
  45.6 0.2 collective-permute-done.21.rest_9_
  45.8 2.7 %last_terms.1 = (f32[32,16,192]{2,1,0:T(8,128)}, f32[32,16,192]{2,1,0:T(8,128)}) custom-call(bf16[32,96,192]{2,1,0:T(8,128)(2,1)S(1)} %get-tuple-element.43.pre_v, bf16[32,96,192]{2,1,0:T(8,128)(2,1)S(1)} %collective-permute-done.3.pre_other, f32[32,16,192]{2,1,0:T(8,128)S(1)} %copy-done, bf16[32,16,192]{2,1,0:T(8,128)(2,1)S(1)} %get-tuple-element.63.vb, ...), custom_call_target="tpu_custom_call" | custom-call | tf_op jit(solution)/shard_map/last_terms/pallas_call | solution.py:376
  (31 shorter events, 0.6 us)
Async XLA Ops:
  0.6 17.1 %collective-permute-start.3 = (bf16[32,96,192]{2,1,0:T(8,128)(2,1)}, bf16[32,96,192]{2,1,0:T(8,128)(2,1)S(1)}, u32[]{:S(2)}, u32[]{:S(2)}) collective-permute-start(bf16[32,96,192]{2,1,0:T(8,128)(2,1)} %precond.1), channel_id=1, source_target_pairs={{0,1},{1,0},{2,3},{3,2},{4,5},{5,4},{6,7},{7,6},{8,9},{9,8},{10,11... | collective-permute-start | bytes 3538952 | tf_op jit(solution)/shard_map/ppermute | solution.py:295
  6.5 1.4 %collective-permute-start = (bf16[400,128]{1,0:T(8,128)(2,1)S(1)}, bf16[400,128]{1,0:T(8,128)(2,1)S(1)}, u32[]{:S(2)}, u32[]{:S(2)}) collective-permute-start(bf16[400,128]{1,0:T(8,128)(2,1)S(1)} %get-tuple-element.45), channel_id=1, source_target_pairs={{0,1},{1,0},{2,3},{3,2},{4,5},{5,4},{6,7},{7,6},{8,9},{9,8},{10,11... | collective-permute-start | bytes 307208 | tf_op jit(solution)/shard_map/ppermute | solution.py:295
  6.6 10.2 %collective-permute-start.1 = (bf16[400,128]{1,0:T(8,128)(2,1)S(1)}, bf16[400,128]{1,0:T(8,128)(2,1)S(1)}, u32[]{:S(2)}, u32[]{:S(2)}) collective-permute-start(bf16[400,128]{1,0:T(8,128)(2,1)S(1)} %get-tuple-element.47), channel_id=1, source_target_pairs={{0,1},{1,0},{2,3},{3,2},{4,5},{5,4},{6,7},{7,6},{8,9},{9,8},{10,11... | collective-permute-start | bytes 307208 | tf_op jit(solution)/shard_map/ppermute | solution.py:295
  7.1 10.5 %collective-permute-start.2 = (bf16[400,128]{1,0:T(8,128)(2,1)S(1)}, bf16[400,128]{1,0:T(8,128)(2,1)S(1)}, u32[]{:S(2)}, u32[]{:S(2)}) collective-permute-start(bf16[400,128]{1,0:T(8,128)(2,1)S(1)} %get-tuple-element.49), channel_id=1, source_target_pairs={{0,1},{1,0},{2,3},{3,2},{4,5},{5,4},{6,7},{7,6},{8,9},{9,8},{10,11... | collective-permute-start | bytes 307208 | tf_op jit(solution)/shard_map/ppermute | solution.py:295
  7.9 17.2 %collective-permute-start.7 = (bf16[400,128]{1,0:T(8,128)(2,1)S(1)}, bf16[400,128]{1,0:T(8,128)(2,1)S(1)}, u32[]{:S(2)}, u32[]{:S(2)}) collective-permute-start(bf16[400,128]{1,0:T(8,128)(2,1)S(1)} %add_convert_fusion.2), channel_id=1, source_target_pairs={{0,126},{1,125},{2,4},{3,127},{4,2},{5,9},{6,8},{7,11},{8,6},{9,5}... | collective-permute-start | bytes 307208 | tf_op jit(solution)/shard_map/ppermute | solution.py:299
  16.8 7.8 %collective-permute-start.4 = (bf16[400,128]{1,0:T(8,128)(2,1)S(1)}, bf16[400,128]{1,0:T(8,128)(2,1)S(1)}, u32[]{:S(2)}, u32[]{:S(2)}) collective-permute-start(bf16[400,128]{1,0:T(8,128)(2,1)S(1)} %add_convert_fusion.1), channel_id=1, source_target_pairs={{0,64},{1,67},{2,66},{3,69},{4,68},{5,71},{6,70},{7,73},{8,72},{9,... | collective-permute-start | bytes 307208 | tf_op jit(solution)/shard_map/ppermute | solution.py:299
  17.6 7.5 %collective-permute-start.8 = (bf16[400,128]{1,0:T(8,128)(2,1)S(1)}, bf16[400,128]{1,0:T(8,128)(2,1)S(1)}, u32[]{:S(2)}, u32[]{:S(2)}) collective-permute-start(bf16[400,128]{1,0:T(8,128)(2,1)S(1)} %add_convert_fusion), channel_id=1, source_target_pairs={{0,2},{1,5},{2,0},{3,7},{4,6},{5,1},{6,4},{7,3},{8,10},{9,13},{10,... | collective-permute-start | bytes 307208 | tf_op jit(solution)/shard_map/ppermute | solution.py:299
  17.7 9.3 %copy-start = (f32[32,16,192]{2,1,0:T(8,128)S(1)}, f32[32,16,192]{2,1,0:T(8,128)}, u32[]{:S(2)}) copy-start(f32[32,16,192]{2,1,0:T(8,128)} %rhs.5) | copy-start | bytes 1179652
  24.6 2.4 %collective-permute-start.5 = (f32[16,16,192]{2,1,0:T(8,128)S(1)}, f32[16,16,192]{2,1,0:T(8,128)S(1)}, u32[]{:S(2)}, u32[]{:S(2)}) collective-permute-start(f32[16,16,192]{2,1,0:T(8,128)S(1)} %get-tuple-element.58.rest_0_), channel_id=1, source_target_pairs={{0,1},{1,0},{2,3},{3,2},{4,5},{5,4},{6,7},{7,6},{8,9},{9,8},{10,11... | collective-permute-start | bytes 589832 | tf_op jit(solution)/shard_map/ppermute | solution.py:295
  24.6 2.4 %collective-permute-start.6 = (f32[16,16,192]{2,1,0:T(8,128)S(1)}, f32[16,16,192]{2,1,0:T(8,128)S(1)}, u32[]{:S(2)}, u32[]{:S(2)}) collective-permute-start(f32[16,16,192]{2,1,0:T(8,128)S(1)} %get-tuple-element.59.rest_1_), channel_id=1, source_target_pairs={{0,1},{1,0},{2,3},{3,2},{4,5},{5,4},{6,7},{7,6},{8,9},{9,8},{10,11... | collective-permute-start | bytes 589832 | tf_op jit(solution)/shard_map/ppermute | solution.py:295
  25.1 1.5 %collective-permute-start.11 = (bf16[400,128]{1,0:T(8,128)(2,1)S(1)}, bf16[400,128]{1,0:T(8,128)(2,1)S(1)}, u32[]{:S(2)}, u32[]{:S(2)}) collective-permute-start(bf16[400,128]{1,0:T(8,128)(2,1)S(1)} %collective-permute-done.8.rest_6_), channel_id=1, source_target_pairs={{0,1},{1,0},{2,3},{3,2},{4,5},{5,4},{6,7},{7,6},{8,9},{9,8},{10,11... | collective-permute-start | bytes 307208 | tf_op jit(solution)/shard_map/ppermute | solution.py:295
  25.2 1.6 %collective-permute-start.10 = (bf16[400,128]{1,0:T(8,128)(2,1)S(1)}, bf16[400,128]{1,0:T(8,128)(2,1)S(1)}, u32[]{:S(2)}, u32[]{:S(2)}) collective-permute-start(bf16[400,128]{1,0:T(8,128)(2,1)S(1)} %collective-permute-done.4.rest_5_), channel_id=1, source_target_pairs={{0,1},{1,0},{2,3},{3,2},{4,5},{5,4},{6,7},{7,6},{8,9},{9,8},{10,11... | collective-permute-start | bytes 307208 | tf_op jit(solution)/shard_map/ppermute | solution.py:295
  25.7 1.3 %collective-permute-start.9 = (bf16[400,128]{1,0:T(8,128)(2,1)S(1)}, bf16[400,128]{1,0:T(8,128)(2,1)S(1)}, u32[]{:S(2)}, u32[]{:S(2)}) collective-permute-start(bf16[400,128]{1,0:T(8,128)(2,1)S(1)} %collective-permute-done.7.rest_4_), channel_id=1, source_target_pairs={{0,1},{1,0},{2,3},{3,2},{4,5},{5,4},{6,7},{7,6},{8,9},{9,8},{10,11... | collective-permute-start | bytes 307208 | tf_op jit(solution)/shard_map/ppermute | solution.py:295
  27.0 10.1 %copy-start.1 = (s32[32,6]{0,1:T(8,128)S(1)}, s32[32,6]{0,1:T(8,128)}, u32[]{:S(2)}) copy-start(s32[32,6]{0,1:T(8,128)} %param.10) | copy-start | bytes 2308
  27.0 10.1 %copy-start.2 = (s32[32,6]{0,1:T(8,128)S(1)}, s32[32,6]{0,1:T(8,128)}, u32[]{:S(2)}) copy-start(s32[32,6]{0,1:T(8,128)} %param.11) | copy-start | bytes 2308
  29.5 1.4 %collective-permute-start.12 = (bf16[384,128]{1,0:T(8,128)(2,1)S(1)}, bf16[384,128]{1,0:T(8,128)(2,1)S(1)}, u32[]{:S(2)}, u32[]{:S(2)}) collective-permute-start(bf16[384,128]{1,0:T(8,128)(2,1)S(1)} %get-tuple-element.67), channel_id=1, source_target_pairs={{0,1},{1,0},{2,3},{3,2},{4,5},{5,4},{6,7},{7,6},{8,9},{9,8},{10,11... | collective-permute-start | bytes 294920 | tf_op jit(solution)/shard_map/ppermute | solution.py:295
  30.9 4.6 %collective-permute-start.13 = (bf16[384,128]{1,0:T(8,128)(2,1)S(1)}, bf16[384,128]{1,0:T(8,128)(2,1)S(1)}, u32[]{:S(2)}, u32[]{:S(2)}) collective-permute-start(bf16[384,128]{1,0:T(8,128)(2,1)S(1)} %get-tuple-element.68), channel_id=1, source_target_pairs={{0,1},{1,0},{2,3},{3,2},{4,5},{5,4},{6,7},{7,6},{8,9},{9,8},{10,11... | collective-permute-start | bytes 294920 | tf_op jit(solution)/shard_map/ppermute | solution.py:295
  31.1 5.9 %collective-permute-start.15 = (bf16[384,128]{1,0:T(8,128)(2,1)S(1)}, bf16[384,128]{1,0:T(8,128)(2,1)S(1)}, u32[]{:S(2)}, u32[]{:S(2)}) collective-permute-start(bf16[384,128]{1,0:T(8,128)(2,1)S(1)} %get-tuple-element.74), channel_id=1, source_target_pairs={{0,1},{1,0},{2,3},{3,2},{4,5},{5,4},{6,7},{7,6},{8,9},{9,8},{10,11... | collective-permute-start | bytes 294920 | tf_op jit(solution)/shard_map/ppermute | solution.py:295
  31.5 12.4 %collective-permute-start.18 = (bf16[384,128]{1,0:T(8,128)(2,1)S(1)}, bf16[384,128]{1,0:T(8,128)(2,1)S(1)}, u32[]{:S(2)}, u32[]{:S(2)}) collective-permute-start(bf16[384,128]{1,0:T(8,128)(2,1)S(1)} %add_convert_fusion.5), channel_id=1, source_target_pairs={{0,126},{1,125},{2,4},{3,127},{4,2},{5,9},{6,8},{7,11},{8,6},{9,5}... | collective-permute-start | bytes 294920 | tf_op jit(solution)/shard_map/ppermute | solution.py:299
  35.5 8.4 %collective-permute-start.14 = (bf16[384,128]{1,0:T(8,128)(2,1)S(1)}, bf16[384,128]{1,0:T(8,128)(2,1)S(1)}, u32[]{:S(2)}, u32[]{:S(2)}) collective-permute-start(bf16[384,128]{1,0:T(8,128)(2,1)S(1)} %add_convert_fusion.4), channel_id=1, source_target_pairs={{0,64},{1,67},{2,66},{3,69},{4,68},{5,71},{6,70},{7,73},{8,72},{9,... | collective-permute-start | bytes 294920 | tf_op jit(solution)/shard_map/ppermute | solution.py:299
  37.0 7.3 %collective-permute-start.19 = (bf16[384,128]{1,0:T(8,128)(2,1)S(1)}, bf16[384,128]{1,0:T(8,128)(2,1)S(1)}, u32[]{:S(2)}, u32[]{:S(2)}) collective-permute-start(bf16[384,128]{1,0:T(8,128)(2,1)S(1)} %add_convert_fusion.3), channel_id=1, source_target_pairs={{0,2},{1,5},{2,0},{3,7},{4,6},{5,1},{6,4},{7,3},{8,10},{9,13},{10,... | collective-permute-start | bytes 294920 | tf_op jit(solution)/shard_map/ppermute | solution.py:299
  39.6 6.2 %collective-permute-start.17 = (f32[16,16,192]{2,1,0:T(8,128)S(1)}, f32[16,16,192]{2,1,0:T(8,128)S(1)}, u32[]{:S(2)}, u32[]{:S(2)}) collective-permute-start(f32[16,16,192]{2,1,0:T(8,128)S(1)} %get-tuple-element.79.rest_1_), channel_id=1, source_target_pairs={{0,1},{1,0},{2,3},{3,2},{4,5},{5,4},{6,7},{7,6},{8,9},{9,8},{10,11... | collective-permute-start | bytes 589832 | tf_op jit(solution)/shard_map/ppermute | solution.py:295
  43.8 2.0 %collective-permute-start.16 = (f32[16,16,192]{2,1,0:T(8,128)S(1)}, f32[16,16,192]{2,1,0:T(8,128)S(1)}, u32[]{:S(2)}, u32[]{:S(2)}) collective-permute-start(f32[16,16,192]{2,1,0:T(8,128)S(1)} %get-tuple-element.78.rest_0_), channel_id=1, source_target_pairs={{0,1},{1,0},{2,3},{3,2},{4,5},{5,4},{6,7},{7,6},{8,9},{9,8},{10,11... | collective-permute-start | bytes 589832 | tf_op jit(solution)/shard_map/ppermute | solution.py:295
  43.8 1.7 %collective-permute-start.20 = (bf16[384,128]{1,0:T(8,128)(2,1)S(1)}, bf16[384,128]{1,0:T(8,128)(2,1)S(1)}, u32[]{:S(2)}, u32[]{:S(2)}) collective-permute-start(bf16[384,128]{1,0:T(8,128)(2,1)S(1)} %collective-permute-done.18.rest_5_), channel_id=1, source_target_pairs={{0,1},{1,0},{2,3},{3,2},{4,5},{5,4},{6,7},{7,6},{8,9},{9,8},{10,11... | collective-permute-start | bytes 294920 | tf_op jit(solution)/shard_map/ppermute | solution.py:295
  44.3 1.3 %collective-permute-start.22 = (bf16[384,128]{1,0:T(8,128)(2,1)S(1)}, bf16[384,128]{1,0:T(8,128)(2,1)S(1)}, u32[]{:S(2)}, u32[]{:S(2)}) collective-permute-start(bf16[384,128]{1,0:T(8,128)(2,1)S(1)} %collective-permute-done.19.rest_7_), channel_id=1, source_target_pairs={{0,1},{1,0},{2,3},{3,2},{4,5},{5,4},{6,7},{7,6},{8,9},{9,8},{10,11... | collective-permute-start | bytes 294920 | tf_op jit(solution)/shard_map/ppermute | solution.py:295
  44.4 1.4 %collective-permute-start.21 = (bf16[384,128]{1,0:T(8,128)(2,1)S(1)}, bf16[384,128]{1,0:T(8,128)(2,1)S(1)}, u32[]{:S(2)}, u32[]{:S(2)}) collective-permute-start(bf16[384,128]{1,0:T(8,128)(2,1)S(1)} %collective-permute-done.14.rest_6_), channel_id=1, source_target_pairs={{0,1},{1,0},{2,3},{3,2},{4,5},{5,4},{6,7},{7,6},{8,9},{9,8},{10,11... | collective-permute-start | bytes 294920 | tf_op jit(solution)/shard_map/ppermute | solution.py:295

commit v4 on v3

--- a/solution.py
+++ b/solution.py
@@ -14,7 +14,7 @@
 WIDE = CAP * ADJ
 BODY = WIDE + WIDE // 2
 NEAR, SEAM, FAR = 0, 1, 2
-ORDER = (SEAM, FAR, NEAR)
+ORDER = (FAR, SEAM, NEAR)
 FACES = (
     ((0, 1, 0, 1), (2, 2, 3, 3)),
     ((1, 0, 1, 0), (3, 3, 2, 2)),
@@ -24,7 +24,8 @@
 COUNTS = FAN * STRIDE
 CHUNKS = 8
 PIECES = 2
-TIE = 1
+TIE = 0
+LAST = 2
 PARTS = 4
 UNROLL = 32
 LOCAL_UNROLL = 16
@@ -317,7 +318,11 @@
                 got[p], parts[0] = tie(got[p], parts[0])
             else:
                 got[p] = tie(got[p], parts[0])[0]
-        return parts, [across(x) for x in parts], got, [across(g) for g in got]
+        others = [across(x) for x in parts]
+        forwarded = [across(g) if p != LAST else None for p, g in enumerate(got)]
+        got[LAST], forwarded[0] = tie(got[LAST], forwarded[0])
+        forwarded[LAST] = across(got[LAST])
+        return parts, others, got, forwarded
 
     def in_hbm(*arrays):
         return [pltpu.with_memory_space_constraint(x, pltpu.HBM) for x in arrays]
@@ -361,7 +366,7 @@
         [VM] * 9,
         received + [pltpu.SMEM((1, 128), i32), pltpu.SMEM((1, 128), i32), dma((2,))],
     )(off_v, pre_v, adj_rhs, table, x_half, *partial, *other, *got, *forwarded)
-    got, xb = exchange(messages[:3], messages[3:], xb, chain=True)
+    got, xb = exchange(messages[:3], messages[3:], xb, chain=False)
     partial = call(
         middle_local_kernel,
         "middle_local_terms",

time: 48.8 us -> 47.3 us (0.969)
  waiting for transfers between devices: 9.56 us -> 7.17 us
  starting transfers between devices: 20.9 us -> 22 us
    ppermute x6, waiting for transfers between devices: 5.5 us -> 3.22 us  [to_faces(): return lax.ppermute(x, ('rows', 'blk'), pairs)]
    ppermute x6, starting transfers between devices: 15.3 us -> 16.7 us  [to_faces(): return lax.ppermute(x, ('rows', 'blk'), pairs)]
  transfers between devices with their start and end apart: 23 -> 23, of which waited for: 10 -> 8; matrix products, arithmetic and copies ran while one was open for 0% -> 0% of each run, Pallas kernels for 25% -> 25%
where the time goes in v4:
time: 47.3 us; the launch traced here: 47.2 us
  starting transfers between devices  22 us (47%)
  Pallas kernels  17.1 us (36%)
  waiting for transfers between devices  7.17 us (15%)
  between operations  0.77 us (2%)
    ppermute x6, starting transfers between devices, to_faces(): return lax.ppermute(x, ('rows', 'blk'), pairs)  16.7 us
    ppermute x17, starting transfers between devices, across(): return lax.ppermute(x, 'blk', [(0, 1), (1, 0)])  5.32 us
    pallas_call x1, Pallas kernels, on_device(): call(first_local_kernel, 'first_local_terms', [shape((ROWS, FAN, HALF, WI...  5.09 us
    pallas_call x1, Pallas kernels, on_device(): call(first_kernel, 'first_remote_terms', [shape((ROWS, ADJ, HALF), f32),...  4.41 us
    ppermute x17, waiting for transfers between devices, across(): return lax.ppermute(x, 'blk', [(0, 1), (1, 0)])  3.94 us
    ppermute x6, waiting for transfers between devices, to_faces(): return lax.ppermute(x, ('rows', 'blk'), pairs)  3.22 us
    pallas_call x1, Pallas kernels, on_device(): call(last_kernel, 'last_terms', [field, field], [VM] * (4 + 2 * PIECES) +...  2.72 us
    pallas_call x1, Pallas kernels, on_device(): call(middle_local_kernel, 'middle_local_terms', pieces, [VM, VM, VM, SM,...  2.45 us
  transfers between devices with their start and end apart: 23, of which 8 were waited for; matrix products, arithmetic and copies ran while one was open for 0% of the time, Pallas kernels for 25%

profile of v4, /device:TPU:1, one launch (start us, length us, event | category | flops | bytes accessed | tf_op | source)
XLA Modules:
  0.0 47.2 jit_solution(14289455628591121134)
XLA Ops:
  0.6 1.5 %collective-permute-start.3 = (bf16[32,96,192]{2,1,0:T(8,128)(2,1)}, bf16[32,96,192]{2,1,0:T(8,128)(2,1)S(1)}, u32[]{:S(2)}, u32[]{:S(2)}) collective-permute-start(bf16[32,96,192]{2,1,0:T(8,128)(2,1)} %precond.1), channel_id=1, source_target_pairs={{0,1},{1,0},{2,3},{3,2},{4,5},{5,4},{6,7},{7,6},{8,9},{9,8},{10,11... | collective-permute-start | bytes 3538952 | tf_op jit(solution)/shard_map/ppermute | solution.py:296
  2.1 4.4 %first_remote_terms.1 = (f32[32,16,96]{2,1,0:T(8,128)S(1)}, bf16[32,16,96]{2,1,0:T(8,128)(2,1)S(1)}, bf16[32,96,192]{2,1,0:T(8,128)(2,1)S(1)}, f32[400,128]{1,0:...) custom-call(bf16[32,6,96,192]{3,2,1,0:T(8,128)(2,1)} %off.3, ...), custom_call_target="tpu_custom_call" | custom-call | tf_op jit(solution)/shard_map/first_remote_terms/pallas_call | solution.py:337
  6.6 0.1 collective-permute-start
  6.7 0.5 %collective-permute-start.1 = (bf16[400,128]{1,0:T(8,128)(2,1)S(1)}, bf16[400,128]{1,0:T(8,128)(2,1)S(1)}, u32[]{:S(2)}, u32[]{:S(2)}) collective-permute-start(bf16[400,128]{1,0:T(8,128)(2,1)S(1)} %get-tuple-element.47), channel_id=1, source_target_pairs={{0,1},{1,0},{2,3},{3,2},{4,5},{5,4},{6,7},{7,6},{8,9},{9,8},{10,11... | collective-permute-start | bytes 307208 | tf_op jit(solution)/shard_map/ppermute | solution.py:296
  7.1 0.1 collective-permute-start.2
  7.2 0.7 %collective-permute-done = bf16[400,128]{1,0:T(8,128)(2,1)S(1)} collective-permute-done((bf16[400,128]{1,0:T(8,128)(2,1)S(1)}, bf16[400,128]{1,0:T(8,128)(2,1)S(1)}, u32[]{:S(2)}, u32[]{:S(2)}) %collective-permute-start) | collective-permute-done | bytes 102432 | tf_op jit(solution)/shard_map/ppermute | solution.py:296
  8.0 4.1 %collective-permute-start.4 = (bf16[400,128]{1,0:T(8,128)(2,1)S(1)}, bf16[400,128]{1,0:T(8,128)(2,1)S(1)}, u32[]{:S(2)}, u32[]{:S(2)}) collective-permute-start(bf16[400,128]{1,0:T(8,128)(2,1)S(1)} %add_convert_fusion.2), channel_id=1, source_target_pairs={{0,64},{1,67},{2,66},{3,69},{4,68},{5,71},{6,70},{7,73},{8,72},{9,... | collective-permute-start | bytes 307208 | tf_op jit(solution)/shard_map/ppermute | solution.py:300
  12.1 6.6 %collective-permute-start.7 = (bf16[400,128]{1,0:T(8,128)(2,1)S(1)}, bf16[400,128]{1,0:T(8,128)(2,1)S(1)}, u32[]{:S(2)}, u32[]{:S(2)}) collective-permute-start(bf16[400,128]{1,0:T(8,128)(2,1)S(1)} %add_convert_fusion.1), channel_id=1, source_target_pairs={{0,126},{1,125},{2,4},{3,127},{4,2},{5,9},{6,8},{7,11},{8,6},{9,5}... | collective-permute-start | bytes 307208 | tf_op jit(solution)/shard_map/ppermute | solution.py:300
  18.8 5.1 %first_local_terms.1 = (bf16[32,6,96,192]{3,2,1,0:T(8,128)(2,1)S(1)}, bf16[32,96,192]{2,1,0:T(8,128)(2,1)S(1)}, s32[1,128]{1,0:T(1,128)S(1)}, f32[16,16,192]{2,1,0:T(8,128)S(1)}, f32[16,16,192]{2,1,0:T(8,128)S(1)}) custom-call(bf16[32,6,96,192]{3,2,1,0:T(8,128)(2,1)} %off.3, bf16[32,96,192]{2,1,0:T(8,128)(2,1)} %diag.1, ...), custom_call_target="tpu_custom_call" | custom-call | flops 132120576 | bytes 40000000 | tf_op jit(solution)/shard_map/first_local_terms/pallas_call | solution.py:349
  24.0 0.5 %collective-permute-start.5 = (f32[16,16,192]{2,1,0:T(8,128)S(1)}, f32[16,16,192]{2,1,0:T(8,128)S(1)}, u32[]{:S(2)}, u32[]{:S(2)}) collective-permute-start(f32[16,16,192]{2,1,0:T(8,128)S(1)} %get-tuple-element.58.rest_0_), channel_id=1, source_target_pairs={{0,1},{1,0},{2,3},{3,2},{4,5},{5,4},{6,7},{7,6},{8,9},{9,8},{10,11... | collective-permute-start | bytes 589832 | tf_op jit(solution)/shard_map/ppermute | solution.py:296
  24.5 0.1 collective-permute-start.6
  24.6 0.4 collective-permute-start.10
  25.0 0.3 collective-permute-done.9.rest_7_
  25.3 0.2 collective-permute-start.11
  25.4 0.7 %collective-permute-done.10.rest_8_ = bf16[400,128]{1,0:T(8,128)(2,1)S(1)} collective-permute-done((bf16[400,128]{1,0:T(8,128)(2,1)S(1)}, bf16[400,128]{1,0:T(8,128)(2,1)S(1)}, u32[]{:S(2)}, u32[]{:S(2)}) %collective-permute-start.10) | collective-permute-done | bytes 102432 | tf_op jit(solution)/shard_map/ppermute | solution.py:296
  26.2 0.4 collective-permute-done.11.rest_9_
  26.6 2.4 %middle_remote_terms.1 = (bf16[32,16,192]{2,1,0:T(8,128)(2,1)S(1)}, bf16[32,16,96]{2,1,0:T(8,128)(2,1)S(1)}, s32[1,128]{1,0:T(1,128)S(1)}, f32[384,128]{1,0:T(8,...) custom-call(bf16[32,6,96,192]{3,2,1,0:T(8,128)(2,1)S(1)} %get-tuple-, ...), custom_call_target="tpu_custom_call" | custom-call | tf_op jit(solution)/shard_map/middle_remote_terms/pallas_call | solution.py:360
  29.0 0.2 collective-permute-start.12
  29.2 0.4 collective-permute-start.14
  29.6 0.1 collective-permute-start.15
  29.8 0.6 %collective-permute-done.12 = bf16[384,128]{1,0:T(8,128)(2,1)S(1)} collective-permute-done((bf16[384,128]{1,0:T(8,128)(2,1)S(1)}, bf16[384,128]{1,0:T(8,128)(2,1)S(1)}, u32[]{:S(2)}, u32[]{:S(2)}) %collective-permute-start.12) | collective-permute-done | bytes 98336 | tf_op jit(solution)/shard_map/ppermute | solution.py:296
  30.4 2.4 %collective-permute-start.13 = (bf16[384,128]{1,0:T(8,128)(2,1)S(1)}, bf16[384,128]{1,0:T(8,128)(2,1)S(1)}, u32[]{:S(2)}, u32[]{:S(2)}) collective-permute-start(bf16[384,128]{1,0:T(8,128)(2,1)S(1)} %add_convert_fusion.5), channel_id=1, source_target_pairs={{0,64},{1,67},{2,66},{3,69},{4,68},{5,71},{6,70},{7,73},{8,72},{9,... | collective-permute-start | bytes 294920 | tf_op jit(solution)/shard_map/ppermute | solution.py:300
  32.8 3.5 %collective-permute-start.18 = (bf16[384,128]{1,0:T(8,128)(2,1)S(1)}, bf16[384,128]{1,0:T(8,128)(2,1)S(1)}, u32[]{:S(2)}, u32[]{:S(2)}) collective-permute-start(bf16[384,128]{1,0:T(8,128)(2,1)S(1)} %add_convert_fusion.4), channel_id=1, source_target_pairs={{0,126},{1,125},{2,4},{3,127},{4,2},{5,9},{6,8},{7,11},{8,6},{9,5}... | collective-permute-start | bytes 294920 | tf_op jit(solution)/shard_map/ppermute | solution.py:300
  36.5 2.4 %middle_local_terms.1 = (f32[16,16,192]{2,1,0:T(8,128)S(1)}, f32[16,16,192]{2,1,0:T(8,128)S(1)}) custom-call(bf16[32,6,96,192]{3,2,1,0:T(8,128)(2,1)S(1)} %get-tuple-element.54.off_v, bf16[32,96,192]{2,1,0:T(8,128)(2,1)S(1)} %get-tuple-element.68.diag_v, bf16[32,16,96]{2,1,0:T(8,128)(2,1)S(1)} %get-tuple-element.74.xb, s32[6,32]{1,0:T(8,128)S(1)} %bitcast.4, ...), custom_call_target="tpu_custom_call" | custom-call | flops 132120576 | bytes 40000000 | tf_op jit(solution)/shard_map/middle_local_terms/pallas_call | solution.py:370
  39.1 0.5 %collective-permute-start.17 = (f32[16,16,192]{2,1,0:T(8,128)S(1)}, f32[16,16,192]{2,1,0:T(8,128)S(1)}, u32[]{:S(2)}, u32[]{:S(2)}) collective-permute-start(f32[16,16,192]{2,1,0:T(8,128)S(1)} %get-tuple-element.77.rest_1_), channel_id=1, source_target_pairs={{0,1},{1,0},{2,3},{3,2},{4,5},{5,4},{6,7},{7,6},{8,9},{9,8},{10,11... | collective-permute-start | bytes 589832 | tf_op jit(solution)/shard_map/ppermute | solution.py:296
  39.6 0.1 collective-permute-start.16
  39.7 3.2 %collective-permute-done.18.rest_6_ = bf16[384,128]{1,0:T(8,128)(2,1)S(1)} collective-permute-done((bf16[384,128]{1,0:T(8,128)(2,1)S(1)}, bf16[384,128]{1,0:T(8,128)(2,1)S(1)}, u32[]{:S(2)}, u32[]{:S(2)}) %collective-permute-start.18) | collective-permute-done | bytes 98336 | tf_op jit(solution)/shard_map/ppermute | solution.py:300
  42.8 0.4 collective-permute-start.21
  43.2 0.2 collective-permute-start.22
  43.3 0.8 %collective-permute-done.21.rest_9_ = bf16[384,128]{1,0:T(8,128)(2,1)S(1)} collective-permute-done((bf16[384,128]{1,0:T(8,128)(2,1)S(1)}, bf16[384,128]{1,0:T(8,128)(2,1)S(1)}, u32[]{:S(2)}, u32[]{:S(2)}) %collective-permute-start.21) | collective-permute-done | bytes 98336 | tf_op jit(solution)/shard_map/ppermute | solution.py:296
  44.1 0.4 collective-permute-done.22.rest_10_
  44.5 2.7 %last_terms.1 = (f32[32,16,192]{2,1,0:T(8,128)}, f32[32,16,192]{2,1,0:T(8,128)}) custom-call(bf16[32,96,192]{2,1,0:T(8,128)(2,1)S(1)} %get-tuple-element.43.pre_v, bf16[32,96,192]{2,1,0:T(8,128)(2,1)S(1)} %collective-permute-done.3.pre_other, f32[32,16,192]{2,1,0:T(8,128)S(1)} %copy-done, bf16[32,16,192]{2,1,0:T(8,128)(2,1)S(1)} %get-tuple-element.65.vb, ...), custom_call_target="tpu_custom_call" | custom-call | tf_op jit(solution)/shard_map/last_terms/pallas_call | solution.py:381
  (31 shorter events, 0.6 us)
Async XLA Ops:
  0.6 18.2 %collective-permute-start.3 = (bf16[32,96,192]{2,1,0:T(8,128)(2,1)}, bf16[32,96,192]{2,1,0:T(8,128)(2,1)S(1)}, u32[]{:S(2)}, u32[]{:S(2)}) collective-permute-start(bf16[32,96,192]{2,1,0:T(8,128)(2,1)} %precond.1), channel_id=1, source_target_pairs={{0,1},{1,0},{2,3},{3,2},{4,5},{5,4},{6,7},{7,6},{8,9},{9,8},{10,11... | collective-permute-start | bytes 3538952 | tf_op jit(solution)/shard_map/ppermute | solution.py:296
  6.6 1.4 %collective-permute-start = (bf16[400,128]{1,0:T(8,128)(2,1)S(1)}, bf16[400,128]{1,0:T(8,128)(2,1)S(1)}, u32[]{:S(2)}, u32[]{:S(2)}) collective-permute-start(bf16[400,128]{1,0:T(8,128)(2,1)S(1)} %get-tuple-element.45), channel_id=1, source_target_pairs={{0,1},{1,0},{2,3},{3,2},{4,5},{5,4},{6,7},{7,6},{8,9},{9,8},{10,11... | collective-permute-start | bytes 307208 | tf_op jit(solution)/shard_map/ppermute | solution.py:296
  6.7 5.4 %collective-permute-start.1 = (bf16[400,128]{1,0:T(8,128)(2,1)S(1)}, bf16[400,128]{1,0:T(8,128)(2,1)S(1)}, u32[]{:S(2)}, u32[]{:S(2)}) collective-permute-start(bf16[400,128]{1,0:T(8,128)(2,1)S(1)} %get-tuple-element.47), channel_id=1, source_target_pairs={{0,1},{1,0},{2,3},{3,2},{4,5},{5,4},{6,7},{7,6},{8,9},{9,8},{10,11... | collective-permute-start | bytes 307208 | tf_op jit(solution)/shard_map/ppermute | solution.py:296
  7.1 11.5 %collective-permute-start.2 = (bf16[400,128]{1,0:T(8,128)(2,1)S(1)}, bf16[400,128]{1,0:T(8,128)(2,1)S(1)}, u32[]{:S(2)}, u32[]{:S(2)}) collective-permute-start(bf16[400,128]{1,0:T(8,128)(2,1)S(1)} %get-tuple-element.49), channel_id=1, source_target_pairs={{0,1},{1,0},{2,3},{3,2},{4,5},{5,4},{6,7},{7,6},{8,9},{9,8},{10,11... | collective-permute-start | bytes 307208 | tf_op jit(solution)/shard_map/ppermute | solution.py:296
  8.0 15.9 %collective-permute-start.4 = (bf16[400,128]{1,0:T(8,128)(2,1)S(1)}, bf16[400,128]{1,0:T(8,128)(2,1)S(1)}, u32[]{:S(2)}, u32[]{:S(2)}) collective-permute-start(bf16[400,128]{1,0:T(8,128)(2,1)S(1)} %add_convert_fusion.2), channel_id=1, source_target_pairs={{0,64},{1,67},{2,66},{3,69},{4,68},{5,71},{6,70},{7,73},{8,72},{9,... | collective-permute-start | bytes 307208 | tf_op jit(solution)/shard_map/ppermute | solution.py:300
  12.1 12.5 %collective-permute-start.7 = (bf16[400,128]{1,0:T(8,128)(2,1)S(1)}, bf16[400,128]{1,0:T(8,128)(2,1)S(1)}, u32[]{:S(2)}, u32[]{:S(2)}) collective-permute-start(bf16[400,128]{1,0:T(8,128)(2,1)S(1)} %add_convert_fusion.1), channel_id=1, source_target_pairs={{0,126},{1,125},{2,4},{3,127},{4,2},{5,9},{6,8},{7,11},{8,6},{9,5}... | collective-permute-start | bytes 307208 | tf_op jit(solution)/shard_map/ppermute | solution.py:300
  18.7 5.9 %collective-permute-start.8 = (bf16[400,128]{1,0:T(8,128)(2,1)S(1)}, bf16[400,128]{1,0:T(8,128)(2,1)S(1)}, u32[]{:S(2)}, u32[]{:S(2)}) collective-permute-start(bf16[400,128]{1,0:T(8,128)(2,1)S(1)} %add_convert_fusion), channel_id=1, source_target_pairs={{0,2},{1,5},{2,0},{3,7},{4,6},{5,1},{6,4},{7,3},{8,10},{9,13},{10,... | collective-permute-start | bytes 307208 | tf_op jit(solution)/shard_map/ppermute | solution.py:300
  18.8 7.8 %copy-start = (f32[32,16,192]{2,1,0:T(8,128)S(1)}, f32[32,16,192]{2,1,0:T(8,128)}, u32[]{:S(2)}) copy-start(f32[32,16,192]{2,1,0:T(8,128)} %rhs.5) | copy-start | bytes 1179652
  23.9 1.4 %collective-permute-start.9 = (bf16[400,128]{1,0:T(8,128)(2,1)S(1)}, bf16[400,128]{1,0:T(8,128)(2,1)S(1)}, u32[]{:S(2)}, u32[]{:S(2)}) collective-permute-start(bf16[400,128]{1,0:T(8,128)(2,1)S(1)} %collective-permute-done.4.rest_4_), channel_id=1, source_target_pairs={{0,1},{1,0},{2,3},{3,2},{4,5},{5,4},{6,7},{7,6},{8,9},{9,8},{10,11... | collective-permute-start | bytes 307208 | tf_op jit(solution)/shard_map/ppermute | solution.py:296
  24.0 2.2 %collective-permute-start.5 = (f32[16,16,192]{2,1,0:T(8,128)S(1)}, f32[16,16,192]{2,1,0:T(8,128)S(1)}, u32[]{:S(2)}, u32[]{:S(2)}) collective-permute-start(f32[16,16,192]{2,1,0:T(8,128)S(1)} %get-tuple-element.58.rest_0_), channel_id=1, source_target_pairs={{0,1},{1,0},{2,3},{3,2},{4,5},{5,4},{6,7},{7,6},{8,9},{9,8},{10,11... | collective-permute-start | bytes 589832 | tf_op jit(solution)/shard_map/ppermute | solution.py:296
  24.5 1.7 %collective-permute-start.6 = (f32[16,16,192]{2,1,0:T(8,128)S(1)}, f32[16,16,192]{2,1,0:T(8,128)S(1)}, u32[]{:S(2)}, u32[]{:S(2)}) collective-permute-start(f32[16,16,192]{2,1,0:T(8,128)S(1)} %get-tuple-element.59.rest_1_), channel_id=1, source_target_pairs={{0,1},{1,0},{2,3},{3,2},{4,5},{5,4},{6,7},{7,6},{8,9},{9,8},{10,11... | collective-permute-start | bytes 589832 | tf_op jit(solution)/shard_map/ppermute | solution.py:296
  24.6 1.6 %collective-permute-start.10 = (bf16[400,128]{1,0:T(8,128)(2,1)S(1)}, bf16[400,128]{1,0:T(8,128)(2,1)S(1)}, u32[]{:S(2)}, u32[]{:S(2)}) collective-permute-start(bf16[400,128]{1,0:T(8,128)(2,1)S(1)} %collective-permute-done.7.rest_5_), channel_id=1, source_target_pairs={{0,1},{1,0},{2,3},{3,2},{4,5},{5,4},{6,7},{7,6},{8,9},{9,8},{10,11... | collective-permute-start | bytes 307208 | tf_op jit(solution)/shard_map/ppermute | solution.py:296
  25.3 1.3 %collective-permute-start.11 = (bf16[400,128]{1,0:T(8,128)(2,1)S(1)}, bf16[400,128]{1,0:T(8,128)(2,1)S(1)}, u32[]{:S(2)}, u32[]{:S(2)}) collective-permute-start(bf16[400,128]{1,0:T(8,128)(2,1)S(1)} %collective-permute-done.8.rest_6_), channel_id=1, source_target_pairs={{0,1},{1,0},{2,3},{3,2},{4,5},{5,4},{6,7},{7,6},{8,9},{9,8},{10,11... | collective-permute-start | bytes 307208 | tf_op jit(solution)/shard_map/ppermute | solution.py:296
  26.6 9.9 %copy-start.1 = (s32[32,6]{0,1:T(8,128)S(1)}, s32[32,6]{0,1:T(8,128)}, u32[]{:S(2)}) copy-start(s32[32,6]{0,1:T(8,128)} %param.10) | copy-start | bytes 2308
  26.6 9.9 %copy-start.2 = (s32[32,6]{0,1:T(8,128)S(1)}, s32[32,6]{0,1:T(8,128)}, u32[]{:S(2)}) copy-start(s32[32,6]{0,1:T(8,128)} %param.11) | copy-start | bytes 2308
  29.0 1.4 %collective-permute-start.12 = (bf16[384,128]{1,0:T(8,128)(2,1)S(1)}, bf16[384,128]{1,0:T(8,128)(2,1)S(1)}, u32[]{:S(2)}, u32[]{:S(2)}) collective-permute-start(bf16[384,128]{1,0:T(8,128)(2,1)S(1)} %get-tuple-element.67), channel_id=1, source_target_pairs={{0,1},{1,0},{2,3},{3,2},{4,5},{5,4},{6,7},{7,6},{8,9},{9,8},{10,11... | collective-permute-start | bytes 294920 | tf_op jit(solution)/shard_map/ppermute | solution.py:296
  29.2 3.6 %collective-permute-start.14 = (bf16[384,128]{1,0:T(8,128)(2,1)S(1)}, bf16[384,128]{1,0:T(8,128)(2,1)S(1)}, u32[]{:S(2)}, u32[]{:S(2)}) collective-permute-start(bf16[384,128]{1,0:T(8,128)(2,1)S(1)} %get-tuple-element.70), channel_id=1, source_target_pairs={{0,1},{1,0},{2,3},{3,2},{4,5},{5,4},{6,7},{7,6},{8,9},{9,8},{10,11... | collective-permute-start | bytes 294920 | tf_op jit(solution)/shard_map/ppermute | solution.py:296
  29.6 6.8 %collective-permute-start.15 = (bf16[384,128]{1,0:T(8,128)(2,1)S(1)}, bf16[384,128]{1,0:T(8,128)(2,1)S(1)}, u32[]{:S(2)}, u32[]{:S(2)}) collective-permute-start(bf16[384,128]{1,0:T(8,128)(2,1)S(1)} %get-tuple-element.72), channel_id=1, source_target_pairs={{0,1},{1,0},{2,3},{3,2},{4,5},{5,4},{6,7},{7,6},{8,9},{9,8},{10,11... | collective-permute-start | bytes 294920 | tf_op jit(solution)/shard_map/ppermute | solution.py:296
  30.4 8.6 %collective-permute-start.13 = (bf16[384,128]{1,0:T(8,128)(2,1)S(1)}, bf16[384,128]{1,0:T(8,128)(2,1)S(1)}, u32[]{:S(2)}, u32[]{:S(2)}) collective-permute-start(bf16[384,128]{1,0:T(8,128)(2,1)S(1)} %add_convert_fusion.5), channel_id=1, source_target_pairs={{0,64},{1,67},{2,66},{3,69},{4,68},{5,71},{6,70},{7,73},{8,72},{9,... | collective-permute-start | bytes 294920 | tf_op jit(solution)/shard_map/ppermute | solution.py:300
  32.8 10.0 %collective-permute-start.18 = (bf16[384,128]{1,0:T(8,128)(2,1)S(1)}, bf16[384,128]{1,0:T(8,128)(2,1)S(1)}, u32[]{:S(2)}, u32[]{:S(2)}) collective-permute-start(bf16[384,128]{1,0:T(8,128)(2,1)S(1)} %add_convert_fusion.4), channel_id=1, source_target_pairs={{0,126},{1,125},{2,4},{3,127},{4,2},{5,9},{6,8},{7,11},{8,6},{9,5}... | collective-permute-start | bytes 294920 | tf_op jit(solution)/shard_map/ppermute | solution.py:300
  36.4 6.8 %collective-permute-start.19 = (bf16[384,128]{1,0:T(8,128)(2,1)S(1)}, bf16[384,128]{1,0:T(8,128)(2,1)S(1)}, u32[]{:S(2)}, u32[]{:S(2)}) collective-permute-start(bf16[384,128]{1,0:T(8,128)(2,1)S(1)} %add_convert_fusion.3), channel_id=1, source_target_pairs={{0,2},{1,5},{2,0},{3,7},{4,6},{5,1},{6,4},{7,3},{8,10},{9,13},{10,... | collective-permute-start | bytes 294920 | tf_op jit(solution)/shard_map/ppermute | solution.py:300
  39.0 4.2 %collective-permute-start.20 = (bf16[384,128]{1,0:T(8,128)(2,1)S(1)}, bf16[384,128]{1,0:T(8,128)(2,1)S(1)}, u32[]{:S(2)}, u32[]{:S(2)}) collective-permute-start(bf16[384,128]{1,0:T(8,128)(2,1)S(1)} %collective-permute-done.13.rest_5_), channel_id=1, source_target_pairs={{0,1},{1,0},{2,3},{3,2},{4,5},{5,4},{6,7},{7,6},{8,9},{9,8},{10,11... | collective-permute-start | bytes 294920 | tf_op jit(solution)/shard_map/ppermute | solution.py:296
  39.1 5.1 %collective-permute-start.17 = (f32[16,16,192]{2,1,0:T(8,128)S(1)}, f32[16,16,192]{2,1,0:T(8,128)S(1)}, u32[]{:S(2)}, u32[]{:S(2)}) collective-permute-start(f32[16,16,192]{2,1,0:T(8,128)S(1)} %get-tuple-element.77.rest_1_), channel_id=1, source_target_pairs={{0,1},{1,0},{2,3},{3,2},{4,5},{5,4},{6,7},{7,6},{8,9},{9,8},{10,11... | collective-permute-start | bytes 589832 | tf_op jit(solution)/shard_map/ppermute | solution.py:296
  39.6 4.9 %collective-permute-start.16 = (f32[16,16,192]{2,1,0:T(8,128)S(1)}, f32[16,16,192]{2,1,0:T(8,128)S(1)}, u32[]{:S(2)}, u32[]{:S(2)}) collective-permute-start(f32[16,16,192]{2,1,0:T(8,128)S(1)} %get-tuple-element.76.rest_0_), channel_id=1, source_target_pairs={{0,1},{1,0},{2,3},{3,2},{4,5},{5,4},{6,7},{7,6},{8,9},{9,8},{10,11... | collective-permute-start | bytes 589832 | tf_op jit(solution)/shard_map/ppermute | solution.py:296
  42.8 1.3 %collective-permute-start.21 = (bf16[384,128]{1,0:T(8,128)(2,1)S(1)}, bf16[384,128]{1,0:T(8,128)(2,1)S(1)}, u32[]{:S(2)}, u32[]{:S(2)}) collective-permute-start(bf16[384,128]{1,0:T(8,128)(2,1)S(1)} %collective-permute-done.18.rest_6_), channel_id=1, source_target_pairs={{0,1},{1,0},{2,3},{3,2},{4,5},{5,4},{6,7},{7,6},{8,9},{9,8},{10,11... | collective-permute-start | bytes 294920 | tf_op jit(solution)/shard_map/ppermute | solution.py:296
  43.2 1.3 %collective-permute-start.22 = (bf16[384,128]{1,0:T(8,128)(2,1)S(1)}, bf16[384,128]{1,0:T(8,128)(2,1)S(1)}, u32[]{:S(2)}, u32[]{:S(2)}) collective-permute-start(bf16[384,128]{1,0:T(8,128)(2,1)S(1)} %collective-permute-done.19.rest_7_), channel_id=1, source_target_pairs={{0,1},{1,0},{2,3},{3,2},{4,5},{5,4},{6,7},{7,6},{8,9},{9,8},{10,11... | collective-permute-start | bytes 294920 | tf_op jit(solution)/shard_map/ppermute | solution.py:296

commit v5 on v4

--- a/solution.py
+++ b/solution.py
@@ -18,7 +18,7 @@
 FACES = (
     ((0, 1, 0, 1), (2, 2, 3, 3)),
     ((1, 0, 1, 0), (3, 3, 2, 2)),
-    ((4, 4, 4, 4), (5, 5, 5, 5)),
+    ((5, 5, 5, 5), (4, 4, 4, 4)),
 )
 STRIDE = CAP + 1
 COUNTS = FAN * STRIDE
@@ -302,12 +302,8 @@
     def tie(*arrays):
         return lax.optimization_barrier(arrays)
 
-    def exchange(mine, theirs, *later, chain=False):
-        sums = []
-        for m, t in zip(mine, theirs):
-            if sums and chain:
-                t, sums[0] = tie(t, sums[0])
-            sums.append((m + across(t).astype(f32)).astype(bf16))
+    def exchange(mine, theirs, *later):
+        sums = [(m + across(t).astype(f32)).astype(bf16) for m, t in zip(mine, theirs)]
         got = [to_faces(x, p) for p, x in enumerate(sums)]
         later = lax.optimization_barrier((*sums, *later))[len(sums) :]
         return got, *later
@@ -366,7 +362,7 @@
         [VM] * 9,
         received + [pltpu.SMEM((1, 128), i32), pltpu.SMEM((1, 128), i32), dma((2,))],
     )(off_v, pre_v, adj_rhs, table, x_half, *partial, *other, *got, *forwarded)
-    got, xb = exchange(messages[:3], messages[3:], xb, chain=False)
+    got, xb = exchange(messages[:3], messages[3:], xb)
     partial = call(
         middle_local_kernel,
         "middle_local_terms",

time: 47.3 us -> 46.5 us (0.983)
  waiting for transfers between devices: 7.17 us -> 5.02 us
  starting transfers between devices: 22 us -> 22.9 us
    ppermute x17, starting transfers between devices: 5.32 us -> 8.26 us  [across(): return lax.ppermute(x, 'blk', [(0, 1), (1, 0)])]
    ppermute x6, waiting for transfers between devices: 3.22 us -> 1.01 us  [to_faces(): return lax.ppermute(x, ('rows', 'blk'), pairs)]
    ppermute x6, starting transfers between devices: 16.7 us -> 14.6 us  [to_faces(): return lax.ppermute(x, ('rows', 'blk'), pairs)]
  transfers between devices with their start and end apart: 23 -> 23, of which waited for: 8 -> 8; matrix products, arithmetic and copies ran while one was open for 0% -> 0% of each run, Pallas kernels for 25% -> 27%
where the time goes in v5:
time: 46.5 us; the launch traced here: 46.2 us
  starting transfers between devices  22.9 us (49%)
  Pallas kernels  17.4 us (37%)
  waiting for transfers between devices  5.02 us (11%)
  between operations  0.77 us (2%)
    ppermute x6, starting transfers between devices, to_faces(): return lax.ppermute(x, ('rows', 'blk'), pairs)  14.6 us
    ppermute x17, starting transfers between devices, across(): return lax.ppermute(x, 'blk', [(0, 1), (1, 0)])  8.26 us
    pallas_call x1, Pallas kernels, on_device(): call(first_local_kernel, 'first_local_terms', [shape((ROWS, FAN, HALF, WI...  5.09 us
    pallas_call x1, Pallas kernels, on_device(): call(first_kernel, 'first_remote_terms', [shape((ROWS, ADJ, HALF), f32),...  4.69 us
    ppermute x17, waiting for transfers between devices, across(): return lax.ppermute(x, 'blk', [(0, 1), (1, 0)])  4.01 us
    pallas_call x1, Pallas kernels, on_device(): call(last_kernel, 'last_terms', [field, field], [VM] * (4 + 2 * PIECES) +...  2.72 us
    pallas_call x1, Pallas kernels, on_device(): call(middle_local_kernel, 'middle_local_terms', pieces, [VM, VM, VM, SM,...  2.47 us
    pallas_call x1, Pallas kernels, on_device(): call(middle_kernel, 'middle_remote_terms', [shape((ROWS, ADJ, WIDTH), bf1...  2.41 us
  transfers between devices with their start and end apart: 23, of which 8 were waited for; matrix products, arithmetic and copies ran while one was open for 0% of the time, Pallas kernels for 27%

profile of v5, /device:TPU:1, one launch (start us, length us, event | category | flops | bytes accessed | tf_op | source)
XLA Modules:
  0.0 46.2 jit_solution(14148128786340596829)
XLA Ops:
  0.6 1.5 %collective-permute-start.3 = (bf16[32,96,192]{2,1,0:T(8,128)(2,1)}, bf16[32,96,192]{2,1,0:T(8,128)(2,1)S(1)}, u32[]{:S(2)}, u32[]{:S(2)}) collective-permute-start(bf16[32,96,192]{2,1,0:T(8,128)(2,1)} %precond.1), channel_id=1, source_target_pairs={{0,1},{1,0},{2,3},{3,2},{4,5},{5,4},{6,7},{7,6},{8,9},{9,8},{10,11... | collective-permute-start | bytes 3538952 | tf_op jit(solution)/shard_map/ppermute | solution.py:296
  2.1 4.7 %first_remote_terms.1 = (f32[32,16,96]{2,1,0:T(8,128)S(1)}, bf16[32,16,96]{2,1,0:T(8,128)(2,1)S(1)}, bf16[32,96,192]{2,1,0:T(8,128)(2,1)S(1)}, f32[400,128]{1,0:...) custom-call(bf16[32,6,96,192]{3,2,1,0:T(8,128)(2,1)} %off.3, ...), custom_call_target="tpu_custom_call" | custom-call | tf_op jit(solution)/shard_map/first_remote_terms/pallas_call | solution.py:333
  6.8 0.1 collective-permute-start
  6.9 0.5 %collective-permute-start.1 = (bf16[400,128]{1,0:T(8,128)(2,1)S(1)}, bf16[400,128]{1,0:T(8,128)(2,1)S(1)}, u32[]{:S(2)}, u32[]{:S(2)}) collective-permute-start(bf16[400,128]{1,0:T(8,128)(2,1)S(1)} %get-tuple-element.47), channel_id=1, source_target_pairs={{0,1},{1,0},{2,3},{3,2},{4,5},{5,4},{6,7},{7,6},{8,9},{9,8},{10,11... | collective-permute-start | bytes 307208 | tf_op jit(solution)/shard_map/ppermute | solution.py:296
  7.4 0.1 collective-permute-start.2
  7.5 0.7 %collective-permute-done = bf16[400,128]{1,0:T(8,128)(2,1)S(1)} collective-permute-done((bf16[400,128]{1,0:T(8,128)(2,1)S(1)}, bf16[400,128]{1,0:T(8,128)(2,1)S(1)}, u32[]{:S(2)}, u32[]{:S(2)}) %collective-permute-start) | collective-permute-done | bytes 102432 | tf_op jit(solution)/shard_map/ppermute | solution.py:296
  8.2 2.8 %collective-permute-start.4 = (bf16[400,128]{1,0:T(8,128)(2,1)S(1)}, bf16[400,128]{1,0:T(8,128)(2,1)S(1)}, u32[]{:S(2)}, u32[]{:S(2)}) collective-permute-start(bf16[400,128]{1,0:T(8,128)(2,1)S(1)} %add_convert_fusion.2), channel_id=1, source_target_pairs={{0,66},{1,65},{2,68},{3,67},{4,70},{5,69},{6,72},{7,71},{8,74},{9,... | collective-permute-start | bytes 307208 | tf_op jit(solution)/shard_map/ppermute | solution.py:300
  11.1 6.8 %collective-permute-start.7 = (bf16[400,128]{1,0:T(8,128)(2,1)S(1)}, bf16[400,128]{1,0:T(8,128)(2,1)S(1)}, u32[]{:S(2)}, u32[]{:S(2)}) collective-permute-start(bf16[400,128]{1,0:T(8,128)(2,1)S(1)} %add_convert_fusion.1), channel_id=1, source_target_pairs={{0,126},{1,125},{2,4},{3,127},{4,2},{5,9},{6,8},{7,11},{8,6},{9,5}... | collective-permute-start | bytes 307208 | tf_op jit(solution)/shard_map/ppermute | solution.py:300
  18.1 5.1 %first_local_terms.1 = (bf16[32,6,96,192]{3,2,1,0:T(8,128)(2,1)S(1)}, bf16[32,96,192]{2,1,0:T(8,128)(2,1)S(1)}, s32[1,128]{1,0:T(1,128)S(1)}, f32[16,16,192]{2,1,0:T(8,128)S(1)}, f32[16,16,192]{2,1,0:T(8,128)S(1)}) custom-call(bf16[32,6,96,192]{3,2,1,0:T(8,128)(2,1)} %off.3, bf16[32,96,192]{2,1,0:T(8,128)(2,1)} %diag.1, ...), custom_call_target="tpu_custom_call" | custom-call | flops 132120576 | bytes 40000000 | tf_op jit(solution)/shard_map/first_local_terms/pallas_call | solution.py:345
  23.2 0.5 %collective-permute-start.5 = (f32[16,16,192]{2,1,0:T(8,128)S(1)}, f32[16,16,192]{2,1,0:T(8,128)S(1)}, u32[]{:S(2)}, u32[]{:S(2)}) collective-permute-start(f32[16,16,192]{2,1,0:T(8,128)S(1)} %get-tuple-element.58.rest_0_), channel_id=1, source_target_pairs={{0,1},{1,0},{2,3},{3,2},{4,5},{5,4},{6,7},{7,6},{8,9},{9,8},{10,11... | collective-permute-start | bytes 589832 | tf_op jit(solution)/shard_map/ppermute | solution.py:296
  23.7 0.1 collective-permute-start.6
  23.8 0.4 collective-permute-start.10
  24.3 0.3 collective-permute-done.9.rest_7_
  24.5 0.2 collective-permute-start.11
  24.7 0.7 %collective-permute-done.10.rest_8_ = bf16[400,128]{1,0:T(8,128)(2,1)S(1)} collective-permute-done((bf16[400,128]{1,0:T(8,128)(2,1)S(1)}, bf16[400,128]{1,0:T(8,128)(2,1)S(1)}, u32[]{:S(2)}, u32[]{:S(2)}) %collective-permute-start.10) | collective-permute-done | bytes 102432 | tf_op jit(solution)/shard_map/ppermute | solution.py:296
  25.4 0.4 collective-permute-done.11.rest_9_
  25.9 2.4 %middle_remote_terms.1 = (bf16[32,16,192]{2,1,0:T(8,128)(2,1)S(1)}, bf16[32,16,96]{2,1,0:T(8,128)(2,1)S(1)}, s32[1,128]{1,0:T(1,128)S(1)}, f32[384,128]{1,0:T(8,...) custom-call(bf16[32,6,96,192]{3,2,1,0:T(8,128)(2,1)S(1)} %get-tuple-, ...), custom_call_target="tpu_custom_call" | custom-call | tf_op jit(solution)/shard_map/middle_remote_terms/pallas_call | solution.py:356
  28.3 0.2 collective-permute-start.12
  28.5 0.4 collective-permute-start.14
  28.9 0.1 collective-permute-start.15
  29.0 0.6 %collective-permute-done.12 = bf16[384,128]{1,0:T(8,128)(2,1)S(1)} collective-permute-done((bf16[384,128]{1,0:T(8,128)(2,1)S(1)}, bf16[384,128]{1,0:T(8,128)(2,1)S(1)}, u32[]{:S(2)}, u32[]{:S(2)}) %collective-permute-start.12) | collective-permute-done | bytes 98336 | tf_op jit(solution)/shard_map/ppermute | solution.py:296
  29.7 1.4 %collective-permute-start.13 = (bf16[384,128]{1,0:T(8,128)(2,1)S(1)}, bf16[384,128]{1,0:T(8,128)(2,1)S(1)}, u32[]{:S(2)}, u32[]{:S(2)}) collective-permute-start(bf16[384,128]{1,0:T(8,128)(2,1)S(1)} %add_convert_fusion.5), channel_id=1, source_target_pairs={{0,66},{1,65},{2,68},{3,67},{4,70},{5,69},{6,72},{7,71},{8,74},{9,... | collective-permute-start | bytes 294920 | tf_op jit(solution)/shard_map/ppermute | solution.py:300
  31.2 3.4 %collective-permute-start.18 = (bf16[384,128]{1,0:T(8,128)(2,1)S(1)}, bf16[384,128]{1,0:T(8,128)(2,1)S(1)}, u32[]{:S(2)}, u32[]{:S(2)}) collective-permute-start(bf16[384,128]{1,0:T(8,128)(2,1)S(1)} %add_convert_fusion.4), channel_id=1, source_target_pairs={{0,126},{1,125},{2,4},{3,127},{4,2},{5,9},{6,8},{7,11},{8,6},{9,5}... | collective-permute-start | bytes 294920 | tf_op jit(solution)/shard_map/ppermute | solution.py:300
  34.7 2.5 %middle_local_terms.1 = (f32[16,16,192]{2,1,0:T(8,128)S(1)}, f32[16,16,192]{2,1,0:T(8,128)S(1)}) custom-call(bf16[32,6,96,192]{3,2,1,0:T(8,128)(2,1)S(1)} %get-tuple-element.54.off_v, bf16[32,96,192]{2,1,0:T(8,128)(2,1)S(1)} %get-tuple-element.68.diag_v, bf16[32,16,96]{2,1,0:T(8,128)(2,1)S(1)} %get-tuple-element.74.xb, s32[6,32]{1,0:T(8,128)S(1)} %bitcast.4, ...), custom_call_target="tpu_custom_call" | custom-call | flops 132120576 | bytes 40000000 | tf_op jit(solution)/shard_map/middle_local_terms/pallas_call | solution.py:366
  37.2 2.0 %collective-permute-start.20 = (bf16[384,128]{1,0:T(8,128)(2,1)S(1)}, bf16[384,128]{1,0:T(8,128)(2,1)S(1)}, u32[]{:S(2)}, u32[]{:S(2)}) collective-permute-start(bf16[384,128]{1,0:T(8,128)(2,1)S(1)} %collective-permute-done.13.rest_5_), channel_id=1, source_target_pairs={{0,1},{1,0},{2,3},{3,2},{4,5},{5,4},{6,7},{7,6},{8,9},{9,8},{10,11... | collective-permute-start | bytes 294920 | tf_op jit(solution)/shard_map/ppermute | solution.py:296
  39.2 0.1 collective-permute-start.17
  39.3 0.4 collective-permute-start.16
  39.7 1.0 %collective-permute-done.18.rest_6_ = bf16[384,128]{1,0:T(8,128)(2,1)S(1)} collective-permute-done((bf16[384,128]{1,0:T(8,128)(2,1)S(1)}, bf16[384,128]{1,0:T(8,128)(2,1)S(1)}, u32[]{:S(2)}, u32[]{:S(2)}) %collective-permute-start.18) | collective-permute-done | bytes 98336 | tf_op jit(solution)/shard_map/ppermute | solution.py:300
  40.7 1.5 %collective-permute-start.21 = (bf16[384,128]{1,0:T(8,128)(2,1)S(1)}, bf16[384,128]{1,0:T(8,128)(2,1)S(1)}, u32[]{:S(2)}, u32[]{:S(2)}) collective-permute-start(bf16[384,128]{1,0:T(8,128)(2,1)S(1)} %collective-permute-done.18.rest_6_), channel_id=1, source_target_pairs={{0,1},{1,0},{2,3},{3,2},{4,5},{5,4},{6,7},{7,6},{8,9},{9,8},{10,11... | collective-permute-start | bytes 294920 | tf_op jit(solution)/shard_map/ppermute | solution.py:296
  42.3 0.9 %collective-permute-done.21.rest_9_ = bf16[384,128]{1,0:T(8,128)(2,1)S(1)} collective-permute-done((bf16[384,128]{1,0:T(8,128)(2,1)S(1)}, bf16[384,128]{1,0:T(8,128)(2,1)S(1)}, u32[]{:S(2)}, u32[]{:S(2)}) %collective-permute-start.21) | collective-permute-done | bytes 98336 | tf_op jit(solution)/shard_map/ppermute | solution.py:296
  43.2 0.4 collective-permute-done.22.rest_10_
  43.5 2.7 %last_terms.1 = (f32[32,16,192]{2,1,0:T(8,128)}, f32[32,16,192]{2,1,0:T(8,128)}) custom-call(bf16[32,96,192]{2,1,0:T(8,128)(2,1)S(1)} %get-tuple-element.43.pre_v, bf16[32,96,192]{2,1,0:T(8,128)(2,1)S(1)} %collective-permute-done.3.pre_other, f32[32,16,192]{2,1,0:T(8,128)S(1)} %copy-done, bf16[32,16,192]{2,1,0:T(8,128)(2,1)S(1)} %get-tuple-element.65.vb, ...), custom_call_target="tpu_custom_call" | custom-call | tf_op jit(solution)/shard_map/last_terms/pallas_call | solution.py:377
  (31 shorter events, 0.6 us)
Async XLA Ops:
  0.6 17.4 %collective-permute-start.3 = (bf16[32,96,192]{2,1,0:T(8,128)(2,1)}, bf16[32,96,192]{2,1,0:T(8,128)(2,1)S(1)}, u32[]{:S(2)}, u32[]{:S(2)}) collective-permute-start(bf16[32,96,192]{2,1,0:T(8,128)(2,1)} %precond.1), channel_id=1, source_target_pairs={{0,1},{1,0},{2,3},{3,2},{4,5},{5,4},{6,7},{7,6},{8,9},{9,8},{10,11... | collective-permute-start | bytes 3538952 | tf_op jit(solution)/shard_map/ppermute | solution.py:296
  6.8 1.4 %collective-permute-start = (bf16[400,128]{1,0:T(8,128)(2,1)S(1)}, bf16[400,128]{1,0:T(8,128)(2,1)S(1)}, u32[]{:S(2)}, u32[]{:S(2)}) collective-permute-start(bf16[400,128]{1,0:T(8,128)(2,1)S(1)} %get-tuple-element.45), channel_id=1, source_target_pairs={{0,1},{1,0},{2,3},{3,2},{4,5},{5,4},{6,7},{7,6},{8,9},{9,8},{10,11... | collective-permute-start | bytes 307208 | tf_op jit(solution)/shard_map/ppermute | solution.py:296
  6.9 4.1 %collective-permute-start.1 = (bf16[400,128]{1,0:T(8,128)(2,1)S(1)}, bf16[400,128]{1,0:T(8,128)(2,1)S(1)}, u32[]{:S(2)}, u32[]{:S(2)}) collective-permute-start(bf16[400,128]{1,0:T(8,128)(2,1)S(1)} %get-tuple-element.47), channel_id=1, source_target_pairs={{0,1},{1,0},{2,3},{3,2},{4,5},{5,4},{6,7},{7,6},{8,9},{9,8},{10,11... | collective-permute-start | bytes 307208 | tf_op jit(solution)/shard_map/ppermute | solution.py:296
  7.4 10.5 %collective-permute-start.2 = (bf16[400,128]{1,0:T(8,128)(2,1)S(1)}, bf16[400,128]{1,0:T(8,128)(2,1)S(1)}, u32[]{:S(2)}, u32[]{:S(2)}) collective-permute-start(bf16[400,128]{1,0:T(8,128)(2,1)S(1)} %get-tuple-element.49), channel_id=1, source_target_pairs={{0,1},{1,0},{2,3},{3,2},{4,5},{5,4},{6,7},{7,6},{8,9},{9,8},{10,11... | collective-permute-start | bytes 307208 | tf_op jit(solution)/shard_map/ppermute | solution.py:296
  8.2 14.9 %collective-permute-start.4 = (bf16[400,128]{1,0:T(8,128)(2,1)S(1)}, bf16[400,128]{1,0:T(8,128)(2,1)S(1)}, u32[]{:S(2)}, u32[]{:S(2)}) collective-permute-start(bf16[400,128]{1,0:T(8,128)(2,1)S(1)} %add_convert_fusion.2), channel_id=1, source_target_pairs={{0,66},{1,65},{2,68},{3,67},{4,70},{5,69},{6,72},{7,71},{8,74},{9,... | collective-permute-start | bytes 307208 | tf_op jit(solution)/shard_map/ppermute | solution.py:300
  11.1 12.8 %collective-permute-start.7 = (bf16[400,128]{1,0:T(8,128)(2,1)S(1)}, bf16[400,128]{1,0:T(8,128)(2,1)S(1)}, u32[]{:S(2)}, u32[]{:S(2)}) collective-permute-start(bf16[400,128]{1,0:T(8,128)(2,1)S(1)} %add_convert_fusion.1), channel_id=1, source_target_pairs={{0,126},{1,125},{2,4},{3,127},{4,2},{5,9},{6,8},{7,11},{8,6},{9,5}... | collective-permute-start | bytes 307208 | tf_op jit(solution)/shard_map/ppermute | solution.py:300
  17.9 5.9 %collective-permute-start.8 = (bf16[400,128]{1,0:T(8,128)(2,1)S(1)}, bf16[400,128]{1,0:T(8,128)(2,1)S(1)}, u32[]{:S(2)}, u32[]{:S(2)}) collective-permute-start(bf16[400,128]{1,0:T(8,128)(2,1)S(1)} %add_convert_fusion), channel_id=1, source_target_pairs={{0,2},{1,5},{2,0},{3,7},{4,6},{5,1},{6,4},{7,3},{8,10},{9,13},{10,... | collective-permute-start | bytes 307208 | tf_op jit(solution)/shard_map/ppermute | solution.py:300
  18.0 7.8 %copy-start = (f32[32,16,192]{2,1,0:T(8,128)S(1)}, f32[32,16,192]{2,1,0:T(8,128)}, u32[]{:S(2)}) copy-start(f32[32,16,192]{2,1,0:T(8,128)} %rhs.5) | copy-start | bytes 1179652
  23.2 1.4 %collective-permute-start.9 = (bf16[400,128]{1,0:T(8,128)(2,1)S(1)}, bf16[400,128]{1,0:T(8,128)(2,1)S(1)}, u32[]{:S(2)}, u32[]{:S(2)}) collective-permute-start(bf16[400,128]{1,0:T(8,128)(2,1)S(1)} %collective-permute-done.4.rest_4_), channel_id=1, source_target_pairs={{0,1},{1,0},{2,3},{3,2},{4,5},{5,4},{6,7},{7,6},{8,9},{9,8},{10,11... | collective-permute-start | bytes 307208 | tf_op jit(solution)/shard_map/ppermute | solution.py:296
  23.2 2.2 %collective-permute-start.5 = (f32[16,16,192]{2,1,0:T(8,128)S(1)}, f32[16,16,192]{2,1,0:T(8,128)S(1)}, u32[]{:S(2)}, u32[]{:S(2)}) collective-permute-start(f32[16,16,192]{2,1,0:T(8,128)S(1)} %get-tuple-element.58.rest_0_), channel_id=1, source_target_pairs={{0,1},{1,0},{2,3},{3,2},{4,5},{5,4},{6,7},{7,6},{8,9},{9,8},{10,11... | collective-permute-start | bytes 589832 | tf_op jit(solution)/shard_map/ppermute | solution.py:296
  23.7 1.7 %collective-permute-start.6 = (f32[16,16,192]{2,1,0:T(8,128)S(1)}, f32[16,16,192]{2,1,0:T(8,128)S(1)}, u32[]{:S(2)}, u32[]{:S(2)}) collective-permute-start(f32[16,16,192]{2,1,0:T(8,128)S(1)} %get-tuple-element.59.rest_1_), channel_id=1, source_target_pairs={{0,1},{1,0},{2,3},{3,2},{4,5},{5,4},{6,7},{7,6},{8,9},{9,8},{10,11... | collective-permute-start | bytes 589832 | tf_op jit(solution)/shard_map/ppermute | solution.py:296
  23.8 1.6 %collective-permute-start.10 = (bf16[400,128]{1,0:T(8,128)(2,1)S(1)}, bf16[400,128]{1,0:T(8,128)(2,1)S(1)}, u32[]{:S(2)}, u32[]{:S(2)}) collective-permute-start(bf16[400,128]{1,0:T(8,128)(2,1)S(1)} %collective-permute-done.7.rest_5_), channel_id=1, source_target_pairs={{0,1},{1,0},{2,3},{3,2},{4,5},{5,4},{6,7},{7,6},{8,9},{9,8},{10,11... | collective-permute-start | bytes 307208 | tf_op jit(solution)/shard_map/ppermute | solution.py:296
  24.5 1.3 %collective-permute-start.11 = (bf16[400,128]{1,0:T(8,128)(2,1)S(1)}, bf16[400,128]{1,0:T(8,128)(2,1)S(1)}, u32[]{:S(2)}, u32[]{:S(2)}) collective-permute-start(bf16[400,128]{1,0:T(8,128)(2,1)S(1)} %collective-permute-done.8.rest_6_), channel_id=1, source_target_pairs={{0,1},{1,0},{2,3},{3,2},{4,5},{5,4},{6,7},{7,6},{8,9},{9,8},{10,11... | collective-permute-start | bytes 307208 | tf_op jit(solution)/shard_map/ppermute | solution.py:296
  25.9 8.8 %copy-start.1 = (s32[32,6]{0,1:T(8,128)S(1)}, s32[32,6]{0,1:T(8,128)}, u32[]{:S(2)}) copy-start(s32[32,6]{0,1:T(8,128)} %param.10) | copy-start | bytes 2308
  25.9 8.9 %copy-start.2 = (s32[32,6]{0,1:T(8,128)S(1)}, s32[32,6]{0,1:T(8,128)}, u32[]{:S(2)}) copy-start(s32[32,6]{0,1:T(8,128)} %param.11) | copy-start | bytes 2308
  28.3 1.4 %collective-permute-start.12 = (bf16[384,128]{1,0:T(8,128)(2,1)S(1)}, bf16[384,128]{1,0:T(8,128)(2,1)S(1)}, u32[]{:S(2)}, u32[]{:S(2)}) collective-permute-start(bf16[384,128]{1,0:T(8,128)(2,1)S(1)} %get-tuple-element.67), channel_id=1, source_target_pairs={{0,1},{1,0},{2,3},{3,2},{4,5},{5,4},{6,7},{7,6},{8,9},{9,8},{10,11... | collective-permute-start | bytes 294920 | tf_op jit(solution)/shard_map/ppermute | solution.py:296
  28.5 2.6 %collective-permute-start.14 = (bf16[384,128]{1,0:T(8,128)(2,1)S(1)}, bf16[384,128]{1,0:T(8,128)(2,1)S(1)}, u32[]{:S(2)}, u32[]{:S(2)}) collective-permute-start(bf16[384,128]{1,0:T(8,128)(2,1)S(1)} %get-tuple-element.70), channel_id=1, source_target_pairs={{0,1},{1,0},{2,3},{3,2},{4,5},{5,4},{6,7},{7,6},{8,9},{9,8},{10,11... | collective-permute-start | bytes 294920 | tf_op jit(solution)/shard_map/ppermute | solution.py:296
  28.9 5.7 %collective-permute-start.15 = (bf16[384,128]{1,0:T(8,128)(2,1)S(1)}, bf16[384,128]{1,0:T(8,128)(2,1)S(1)}, u32[]{:S(2)}, u32[]{:S(2)}) collective-permute-start(bf16[384,128]{1,0:T(8,128)(2,1)S(1)} %get-tuple-element.72), channel_id=1, source_target_pairs={{0,1},{1,0},{2,3},{3,2},{4,5},{5,4},{6,7},{7,6},{8,9},{9,8},{10,11... | collective-permute-start | bytes 294920 | tf_op jit(solution)/shard_map/ppermute | solution.py:296
  29.7 7.5 %collective-permute-start.13 = (bf16[384,128]{1,0:T(8,128)(2,1)S(1)}, bf16[384,128]{1,0:T(8,128)(2,1)S(1)}, u32[]{:S(2)}, u32[]{:S(2)}) collective-permute-start(bf16[384,128]{1,0:T(8,128)(2,1)S(1)} %add_convert_fusion.5), channel_id=1, source_target_pairs={{0,66},{1,65},{2,68},{3,67},{4,70},{5,69},{6,72},{7,71},{8,74},{9,... | collective-permute-start | bytes 294920 | tf_op jit(solution)/shard_map/ppermute | solution.py:300
  31.2 9.5 %collective-permute-start.18 = (bf16[384,128]{1,0:T(8,128)(2,1)S(1)}, bf16[384,128]{1,0:T(8,128)(2,1)S(1)}, u32[]{:S(2)}, u32[]{:S(2)}) collective-permute-start(bf16[384,128]{1,0:T(8,128)(2,1)S(1)} %add_convert_fusion.4), channel_id=1, source_target_pairs={{0,126},{1,125},{2,4},{3,127},{4,2},{5,9},{6,8},{7,11},{8,6},{9,5}... | collective-permute-start | bytes 294920 | tf_op jit(solution)/shard_map/ppermute | solution.py:300
  34.6 7.6 %collective-permute-start.19 = (bf16[384,128]{1,0:T(8,128)(2,1)S(1)}, bf16[384,128]{1,0:T(8,128)(2,1)S(1)}, u32[]{:S(2)}, u32[]{:S(2)}) collective-permute-start(bf16[384,128]{1,0:T(8,128)(2,1)S(1)} %add_convert_fusion.3), channel_id=1, source_target_pairs={{0,2},{1,5},{2,0},{3,7},{4,6},{5,1},{6,4},{7,3},{8,10},{9,13},{10,... | collective-permute-start | bytes 294920 | tf_op jit(solution)/shard_map/ppermute | solution.py:300
  37.2 5.0 %collective-permute-start.20 = (bf16[384,128]{1,0:T(8,128)(2,1)S(1)}, bf16[384,128]{1,0:T(8,128)(2,1)S(1)}, u32[]{:S(2)}, u32[]{:S(2)}) collective-permute-start(bf16[384,128]{1,0:T(8,128)(2,1)S(1)} %collective-permute-done.13.rest_5_), channel_id=1, source_target_pairs={{0,1},{1,0},{2,3},{3,2},{4,5},{5,4},{6,7},{7,6},{8,9},{9,8},{10,11... | collective-permute-start | bytes 294920 | tf_op jit(solution)/shard_map/ppermute | solution.py:296
  39.2 4.0 %collective-permute-start.17 = (f32[16,16,192]{2,1,0:T(8,128)S(1)}, f32[16,16,192]{2,1,0:T(8,128)S(1)}, u32[]{:S(2)}, u32[]{:S(2)}) collective-permute-start(f32[16,16,192]{2,1,0:T(8,128)S(1)} %get-tuple-element.77.rest_1_), channel_id=1, source_target_pairs={{0,1},{1,0},{2,3},{3,2},{4,5},{5,4},{6,7},{7,6},{8,9},{9,8},{10,11... | collective-permute-start | bytes 589832 | tf_op jit(solution)/shard_map/ppermute | solution.py:296
  39.3 4.2 %collective-permute-start.16 = (f32[16,16,192]{2,1,0:T(8,128)S(1)}, f32[16,16,192]{2,1,0:T(8,128)S(1)}, u32[]{:S(2)}, u32[]{:S(2)}) collective-permute-start(f32[16,16,192]{2,1,0:T(8,128)S(1)} %get-tuple-element.76.rest_0_), channel_id=1, source_target_pairs={{0,1},{1,0},{2,3},{3,2},{4,5},{5,4},{6,7},{7,6},{8,9},{9,8},{10,11... | collective-permute-start | bytes 589832 | tf_op jit(solution)/shard_map/ppermute | solution.py:296
  40.7 2.5 %collective-permute-start.21 = (bf16[384,128]{1,0:T(8,128)(2,1)S(1)}, bf16[384,128]{1,0:T(8,128)(2,1)S(1)}, u32[]{:S(2)}, u32[]{:S(2)}) collective-permute-start(bf16[384,128]{1,0:T(8,128)(2,1)S(1)} %collective-permute-done.18.rest_6_), channel_id=1, source_target_pairs={{0,1},{1,0},{2,3},{3,2},{4,5},{5,4},{6,7},{7,6},{8,9},{9,8},{10,11... | collective-permute-start | bytes 294920 | tf_op jit(solution)/shard_map/ppermute | solution.py:296
  42.2 1.3 %collective-permute-start.22 = (bf16[384,128]{1,0:T(8,128)(2,1)S(1)}, bf16[384,128]{1,0:T(8,128)(2,1)S(1)}, u32[]{:S(2)}, u32[]{:S(2)}) collective-permute-start(bf16[384,128]{1,0:T(8,128)(2,1)S(1)} %collective-permute-done.19.rest_7_), channel_id=1, source_target_pairs={{0,1},{1,0},{2,3},{3,2},{4,5},{5,4},{6,7},{7,6},{8,9},{9,8},{10,11... | collective-permute-start | bytes 294920 | tf_op jit(solution)/shard_map/ppermute | solution.py:296

commit v6 on v5

--- a/solution.py
+++ b/solution.py
@@ -150,7 +150,7 @@
     lax.fori_loop(first, last, row, 0, unroll=min(last - first, LOCAL_UNROLL))
 
 
-def first_local_kernel(off, diag, xb, owner, local, off_v, diag_v, table, *rest):
+def first_local_kernel(off, diag_v, xb, owner, local, off_v, table, *rest):
     partial, (sums, owner_s, local_s, sems, small_sems) = rest[:PIECES], rest[PIECES:]
     own = lax.axis_index("rows")
     small = [pltpu.make_async_copy(a, b, small_sems.at[k]) for k, (a, b) in enumerate(((owner, owner_s), (local, local_s)))]
@@ -159,7 +159,7 @@
     copies = []
     for chunk in range(CHUNKS):
         part = pl.ds(chunk * PER, PER)
-        copies.append([pltpu.make_async_copy(a.at[part], b.at[part], sems.at[k, chunk]) for k, (a, b) in enumerate(((off, off_v), (diag, diag_v)))])
+        copies.append([pltpu.make_async_copy(a.at[part], b.at[part], sems.at[k, chunk]) for k, (a, b) in enumerate(((off, off_v),))])
         for copy in copies[-1]:
             copy.start()
     sums[...] = jnp.zeros(sums.shape, sums.dtype)
@@ -342,15 +342,15 @@
     )(*in_hbm(off_blocks, precond, adj_rhs, owner, local))
     got, xb = exchange(messages[:3], messages[3:], xb)
     xb, pre_other = tie(xb, pre_other)
-    off_v, diag_v, table, *partial = call(
+    off_v, table, *partial = call(
         first_local_kernel,
         "first_local_terms",
-        [shape((ROWS, FAN, HALF, WIDTH), bf16), half_blocks, row_of_ints] + pieces,
-        [HBM, HBM, VM, HBM, HBM],
-        [VM] * 2 + [SM] + [VM] * PIECES,
-        [sums] + ints + [dma((2, CHUNKS)), dma((2,))],
+        [shape((ROWS, FAN, HALF, WIDTH), bf16), row_of_ints] + pieces,
+        [HBM, VM, VM, HBM, HBM],
+        [VM, SM] + [VM] * PIECES,
+        [sums] + ints + [dma((1, CHUNKS)), dma((2,))],
         cost,
-    )(*in_hbm(off_blocks, diag_blocks), xb, *in_hbm(owner, local))
+    )(*in_hbm(off_blocks), diag_blocks, xb, *in_hbm(owner, local))
     partial, other, got, forwarded = hand_on(got, list(partial))
 
     vb, xb, labels, *messages = call(
@@ -371,7 +371,7 @@
         [VM] * PIECES,
         [sums],
         cost,
-    )(off_v, diag_v, xb, owner, local)
+    )(off_v, diag_blocks, xb, owner, local)
     partial, other, got, forwarded = hand_on(got, list(partial))
 
     return call(

time: 46.5 us -> 46.1 us (level)
  Pallas kernels: 17.4 us -> 16.8 us
  transfers between devices with their start and end apart: 23 -> 23, of which waited for: 8 -> 8; matrix products, arithmetic and copies ran while one was open for 0% -> 0% of each run, Pallas kernels for 27% -> 25%
where the time goes in v6:
time: 46.1 us; the launch traced here: 45.9 us
  starting transfers between devices  23.1 us (50%)
  Pallas kernels  16.8 us (36%)
  waiting for transfers between devices  5.09 us (11%)
  between operations  0.78 us (2%)
    ppermute x6, starting transfers between devices, to_faces(): return lax.ppermute(x, ('rows', 'blk'), pairs)  14.9 us
    ppermute x17, starting transfers between devices, across(): return lax.ppermute(x, 'blk', [(0, 1), (1, 0)])  8.15 us
    pallas_call x1, Pallas kernels, on_device(): call(first_local_kernel, 'first_local_terms', [shape((ROWS, FAN, HALF, WI...  4.64 us
    pallas_call x1, Pallas kernels, on_device(): call(first_kernel, 'first_remote_terms', [shape((ROWS, ADJ, HALF), f32),...  4.49 us
    ppermute x17, waiting for transfers between devices, across(): return lax.ppermute(x, 'blk', [(0, 1), (1, 0)])  4.01 us
    pallas_call x1, Pallas kernels, on_device(): call(last_kernel, 'last_terms', [field, field], [VM] * (4 + 2 * PIECES) +...  2.75 us
    pallas_call x1, Pallas kernels, on_device(): call(middle_local_kernel, 'middle_local_terms', pieces, [VM, VM, VM, SM,...  2.46 us
    pallas_call x1, Pallas kernels, on_device(): call(middle_kernel, 'middle_remote_terms', [shape((ROWS, ADJ, WIDTH), bf1...  2.45 us
  transfers between devices with their start and end apart: 23, of which 8 were waited for; matrix products, arithmetic and copies ran while one was open for 0% of the time, Pallas kernels for 25%

profile of v6, /device:TPU:1, one launch (start us, length us, event | category | flops | bytes accessed | tf_op | source)
XLA Modules:
  0.0 45.9 jit_solution(1027905016361793369)
XLA Ops:
  0.6 1.5 %collective-permute-start.3 = (bf16[32,96,192]{2,1,0:T(8,128)(2,1)}, bf16[32,96,192]{2,1,0:T(8,128)(2,1)S(1)}, u32[]{:S(2)}, u32[]{:S(2)}) collective-permute-start(bf16[32,96,192]{2,1,0:T(8,128)(2,1)} %precond.1), channel_id=1, source_target_pairs={{0,1},{1,0},{2,3},{3,2},{4,5},{5,4},{6,7},{7,6},{8,9},{9,8},{10,11... | collective-permute-start | bytes 3538952 | tf_op jit(solution)/shard_map/ppermute | solution.py:296
  2.1 4.5 %first_remote_terms.1 = (f32[32,16,96]{2,1,0:T(8,128)S(1)}, bf16[32,16,96]{2,1,0:T(8,128)(2,1)S(1)}, bf16[32,96,192]{2,1,0:T(8,128)(2,1)S(1)}, f32[400,128]{1,0:...) custom-call(bf16[32,6,96,192]{3,2,1,0:T(8,128)(2,1)} %off.3, ...), custom_call_target="tpu_custom_call" | custom-call | tf_op jit(solution)/shard_map/first_remote_terms/pallas_call | solution.py:333
  6.6 0.1 collective-permute-start
  6.7 0.5 %collective-permute-start.1 = (bf16[400,128]{1,0:T(8,128)(2,1)S(1)}, bf16[400,128]{1,0:T(8,128)(2,1)S(1)}, u32[]{:S(2)}, u32[]{:S(2)}) collective-permute-start(bf16[400,128]{1,0:T(8,128)(2,1)S(1)} %get-tuple-element.46), channel_id=1, source_target_pairs={{0,1},{1,0},{2,3},{3,2},{4,5},{5,4},{6,7},{7,6},{8,9},{9,8},{10,11... | collective-permute-start | bytes 307208 | tf_op jit(solution)/shard_map/ppermute | solution.py:296
  7.2 0.1 collective-permute-start.2
  7.3 0.7 %collective-permute-done = bf16[400,128]{1,0:T(8,128)(2,1)S(1)} collective-permute-done((bf16[400,128]{1,0:T(8,128)(2,1)S(1)}, bf16[400,128]{1,0:T(8,128)(2,1)S(1)}, u32[]{:S(2)}, u32[]{:S(2)}) %collective-permute-start) | collective-permute-done | bytes 102432 | tf_op jit(solution)/shard_map/ppermute | solution.py:296
  8.1 2.9 %collective-permute-start.4 = (bf16[400,128]{1,0:T(8,128)(2,1)S(1)}, bf16[400,128]{1,0:T(8,128)(2,1)S(1)}, u32[]{:S(2)}, u32[]{:S(2)}) collective-permute-start(bf16[400,128]{1,0:T(8,128)(2,1)S(1)} %add_convert_fusion.2), channel_id=1, source_target_pairs={{0,66},{1,65},{2,68},{3,67},{4,70},{5,69},{6,72},{7,71},{8,74},{9,... | collective-permute-start | bytes 307208 | tf_op jit(solution)/shard_map/ppermute | solution.py:300
  11.0 7.1 %collective-permute-start.7 = (bf16[400,128]{1,0:T(8,128)(2,1)S(1)}, bf16[400,128]{1,0:T(8,128)(2,1)S(1)}, u32[]{:S(2)}, u32[]{:S(2)}) collective-permute-start(bf16[400,128]{1,0:T(8,128)(2,1)S(1)} %add_convert_fusion.1), channel_id=1, source_target_pairs={{0,126},{1,125},{2,4},{3,127},{4,2},{5,9},{6,8},{7,11},{8,6},{9,5}... | collective-permute-start | bytes 307208 | tf_op jit(solution)/shard_map/ppermute | solution.py:300
  18.3 4.6 %first_local_terms.1 = (bf16[32,6,96,192]{3,2,1,0:T(8,128)(2,1)S(1)}, s32[1,128]{1,0:T(1,128)S(1)}, f32[16,16,192]{2,1,0:T(8,128)S(1)}, f32[16,16,192]{2,1,0:T(8,128)S(1)}) custom-call(bf16[32,6,96,192]{3,2,1,0:T(8,128)(2,1)} %off.3, bf16[32,96,192]{2,1,0:T(8,128)(2,1)S(1)} %copy-done, bf16[32,16,96]{2,1,0:T(8,128)(2,1)S(1)} %get-tuple-element.52.xb, ...), custom_call_target="tpu_custom_call" | custom-call | flops 132120576 | bytes 40000000 | tf_op jit(solution)/shard_map/first_local_terms/pallas_call | solution.py:345
  23.0 0.5 %collective-permute-start.5 = (f32[16,16,192]{2,1,0:T(8,128)S(1)}, f32[16,16,192]{2,1,0:T(8,128)S(1)}, u32[]{:S(2)}, u32[]{:S(2)}) collective-permute-start(f32[16,16,192]{2,1,0:T(8,128)S(1)} %get-tuple-element.57.rest_0_), channel_id=1, source_target_pairs={{0,1},{1,0},{2,3},{3,2},{4,5},{5,4},{6,7},{7,6},{8,9},{9,8},{10,11... | collective-permute-start | bytes 589832 | tf_op jit(solution)/shard_map/ppermute | solution.py:296
  23.5 0.1 collective-permute-start.6
  23.6 0.4 collective-permute-start.10
  24.0 0.3 collective-permute-done.9.rest_7_
  24.3 0.2 collective-permute-start.11
  24.5 0.7 %collective-permute-done.10.rest_8_ = bf16[400,128]{1,0:T(8,128)(2,1)S(1)} collective-permute-done((bf16[400,128]{1,0:T(8,128)(2,1)S(1)}, bf16[400,128]{1,0:T(8,128)(2,1)S(1)}, u32[]{:S(2)}, u32[]{:S(2)}) %collective-permute-start.10) | collective-permute-done | bytes 102432 | tf_op jit(solution)/shard_map/ppermute | solution.py:296
  25.2 0.4 collective-permute-done.11.rest_9_
  25.6 2.5 %middle_remote_terms.1 = (bf16[32,16,192]{2,1,0:T(8,128)(2,1)S(1)}, bf16[32,16,96]{2,1,0:T(8,128)(2,1)S(1)}, s32[1,128]{1,0:T(1,128)S(1)}, f32[384,128]{1,0:T(8,...) custom-call(bf16[32,6,96,192]{3,2,1,0:T(8,128)(2,1)S(1)} %get-tuple-, ...), custom_call_target="tpu_custom_call" | custom-call | tf_op jit(solution)/shard_map/middle_remote_terms/pallas_call | solution.py:356
  28.1 0.2 collective-permute-start.12
  28.3 0.4 collective-permute-start.14
  28.7 0.2 collective-permute-start.15
  28.8 0.6 %collective-permute-done.12 = bf16[384,128]{1,0:T(8,128)(2,1)S(1)} collective-permute-done((bf16[384,128]{1,0:T(8,128)(2,1)S(1)}, bf16[384,128]{1,0:T(8,128)(2,1)S(1)}, u32[]{:S(2)}, u32[]{:S(2)}) %collective-permute-start.12) | collective-permute-done | bytes 98336 | tf_op jit(solution)/shard_map/ppermute | solution.py:296
  29.5 1.3 %collective-permute-start.13 = (bf16[384,128]{1,0:T(8,128)(2,1)S(1)}, bf16[384,128]{1,0:T(8,128)(2,1)S(1)}, u32[]{:S(2)}, u32[]{:S(2)}) collective-permute-start(bf16[384,128]{1,0:T(8,128)(2,1)S(1)} %add_convert_fusion.5), channel_id=1, source_target_pairs={{0,66},{1,65},{2,68},{3,67},{4,70},{5,69},{6,72},{7,71},{8,74},{9,... | collective-permute-start | bytes 294920 | tf_op jit(solution)/shard_map/ppermute | solution.py:300
  30.8 3.5 %collective-permute-start.18 = (bf16[384,128]{1,0:T(8,128)(2,1)S(1)}, bf16[384,128]{1,0:T(8,128)(2,1)S(1)}, u32[]{:S(2)}, u32[]{:S(2)}) collective-permute-start(bf16[384,128]{1,0:T(8,128)(2,1)S(1)} %add_convert_fusion.4), channel_id=1, source_target_pairs={{0,126},{1,125},{2,4},{3,127},{4,2},{5,9},{6,8},{7,11},{8,6},{9,5}... | collective-permute-start | bytes 294920 | tf_op jit(solution)/shard_map/ppermute | solution.py:300
  34.4 2.5 %middle_local_terms.1 = (f32[16,16,192]{2,1,0:T(8,128)S(1)}, f32[16,16,192]{2,1,0:T(8,128)S(1)}) custom-call(bf16[32,6,96,192]{3,2,1,0:T(8,128)(2,1)S(1)} %get-tuple-element.53.off_v, bf16[32,96,192]{2,1,0:T(8,128)(2,1)S(1)} %copy-done, bf16[32,16,96]{2,1,0:T(8,128)(2,1)S(1)} %get-tuple-element.72.xb, s32[6,32]{1,0:T(8,128)S(1)} %bitcast.4, s32[6,32]{1,0:T(8,128)S(1)} %bitcast.7), custom_call_target="tpu_custom_call" | custom-call | flops 132120576 | bytes 40000000 | tf_op jit(solution)/shard_map/middle_local_terms/pallas_call | solution.py:366
  36.9 1.9 %collective-permute-start.20 = (bf16[384,128]{1,0:T(8,128)(2,1)S(1)}, bf16[384,128]{1,0:T(8,128)(2,1)S(1)}, u32[]{:S(2)}, u32[]{:S(2)}) collective-permute-start(bf16[384,128]{1,0:T(8,128)(2,1)S(1)} %collective-permute-done.13.rest_5_), channel_id=1, source_target_pairs={{0,1},{1,0},{2,3},{3,2},{4,5},{5,4},{6,7},{7,6},{8,9},{9,8},{10,11... | collective-permute-start | bytes 294920 | tf_op jit(solution)/shard_map/ppermute | solution.py:296
  38.8 0.1 collective-permute-start.17
  38.9 0.4 collective-permute-start.16
  39.3 1.1 %collective-permute-done.18.rest_6_ = bf16[384,128]{1,0:T(8,128)(2,1)S(1)} collective-permute-done((bf16[384,128]{1,0:T(8,128)(2,1)S(1)}, bf16[384,128]{1,0:T(8,128)(2,1)S(1)}, u32[]{:S(2)}, u32[]{:S(2)}) %collective-permute-start.18) | collective-permute-done | bytes 98336 | tf_op jit(solution)/shard_map/ppermute | solution.py:300
  40.4 1.5 %collective-permute-start.21 = (bf16[384,128]{1,0:T(8,128)(2,1)S(1)}, bf16[384,128]{1,0:T(8,128)(2,1)S(1)}, u32[]{:S(2)}, u32[]{:S(2)}) collective-permute-start(bf16[384,128]{1,0:T(8,128)(2,1)S(1)} %collective-permute-done.18.rest_6_), channel_id=1, source_target_pairs={{0,1},{1,0},{2,3},{3,2},{4,5},{5,4},{6,7},{7,6},{8,9},{9,8},{10,11... | collective-permute-start | bytes 294920 | tf_op jit(solution)/shard_map/ppermute | solution.py:296
  42.0 0.9 %collective-permute-done.21.rest_9_ = bf16[384,128]{1,0:T(8,128)(2,1)S(1)} collective-permute-done((bf16[384,128]{1,0:T(8,128)(2,1)S(1)}, bf16[384,128]{1,0:T(8,128)(2,1)S(1)}, u32[]{:S(2)}, u32[]{:S(2)}) %collective-permute-start.21) | collective-permute-done | bytes 98336 | tf_op jit(solution)/shard_map/ppermute | solution.py:296
  42.8 0.4 collective-permute-done.22.rest_10_
  43.2 2.7 %last_terms.1 = (f32[32,16,192]{2,1,0:T(8,128)}, f32[32,16,192]{2,1,0:T(8,128)}) custom-call(bf16[32,96,192]{2,1,0:T(8,128)(2,1)S(1)} %get-tuple-element.42.pre_v, bf16[32,96,192]{2,1,0:T(8,128)(2,1)S(1)} %collective-permute-done.3.pre_other, f32[32,16,192]{2,1,0:T(8,128)S(1)} %copy-done.1, bf16[32,16,192]{2,1,0:T(8,128)(2,1)S(1)} %get-tuple-element.64.vb, ...), custom_call_target="tpu_custom_call" | custom-call | tf_op jit(solution)/shard_map/last_terms/pallas_call | solution.py:377
  (33 shorter events, 0.6 us)
Async XLA Ops:
  0.6 17.6 %collective-permute-start.3 = (bf16[32,96,192]{2,1,0:T(8,128)(2,1)}, bf16[32,96,192]{2,1,0:T(8,128)(2,1)S(1)}, u32[]{:S(2)}, u32[]{:S(2)}) collective-permute-start(bf16[32,96,192]{2,1,0:T(8,128)(2,1)} %precond.1), channel_id=1, source_target_pairs={{0,1},{1,0},{2,3},{3,2},{4,5},{5,4},{6,7},{7,6},{8,9},{9,8},{10,11... | collective-permute-start | bytes 3538952 | tf_op jit(solution)/shard_map/ppermute | solution.py:296
  2.1 16.1 %copy-start = (bf16[32,96,192]{2,1,0:T(8,128)(2,1)S(1)}, bf16[32,96,192]{2,1,0:T(8,128)(2,1)}, u32[]{:S(2)}) copy-start(bf16[32,96,192]{2,1,0:T(8,128)(2,1)} %diag_v.3) | copy-start | bytes 3538948
  6.6 1.4 %collective-permute-start = (bf16[400,128]{1,0:T(8,128)(2,1)S(1)}, bf16[400,128]{1,0:T(8,128)(2,1)S(1)}, u32[]{:S(2)}, u32[]{:S(2)}) collective-permute-start(bf16[400,128]{1,0:T(8,128)(2,1)S(1)} %get-tuple-element.44), channel_id=1, source_target_pairs={{0,1},{1,0},{2,3},{3,2},{4,5},{5,4},{6,7},{7,6},{8,9},{9,8},{10,11... | collective-permute-start | bytes 307208 | tf_op jit(solution)/shard_map/ppermute | solution.py:296
  6.7 4.2 %collective-permute-start.1 = (bf16[400,128]{1,0:T(8,128)(2,1)S(1)}, bf16[400,128]{1,0:T(8,128)(2,1)S(1)}, u32[]{:S(2)}, u32[]{:S(2)}) collective-permute-start(bf16[400,128]{1,0:T(8,128)(2,1)S(1)} %get-tuple-element.46), channel_id=1, source_target_pairs={{0,1},{1,0},{2,3},{3,2},{4,5},{5,4},{6,7},{7,6},{8,9},{9,8},{10,11... | collective-permute-start | bytes 307208 | tf_op jit(solution)/shard_map/ppermute | solution.py:296
  7.2 10.9 %collective-permute-start.2 = (bf16[400,128]{1,0:T(8,128)(2,1)S(1)}, bf16[400,128]{1,0:T(8,128)(2,1)S(1)}, u32[]{:S(2)}, u32[]{:S(2)}) collective-permute-start(bf16[400,128]{1,0:T(8,128)(2,1)S(1)} %get-tuple-element.48), channel_id=1, source_target_pairs={{0,1},{1,0},{2,3},{3,2},{4,5},{5,4},{6,7},{7,6},{8,9},{9,8},{10,11... | collective-permute-start | bytes 307208 | tf_op jit(solution)/shard_map/ppermute | solution.py:296
  8.1 14.9 %collective-permute-start.4 = (bf16[400,128]{1,0:T(8,128)(2,1)S(1)}, bf16[400,128]{1,0:T(8,128)(2,1)S(1)}, u32[]{:S(2)}, u32[]{:S(2)}) collective-permute-start(bf16[400,128]{1,0:T(8,128)(2,1)S(1)} %add_convert_fusion.2), channel_id=1, source_target_pairs={{0,66},{1,65},{2,68},{3,67},{4,70},{5,69},{6,72},{7,71},{8,74},{9,... | collective-permute-start | bytes 307208 | tf_op jit(solution)/shard_map/ppermute | solution.py:300
  11.0 12.6 %collective-permute-start.7 = (bf16[400,128]{1,0:T(8,128)(2,1)S(1)}, bf16[400,128]{1,0:T(8,128)(2,1)S(1)}, u32[]{:S(2)}, u32[]{:S(2)}) collective-permute-start(bf16[400,128]{1,0:T(8,128)(2,1)S(1)} %add_convert_fusion.1), channel_id=1, source_target_pairs={{0,126},{1,125},{2,4},{3,127},{4,2},{5,9},{6,8},{7,11},{8,6},{9,5}... | collective-permute-start | bytes 307208 | tf_op jit(solution)/shard_map/ppermute | solution.py:300
  18.1 5.5 %collective-permute-start.8 = (bf16[400,128]{1,0:T(8,128)(2,1)S(1)}, bf16[400,128]{1,0:T(8,128)(2,1)S(1)}, u32[]{:S(2)}, u32[]{:S(2)}) collective-permute-start(bf16[400,128]{1,0:T(8,128)(2,1)S(1)} %add_convert_fusion), channel_id=1, source_target_pairs={{0,2},{1,5},{2,0},{3,7},{4,6},{5,1},{6,4},{7,3},{8,10},{9,13},{10,... | collective-permute-start | bytes 307208 | tf_op jit(solution)/shard_map/ppermute | solution.py:300
  18.2 7.4 %copy-start.1 = (f32[32,16,192]{2,1,0:T(8,128)S(1)}, f32[32,16,192]{2,1,0:T(8,128)}, u32[]{:S(2)}) copy-start(f32[32,16,192]{2,1,0:T(8,128)} %rhs.5) | copy-start | bytes 1179652
  22.9 1.4 %collective-permute-start.9 = (bf16[400,128]{1,0:T(8,128)(2,1)S(1)}, bf16[400,128]{1,0:T(8,128)(2,1)S(1)}, u32[]{:S(2)}, u32[]{:S(2)}) collective-permute-start(bf16[400,128]{1,0:T(8,128)(2,1)S(1)} %collective-permute-done.4.rest_4_), channel_id=1, source_target_pairs={{0,1},{1,0},{2,3},{3,2},{4,5},{5,4},{6,7},{7,6},{8,9},{9,8},{10,11... | collective-permute-start | bytes 307208 | tf_op jit(solution)/shard_map/ppermute | solution.py:296
  23.0 2.2 %collective-permute-start.5 = (f32[16,16,192]{2,1,0:T(8,128)S(1)}, f32[16,16,192]{2,1,0:T(8,128)S(1)}, u32[]{:S(2)}, u32[]{:S(2)}) collective-permute-start(f32[16,16,192]{2,1,0:T(8,128)S(1)} %get-tuple-element.57.rest_0_), channel_id=1, source_target_pairs={{0,1},{1,0},{2,3},{3,2},{4,5},{5,4},{6,7},{7,6},{8,9},{9,8},{10,11... | collective-permute-start | bytes 589832 | tf_op jit(solution)/shard_map/ppermute | solution.py:296
  23.5 1.7 %collective-permute-start.6 = (f32[16,16,192]{2,1,0:T(8,128)S(1)}, f32[16,16,192]{2,1,0:T(8,128)S(1)}, u32[]{:S(2)}, u32[]{:S(2)}) collective-permute-start(f32[16,16,192]{2,1,0:T(8,128)S(1)} %get-tuple-element.58.rest_1_), channel_id=1, source_target_pairs={{0,1},{1,0},{2,3},{3,2},{4,5},{5,4},{6,7},{7,6},{8,9},{9,8},{10,11... | collective-permute-start | bytes 589832 | tf_op jit(solution)/shard_map/ppermute | solution.py:296
  23.6 1.6 %collective-permute-start.10 = (bf16[400,128]{1,0:T(8,128)(2,1)S(1)}, bf16[400,128]{1,0:T(8,128)(2,1)S(1)}, u32[]{:S(2)}, u32[]{:S(2)}) collective-permute-start(bf16[400,128]{1,0:T(8,128)(2,1)S(1)} %collective-permute-done.7.rest_5_), channel_id=1, source_target_pairs={{0,1},{1,0},{2,3},{3,2},{4,5},{5,4},{6,7},{7,6},{8,9},{9,8},{10,11... | collective-permute-start | bytes 307208 | tf_op jit(solution)/shard_map/ppermute | solution.py:296
  24.3 1.3 %collective-permute-start.11 = (bf16[400,128]{1,0:T(8,128)(2,1)S(1)}, bf16[400,128]{1,0:T(8,128)(2,1)S(1)}, u32[]{:S(2)}, u32[]{:S(2)}) collective-permute-start(bf16[400,128]{1,0:T(8,128)(2,1)S(1)} %collective-permute-done.8.rest_6_), channel_id=1, source_target_pairs={{0,1},{1,0},{2,3},{3,2},{4,5},{5,4},{6,7},{7,6},{8,9},{9,8},{10,11... | collective-permute-start | bytes 307208 | tf_op jit(solution)/shard_map/ppermute | solution.py:296
  25.6 8.8 %copy-start.2 = (s32[32,6]{0,1:T(8,128)S(1)}, s32[32,6]{0,1:T(8,128)}, u32[]{:S(2)}) copy-start(s32[32,6]{0,1:T(8,128)} %param.10) | copy-start | bytes 2308
  25.6 8.8 %copy-start.3 = (s32[32,6]{0,1:T(8,128)S(1)}, s32[32,6]{0,1:T(8,128)}, u32[]{:S(2)}) copy-start(s32[32,6]{0,1:T(8,128)} %param.11) | copy-start | bytes 2308
  28.1 1.4 %collective-permute-start.12 = (bf16[384,128]{1,0:T(8,128)(2,1)S(1)}, bf16[384,128]{1,0:T(8,128)(2,1)S(1)}, u32[]{:S(2)}, u32[]{:S(2)}) collective-permute-start(bf16[384,128]{1,0:T(8,128)(2,1)S(1)} %get-tuple-element.66), channel_id=1, source_target_pairs={{0,1},{1,0},{2,3},{3,2},{4,5},{5,4},{6,7},{7,6},{8,9},{9,8},{10,11... | collective-permute-start | bytes 294920 | tf_op jit(solution)/shard_map/ppermute | solution.py:296
  28.3 2.5 %collective-permute-start.14 = (bf16[384,128]{1,0:T(8,128)(2,1)S(1)}, bf16[384,128]{1,0:T(8,128)(2,1)S(1)}, u32[]{:S(2)}, u32[]{:S(2)}) collective-permute-start(bf16[384,128]{1,0:T(8,128)(2,1)S(1)} %get-tuple-element.68), channel_id=1, source_target_pairs={{0,1},{1,0},{2,3},{3,2},{4,5},{5,4},{6,7},{7,6},{8,9},{9,8},{10,11... | collective-permute-start | bytes 294920 | tf_op jit(solution)/shard_map/ppermute | solution.py:296
  28.7 5.6 %collective-permute-start.15 = (bf16[384,128]{1,0:T(8,128)(2,1)S(1)}, bf16[384,128]{1,0:T(8,128)(2,1)S(1)}, u32[]{:S(2)}, u32[]{:S(2)}) collective-permute-start(bf16[384,128]{1,0:T(8,128)(2,1)S(1)} %get-tuple-element.70), channel_id=1, source_target_pairs={{0,1},{1,0},{2,3},{3,2},{4,5},{5,4},{6,7},{7,6},{8,9},{9,8},{10,11... | collective-permute-start | bytes 294920 | tf_op jit(solution)/shard_map/ppermute | solution.py:296
  29.5 7.4 %collective-permute-start.13 = (bf16[384,128]{1,0:T(8,128)(2,1)S(1)}, bf16[384,128]{1,0:T(8,128)(2,1)S(1)}, u32[]{:S(2)}, u32[]{:S(2)}) collective-permute-start(bf16[384,128]{1,0:T(8,128)(2,1)S(1)} %add_convert_fusion.5), channel_id=1, source_target_pairs={{0,66},{1,65},{2,68},{3,67},{4,70},{5,69},{6,72},{7,71},{8,74},{9,... | collective-permute-start | bytes 294920 | tf_op jit(solution)/shard_map/ppermute | solution.py:300
  30.8 9.6 %collective-permute-start.18 = (bf16[384,128]{1,0:T(8,128)(2,1)S(1)}, bf16[384,128]{1,0:T(8,128)(2,1)S(1)}, u32[]{:S(2)}, u32[]{:S(2)}) collective-permute-start(bf16[384,128]{1,0:T(8,128)(2,1)S(1)} %add_convert_fusion.4), channel_id=1, source_target_pairs={{0,126},{1,125},{2,4},{3,127},{4,2},{5,9},{6,8},{7,11},{8,6},{9,5}... | collective-permute-start | bytes 294920 | tf_op jit(solution)/shard_map/ppermute | solution.py:300
  34.3 7.6 %collective-permute-start.19 = (bf16[384,128]{1,0:T(8,128)(2,1)S(1)}, bf16[384,128]{1,0:T(8,128)(2,1)S(1)}, u32[]{:S(2)}, u32[]{:S(2)}) collective-permute-start(bf16[384,128]{1,0:T(8,128)(2,1)S(1)} %add_convert_fusion.3), channel_id=1, source_target_pairs={{0,2},{1,5},{2,0},{3,7},{4,6},{5,1},{6,4},{7,3},{8,10},{9,13},{10,... | collective-permute-start | bytes 294920 | tf_op jit(solution)/shard_map/ppermute | solution.py:300
  36.9 5.0 %collective-permute-start.20 = (bf16[384,128]{1,0:T(8,128)(2,1)S(1)}, bf16[384,128]{1,0:T(8,128)(2,1)S(1)}, u32[]{:S(2)}, u32[]{:S(2)}) collective-permute-start(bf16[384,128]{1,0:T(8,128)(2,1)S(1)} %collective-permute-done.13.rest_5_), channel_id=1, source_target_pairs={{0,1},{1,0},{2,3},{3,2},{4,5},{5,4},{6,7},{7,6},{8,9},{9,8},{10,11... | collective-permute-start | bytes 294920 | tf_op jit(solution)/shard_map/ppermute | solution.py:296
  38.8 4.0 %collective-permute-start.17 = (f32[16,16,192]{2,1,0:T(8,128)S(1)}, f32[16,16,192]{2,1,0:T(8,128)S(1)}, u32[]{:S(2)}, u32[]{:S(2)}) collective-permute-start(f32[16,16,192]{2,1,0:T(8,128)S(1)} %get-tuple-element.75.rest_1_), channel_id=1, source_target_pairs={{0,1},{1,0},{2,3},{3,2},{4,5},{5,4},{6,7},{7,6},{8,9},{9,8},{10,11... | collective-permute-start | bytes 589832 | tf_op jit(solution)/shard_map/ppermute | solution.py:296
  38.9 4.3 %collective-permute-start.16 = (f32[16,16,192]{2,1,0:T(8,128)S(1)}, f32[16,16,192]{2,1,0:T(8,128)S(1)}, u32[]{:S(2)}, u32[]{:S(2)}) collective-permute-start(f32[16,16,192]{2,1,0:T(8,128)S(1)} %get-tuple-element.74.rest_0_), channel_id=1, source_target_pairs={{0,1},{1,0},{2,3},{3,2},{4,5},{5,4},{6,7},{7,6},{8,9},{9,8},{10,11... | collective-permute-start | bytes 589832 | tf_op jit(solution)/shard_map/ppermute | solution.py:296
  40.4 2.4 %collective-permute-start.21 = (bf16[384,128]{1,0:T(8,128)(2,1)S(1)}, bf16[384,128]{1,0:T(8,128)(2,1)S(1)}, u32[]{:S(2)}, u32[]{:S(2)}) collective-permute-start(bf16[384,128]{1,0:T(8,128)(2,1)S(1)} %collective-permute-done.18.rest_6_), channel_id=1, source_target_pairs={{0,1},{1,0},{2,3},{3,2},{4,5},{5,4},{6,7},{7,6},{8,9},{9,8},{10,11... | collective-permute-start | bytes 294920 | tf_op jit(solution)/shard_map/ppermute | solution.py:296
  41.9 1.3 %collective-permute-start.22 = (bf16[384,128]{1,0:T(8,128)(2,1)S(1)}, bf16[384,128]{1,0:T(8,128)(2,1)S(1)}, u32[]{:S(2)}, u32[]{:S(2)}) collective-permute-start(bf16[384,128]{1,0:T(8,128)(2,1)S(1)} %collective-permute-done.19.rest_7_), channel_id=1, source_target_pairs={{0,1},{1,0},{2,3},{3,2},{4,5},{5,4},{6,7},{7,6},{8,9},{9,8},{10,11... | collective-permute-start | bytes 294920 | tf_op jit(solution)/shard_map/ppermute | solution.py:296
